TPU v7x, 256 devices: a whole 4x4x8 slice. The times are simulated.
256 devices in a mesh: ens: 16 (over z_lo, x), space: 16 (over z_hi, y, core).
Axes of the slice: x: 4, y: 4, z: 8 (z_hi: 2, z_lo: 4; z = z_hi * 4 + z_lo), core: 2. Of those that a mesh axis runs over, the one named last changes fastest.
Arguments:
- latent: bfloat16 [16, 1024, 24576], P('ens', None, 'space'), may hold values from -6 to 6
- truth: bfloat16 [83, 24576], P(None, 'space'), may hold values from -6 to 6
- w_first: bfloat16 [1024, 1024], replicated, may hold values from -0.1875 to 0.1875
- w_second: bfloat16 [83, 1024], replicated, may hold values from -0.1875 to 0.1875
Outputs:
- loss: float32 [16], P('ens')
- field_grad: float32 [16, 83, 24576], P('ens', None, 'space')
- grad_first: float32 [1024, 1024], P(('ens', 'space'))
- grad_second: float32 [16, 83, 1024], P('ens')
All inputs are finite; a program needn't handle non-finite values.
Results may differ from a plain program's by a relative error of at most 0.007.
Values may be sent and summed in bfloat16 or wider, within the bound.
No kernel may reach another device: no remote copies, remote signals or barrier semaphores. Data moves between devices by JAX's collectives and lax.ppermute only.
A program may use at most 64 MiB of HBM per device.

v0:
```python
import math

import jax
import jax.numpy as jnp
from jax import lax
from jax.sharding import PartitionSpec as P

SMOOTH_SQ = 0.01


def from_behind(value, axis, by):
    size = lax.axis_size(axis)
    return lax.ppermute(value, axis, [(i, (i + by) % size) for i in range(size)])


def on_device(latent, truth, w_first, w_second):
    latent_one = latent[0]
    points = latent_one.shape[1]
    members = lax.axis_size("ens")
    npoints = points * lax.axis_size("space")
    pre_act = jnp.dot(w_first, latent_one, preferred_element_type=jnp.float32)
    hidden = (pre_act * jax.nn.sigmoid(pre_act)).astype(jnp.bfloat16)
    field = jnp.dot(w_second, hidden, preferred_element_type=jnp.float32).astype(jnp.bfloat16)
    member_f = field.astype(jnp.float32)
    truth_f = truth.astype(jnp.float32)
    offset = lax.axis_index("space") * points
    position = (offset + jnp.arange(points)).astype(jnp.float32)
    area = jnp.cos(math.pi * ((position + 0.5) / npoints - 0.5))
    zeros_field = jnp.zeros(member_f.shape, jnp.float32)

    def cycle_step(step, carry):
        moving, value_sum, slope_sum = carry
        moving = from_behind(moving, "ens", 1)
        spread = member_f - moving.astype(jnp.float32)
        smooth_abs = jnp.sqrt(spread * spread + SMOOTH_SQ)
        return (moving, value_sum + smooth_abs, slope_sum + spread / smooth_abs)

    unused, pair_value, pair_slope = lax.fori_loop(
        0, members - 1, cycle_step, (field, zeros_field, zeros_field)
    )
    gap = member_f - truth_f
    gap_abs = jnp.sqrt(gap * gap + SMOOTH_SQ)
    pair_weight = 1.0 / (members * (members - 1))
    grad_field = area * (gap / gap_abs / members - pair_weight * pair_slope)
    loss_local = jnp.sum(area * (gap_abs - pair_value / (2.0 * (members - 1))))
    grad_low = grad_field.astype(jnp.bfloat16)
    second_local = lax.dot_general(
        grad_low, hidden, (((1,), (1,)), ((), ())), preferred_element_type=jnp.float32
    )
    back = jnp.dot(w_second.T, grad_low, preferred_element_type=jnp.float32)
    sigma = jax.nn.sigmoid(pre_act)
    back_pre = (back * sigma * (1.0 + pre_act * (1.0 - sigma))).astype(jnp.bfloat16)
    loss_total, second_total = lax.psum((loss_local, second_local), "space")
    first_total = lax.psum_scatter(
        lax.dot_general(
            back_pre, latent_one, (((1,), (1,)), ((), ())), preferred_element_type=jnp.float32
        ),
        ("ens", "space"),
        scatter_dimension=0,
        tiled=True,
    )
    scale = 1.0 / math.sqrt(members * npoints)
    loss = (loss_total / npoints)[None]
    second_out = (second_total * (members / math.sqrt(npoints)))[None]
    return (loss, grad_field[None], first_total * scale, second_out)


def solution(mesh):
    in_specs = (P("ens", None, "space"), P(None, "space"), P(), P())
    out_specs = (P("ens"), P("ens", None, "space"), P(("ens", "space"), None), P("ens", None, None))
    return jax.shard_map(
        on_device, mesh=mesh, in_specs=in_specs, out_specs=out_specs, check_vma=False
    )
```

profile of v0, /device:TPU:1, one launch (start us, length us, event | category | flops | bytes accessed | tf_op | source)
XLA Modules:
  0.0 708.0 jit_solution(2414170040508547180)
XLA Ops:
  9.1 7.5 %multiply_convert_fusion = (bf16[1024,1536]{1,0:T(8,128)(2,1)S(1)}, f32[1024,1536]{1,0:T(8,128)}) fusion(bf16[1024,1024]{1,0:T(8,128)(2,1)} %param.8, bf16[1,1024,1536]{2,1,0:T(8,128)(2,1)S(1)} %copy-done), kind=kOutput, calls=%fused_computation.7 | convolution fusion | flops 3229089792 | bytes 14680064 | tf_op jit(solution)/shard_map/dot_general | solution.py:21
  21.2 205.1 %while.15 = (s32[]{:T(128)}, bf16[83,1536]{1,0:T(8,128)(2,1)}, f32[83,1536]{1,0:T(8,128)}, f32[83,1536]{1,0:T(8,128)}, f32[83,1536]{1,0:T(8,128)}, /*index=5*/s32[]{:T(128)}, s32[]{:T(128)}) while((s32[]{:T(128)}, bf16[83,1536]{1,0:T(8,128)(2,1)}, f32[83,1536]{1,0:T(8,128)}, f32[83,1536]{1,0:T(8,128)}, f32[83,1536]{1,0:T(8,128)}, ...), condition=%wide.region_1.0_spmd.clone, body=%wide.region_0.0_spmd.clone.sunk | while | flops 1147395 | bytes 4334719 | solution.py:38
  23.4 10.8 %collective-permute-done = bf16[83,1536]{1,0:T(8,128)(2,1)S(1)} collective-permute-done((bf16[83,1536]{1,0:T(8,128)(2,1)}, bf16[83,1536]{1,0:T(8,128)(2,1)S(1)}, u32[]{:S(2)}, u32[]{:S(2)}) %collective-permute-start) | collective-permute-done | bytes 255008 | tf_op jit(solution)/shard_map/while/body/eval_jaxpr/ppermute | solution.py:13
  37.2 9.9 %collective-permute-done = bf16[83,1536]{1,0:T(8,128)(2,1)S(1)} collective-permute-done((bf16[83,1536]{1,0:T(8,128)(2,1)}, bf16[83,1536]{1,0:T(8,128)(2,1)S(1)}, u32[]{:S(2)}, u32[]{:S(2)}) %collective-permute-start) | collective-permute-done | bytes 255008 | tf_op jit(solution)/shard_map/while/body/eval_jaxpr/ppermute | solution.py:13
  47.9 2.7 select_add_fusion.3
  50.6 9.4 %collective-permute-done = bf16[83,1536]{1,0:T(8,128)(2,1)S(1)} collective-permute-done((bf16[83,1536]{1,0:T(8,128)(2,1)}, bf16[83,1536]{1,0:T(8,128)(2,1)S(1)}, u32[]{:S(2)}, u32[]{:S(2)}) %collective-permute-start) | collective-permute-done | bytes 255008 | tf_op jit(solution)/shard_map/while/body/eval_jaxpr/ppermute | solution.py:13
  60.7 2.7 select_add_fusion.3
  63.4 9.4 %collective-permute-done = bf16[83,1536]{1,0:T(8,128)(2,1)S(1)} collective-permute-done((bf16[83,1536]{1,0:T(8,128)(2,1)}, bf16[83,1536]{1,0:T(8,128)(2,1)S(1)}, u32[]{:S(2)}, u32[]{:S(2)}) %collective-permute-start) | collective-permute-done | bytes 255008 | tf_op jit(solution)/shard_map/while/body/eval_jaxpr/ppermute | solution.py:13
  73.5 2.7 select_add_fusion.3
  76.2 9.4 %collective-permute-done = bf16[83,1536]{1,0:T(8,128)(2,1)S(1)} collective-permute-done((bf16[83,1536]{1,0:T(8,128)(2,1)}, bf16[83,1536]{1,0:T(8,128)(2,1)S(1)}, u32[]{:S(2)}, u32[]{:S(2)}) %collective-permute-start) | collective-permute-done | bytes 255008 | tf_op jit(solution)/shard_map/while/body/eval_jaxpr/ppermute | solution.py:13
  86.3 2.7 select_add_fusion.3
  89.0 9.4 %collective-permute-done = bf16[83,1536]{1,0:T(8,128)(2,1)S(1)} collective-permute-done((bf16[83,1536]{1,0:T(8,128)(2,1)}, bf16[83,1536]{1,0:T(8,128)(2,1)S(1)}, u32[]{:S(2)}, u32[]{:S(2)}) %collective-permute-start) | collective-permute-done | bytes 255008 | tf_op jit(solution)/shard_map/while/body/eval_jaxpr/ppermute | solution.py:13
  101.8 9.4 %collective-permute-done = bf16[83,1536]{1,0:T(8,128)(2,1)S(1)} collective-permute-done((bf16[83,1536]{1,0:T(8,128)(2,1)}, bf16[83,1536]{1,0:T(8,128)(2,1)S(1)}, u32[]{:S(2)}, u32[]{:S(2)}) %collective-permute-start) | collective-permute-done | bytes 255008 | tf_op jit(solution)/shard_map/while/body/eval_jaxpr/ppermute | solution.py:13
  111.9 2.7 select_add_fusion.3
  114.6 9.4 %collective-permute-done = bf16[83,1536]{1,0:T(8,128)(2,1)S(1)} collective-permute-done((bf16[83,1536]{1,0:T(8,128)(2,1)}, bf16[83,1536]{1,0:T(8,128)(2,1)S(1)}, u32[]{:S(2)}, u32[]{:S(2)}) %collective-permute-start) | collective-permute-done | bytes 255008 | tf_op jit(solution)/shard_map/while/body/eval_jaxpr/ppermute | solution.py:13
  124.7 2.7 select_add_fusion.3
  127.4 9.4 %collective-permute-done = bf16[83,1536]{1,0:T(8,128)(2,1)S(1)} collective-permute-done((bf16[83,1536]{1,0:T(8,128)(2,1)}, bf16[83,1536]{1,0:T(8,128)(2,1)S(1)}, u32[]{:S(2)}, u32[]{:S(2)}) %collective-permute-start) | collective-permute-done | bytes 255008 | tf_op jit(solution)/shard_map/while/body/eval_jaxpr/ppermute | solution.py:13
  137.5 2.7 select_add_fusion.3
  140.2 9.9 %collective-permute-done = bf16[83,1536]{1,0:T(8,128)(2,1)S(1)} collective-permute-done((bf16[83,1536]{1,0:T(8,128)(2,1)}, bf16[83,1536]{1,0:T(8,128)(2,1)S(1)}, u32[]{:S(2)}, u32[]{:S(2)}) %collective-permute-start) | collective-permute-done | bytes 255008 | tf_op jit(solution)/shard_map/while/body/eval_jaxpr/ppermute | solution.py:13
  150.9 2.7 select_add_fusion.3
  153.5 11.0 %collective-permute-done = bf16[83,1536]{1,0:T(8,128)(2,1)S(1)} collective-permute-done((bf16[83,1536]{1,0:T(8,128)(2,1)}, bf16[83,1536]{1,0:T(8,128)(2,1)S(1)}, u32[]{:S(2)}, u32[]{:S(2)}) %collective-permute-start) | collective-permute-done | bytes 255008 | tf_op jit(solution)/shard_map/while/body/eval_jaxpr/ppermute | solution.py:13
  165.3 2.7 select_add_fusion.3
  168.0 12.2 %collective-permute-done = bf16[83,1536]{1,0:T(8,128)(2,1)S(1)} collective-permute-done((bf16[83,1536]{1,0:T(8,128)(2,1)}, bf16[83,1536]{1,0:T(8,128)(2,1)S(1)}, u32[]{:S(2)}, u32[]{:S(2)}) %collective-permute-start) | collective-permute-done | bytes 255008 | tf_op jit(solution)/shard_map/while/body/eval_jaxpr/ppermute | solution.py:13
  180.9 2.7 select_add_fusion.3
  183.6 11.8 %collective-permute-done = bf16[83,1536]{1,0:T(8,128)(2,1)S(1)} collective-permute-done((bf16[83,1536]{1,0:T(8,128)(2,1)}, bf16[83,1536]{1,0:T(8,128)(2,1)S(1)}, u32[]{:S(2)}, u32[]{:S(2)}) %collective-permute-start) | collective-permute-done | bytes 255008 | tf_op jit(solution)/shard_map/while/body/eval_jaxpr/ppermute | solution.py:13
  198.7 10.9 %collective-permute-done = bf16[83,1536]{1,0:T(8,128)(2,1)S(1)} collective-permute-done((bf16[83,1536]{1,0:T(8,128)(2,1)}, bf16[83,1536]{1,0:T(8,128)(2,1)S(1)}, u32[]{:S(2)}, u32[]{:S(2)}) %collective-permute-start) | collective-permute-done | bytes 255008 | tf_op jit(solution)/shard_map/while/body/eval_jaxpr/ppermute | solution.py:13
  213.0 9.9 %collective-permute-done = bf16[83,1536]{1,0:T(8,128)(2,1)S(1)} collective-permute-done((bf16[83,1536]{1,0:T(8,128)(2,1)}, bf16[83,1536]{1,0:T(8,128)(2,1)S(1)}, u32[]{:S(2)}, u32[]{:S(2)}) %collective-permute-start) | collective-permute-done | bytes 255008 | tf_op jit(solution)/shard_map/while/body/eval_jaxpr/ppermute | solution.py:13
  229.5 3.7 fusion.7
  233.4 10.3 %fusion.2 = f32[1024,1024]{1,0:T(8,128)} fusion(bf16[1,1024,1536]{2,1,0:T(8,128)(2,1)S(1)} %copy-done, f32[1024,1536]{1,0:T(8,128)} %get-tuple-element.75, bf16[83,1024]{1,0:T(8,128)(2,1)S(1)} %copy-done.5, f32[83,1536]{1,0:T(8,128)} %copy-done.2), kind=kOutput, calls=%fused_computation.9 | convolution fusion | flops 3496604160 | bytes 14311424 | tf_op jit(solution)/shard_map/dot_general | solution.py:55
  243.6 61.2 %psum.14 = f32[]{:T(128)} all-reduce(f32[]{:T(128)} %get-tuple-element.73), channel_id=1, replica_groups=mesh['ens'=16,'space'=16] {'space'}, use_global_device_ids=true, to_apply=%region_3.0 | all-reduce | flops 1 | bytes 8 | tf_op jit(solution)/shard_map/psum | solution.py:53
  307.8 115.4 %all-reduce.4.cloned.1.call-done = f32[83,1024]{1,0:T(8,128)} async-done(((f32[83,1024]{1,0:T(8,128)}), f32[83,1024]{1,0:T(8,128)}) %all-reduce.4.cloned.1.call-update) | async-done | bytes 339984 | tf_op jit(solution)/shard_map/psum | solution.py:53
  425.3 273.4 %all-reduce.6.cloned.1.call-done = f32[1024,1024]{1,0:T(8,128)} async-done(((f32[1024,1024]{1,0:T(8,128)}), f32[1024,1024]{1,0:T(8,128)}) %all-reduce.6.cloned.1.call-update) | async-done | bytes 4194320
  (61 shorter events, 41.4 us)
Async XLA Ops:
  7.2 1.9 copy-start
  7.2 416.0 %all-reduce.4.cloned.1.call-start = ((), (), s32[]{:S(2)}) async-start(), calls=%async_computation | async-start | bytes 720896 | tf_op jit(solution)/shard_map/psum | solution.py:53
  9.1 9.3 %copy-start.4 = (bf16[83,1024]{1,0:T(8,128)(2,1)S(1)}, bf16[83,1024]{1,0:T(8,128)(2,1)}, u32[]{:S(2)}) copy-start(bf16[83,1024]{1,0:T(8,128)(2,1)} %param.9) | copy-start | bytes 509956
  16.6 1.7 copy-start.1
  19.8 0.7 copy-start.3
  21.2 12.9 %collective-permute-start = (bf16[83,1536]{1,0:T(8,128)(2,1)}, bf16[83,1536]{1,0:T(8,128)(2,1)S(1)}, u32[]{:S(2)}, u32[]{:S(2)}) collective-permute-start(bf16[83,1536]{1,0:T(8,128)(2,1)} %get-tuple-element.121), channel_id=1, source_target_pairs={{0,16},{16,32},{32,48},{48,64},{64,80},{80,96},{96,112},{112,128},... | collective-permute-start | bytes 764936 | tf_op jit(solution)/shard_map/while/body/eval_jaxpr/ppermute | solution.py:13
  37.2 9.9 %collective-permute-start = (bf16[83,1536]{1,0:T(8,128)(2,1)}, bf16[83,1536]{1,0:T(8,128)(2,1)S(1)}, u32[]{:S(2)}, u32[]{:S(2)}) collective-permute-start(bf16[83,1536]{1,0:T(8,128)(2,1)} %get-tuple-element.121), channel_id=1, source_target_pairs={{0,16},{16,32},{32,48},{48,64},{64,80},{80,96},{96,112},{112,128},... | collective-permute-start | bytes 764936 | tf_op jit(solution)/shard_map/while/body/eval_jaxpr/ppermute | solution.py:13
  50.6 9.4 %collective-permute-start = (bf16[83,1536]{1,0:T(8,128)(2,1)}, bf16[83,1536]{1,0:T(8,128)(2,1)S(1)}, u32[]{:S(2)}, u32[]{:S(2)}) collective-permute-start(bf16[83,1536]{1,0:T(8,128)(2,1)} %get-tuple-element.121), channel_id=1, source_target_pairs={{0,16},{16,32},{32,48},{48,64},{64,80},{80,96},{96,112},{112,128},... | collective-permute-start | bytes 764936 | tf_op jit(solution)/shard_map/while/body/eval_jaxpr/ppermute | solution.py:13
  63.4 9.4 %collective-permute-start = (bf16[83,1536]{1,0:T(8,128)(2,1)}, bf16[83,1536]{1,0:T(8,128)(2,1)S(1)}, u32[]{:S(2)}, u32[]{:S(2)}) collective-permute-start(bf16[83,1536]{1,0:T(8,128)(2,1)} %get-tuple-element.121), channel_id=1, source_target_pairs={{0,16},{16,32},{32,48},{48,64},{64,80},{80,96},{96,112},{112,128},... | collective-permute-start | bytes 764936 | tf_op jit(solution)/shard_map/while/body/eval_jaxpr/ppermute | solution.py:13
  76.2 9.4 %collective-permute-start = (bf16[83,1536]{1,0:T(8,128)(2,1)}, bf16[83,1536]{1,0:T(8,128)(2,1)S(1)}, u32[]{:S(2)}, u32[]{:S(2)}) collective-permute-start(bf16[83,1536]{1,0:T(8,128)(2,1)} %get-tuple-element.121), channel_id=1, source_target_pairs={{0,16},{16,32},{32,48},{48,64},{64,80},{80,96},{96,112},{112,128},... | collective-permute-start | bytes 764936 | tf_op jit(solution)/shard_map/while/body/eval_jaxpr/ppermute | solution.py:13
  89.0 9.4 %collective-permute-start = (bf16[83,1536]{1,0:T(8,128)(2,1)}, bf16[83,1536]{1,0:T(8,128)(2,1)S(1)}, u32[]{:S(2)}, u32[]{:S(2)}) collective-permute-start(bf16[83,1536]{1,0:T(8,128)(2,1)} %get-tuple-element.121), channel_id=1, source_target_pairs={{0,16},{16,32},{32,48},{48,64},{64,80},{80,96},{96,112},{112,128},... | collective-permute-start | bytes 764936 | tf_op jit(solution)/shard_map/while/body/eval_jaxpr/ppermute | solution.py:13
  101.8 9.4 %collective-permute-start = (bf16[83,1536]{1,0:T(8,128)(2,1)}, bf16[83,1536]{1,0:T(8,128)(2,1)S(1)}, u32[]{:S(2)}, u32[]{:S(2)}) collective-permute-start(bf16[83,1536]{1,0:T(8,128)(2,1)} %get-tuple-element.121), channel_id=1, source_target_pairs={{0,16},{16,32},{32,48},{48,64},{64,80},{80,96},{96,112},{112,128},... | collective-permute-start | bytes 764936 | tf_op jit(solution)/shard_map/while/body/eval_jaxpr/ppermute | solution.py:13
  114.6 9.4 %collective-permute-start = (bf16[83,1536]{1,0:T(8,128)(2,1)}, bf16[83,1536]{1,0:T(8,128)(2,1)S(1)}, u32[]{:S(2)}, u32[]{:S(2)}) collective-permute-start(bf16[83,1536]{1,0:T(8,128)(2,1)} %get-tuple-element.121), channel_id=1, source_target_pairs={{0,16},{16,32},{32,48},{48,64},{64,80},{80,96},{96,112},{112,128},... | collective-permute-start | bytes 764936 | tf_op jit(solution)/shard_map/while/body/eval_jaxpr/ppermute | solution.py:13
  127.4 9.4 %collective-permute-start = (bf16[83,1536]{1,0:T(8,128)(2,1)}, bf16[83,1536]{1,0:T(8,128)(2,1)S(1)}, u32[]{:S(2)}, u32[]{:S(2)}) collective-permute-start(bf16[83,1536]{1,0:T(8,128)(2,1)} %get-tuple-element.121), channel_id=1, source_target_pairs={{0,16},{16,32},{32,48},{48,64},{64,80},{80,96},{96,112},{112,128},... | collective-permute-start | bytes 764936 | tf_op jit(solution)/shard_map/while/body/eval_jaxpr/ppermute | solution.py:13
  140.2 10.0 %collective-permute-start = (bf16[83,1536]{1,0:T(8,128)(2,1)}, bf16[83,1536]{1,0:T(8,128)(2,1)S(1)}, u32[]{:S(2)}, u32[]{:S(2)}) collective-permute-start(bf16[83,1536]{1,0:T(8,128)(2,1)} %get-tuple-element.121), channel_id=1, source_target_pairs={{0,16},{16,32},{32,48},{48,64},{64,80},{80,96},{96,112},{112,128},... | collective-permute-start | bytes 764936 | tf_op jit(solution)/shard_map/while/body/eval_jaxpr/ppermute | solution.py:13
  153.5 11.0 %collective-permute-start = (bf16[83,1536]{1,0:T(8,128)(2,1)}, bf16[83,1536]{1,0:T(8,128)(2,1)S(1)}, u32[]{:S(2)}, u32[]{:S(2)}) collective-permute-start(bf16[83,1536]{1,0:T(8,128)(2,1)} %get-tuple-element.121), channel_id=1, source_target_pairs={{0,16},{16,32},{32,48},{48,64},{64,80},{80,96},{96,112},{112,128},... | collective-permute-start | bytes 764936 | tf_op jit(solution)/shard_map/while/body/eval_jaxpr/ppermute | solution.py:13
  168.0 12.2 %collective-permute-start = (bf16[83,1536]{1,0:T(8,128)(2,1)}, bf16[83,1536]{1,0:T(8,128)(2,1)S(1)}, u32[]{:S(2)}, u32[]{:S(2)}) collective-permute-start(bf16[83,1536]{1,0:T(8,128)(2,1)} %get-tuple-element.121), channel_id=1, source_target_pairs={{0,16},{16,32},{32,48},{48,64},{64,80},{80,96},{96,112},{112,128},... | collective-permute-start | bytes 764936 | tf_op jit(solution)/shard_map/while/body/eval_jaxpr/ppermute | solution.py:13
  183.6 11.8 %collective-permute-start = (bf16[83,1536]{1,0:T(8,128)(2,1)}, bf16[83,1536]{1,0:T(8,128)(2,1)S(1)}, u32[]{:S(2)}, u32[]{:S(2)}) collective-permute-start(bf16[83,1536]{1,0:T(8,128)(2,1)} %get-tuple-element.121), channel_id=1, source_target_pairs={{0,16},{16,32},{32,48},{48,64},{64,80},{80,96},{96,112},{112,128},... | collective-permute-start | bytes 764936 | tf_op jit(solution)/shard_map/while/body/eval_jaxpr/ppermute | solution.py:13
  198.7 10.9 %collective-permute-start = (bf16[83,1536]{1,0:T(8,128)(2,1)}, bf16[83,1536]{1,0:T(8,128)(2,1)S(1)}, u32[]{:S(2)}, u32[]{:S(2)}) collective-permute-start(bf16[83,1536]{1,0:T(8,128)(2,1)} %get-tuple-element.121), channel_id=1, source_target_pairs={{0,16},{16,32},{32,48},{48,64},{64,80},{80,96},{96,112},{112,128},... | collective-permute-start | bytes 764936 | tf_op jit(solution)/shard_map/while/body/eval_jaxpr/ppermute | solution.py:13
  213.0 9.9 %collective-permute-start = (bf16[83,1536]{1,0:T(8,128)(2,1)}, bf16[83,1536]{1,0:T(8,128)(2,1)S(1)}, u32[]{:S(2)}, u32[]{:S(2)}) collective-permute-start(bf16[83,1536]{1,0:T(8,128)(2,1)} %get-tuple-element.121), channel_id=1, source_target_pairs={{0,16},{16,32},{32,48},{48,64},{64,80},{80,96},{96,112},{112,128},... | collective-permute-start | bytes 764936 | tf_op jit(solution)/shard_map/while/body/eval_jaxpr/ppermute | solution.py:13
  226.3 7.0 copy-start.5
  228.7 0.8 copy-start.2
  233.3 465.4 %all-reduce.6.cloned.1.call-start = ((), (), s32[]{:S(2)}) async-start(), calls=%async_computation.1 | async-start | bytes 8388608
Sparse Core Ops, SparseCore 0:
  233.4 189.7 all-reduce.3
  429.6 269.0 all-reduce.5
where the time goes:
time: 710 us; the launch traced here: 708 us
  waiting for transfers between devices  541 us (76%)
  blocking collectives  61.2 us (9%)
  other arithmetic  44.6 us (6%)
  matrix products  23 us (3%)
  local copies, waits for them, and re-layouts  19.8 us (3%)
  between operations  15.9 us (2%)
    unnamed x3, waiting for transfers between devices  273 us
    ppermute x15, waiting for transfers between devices, from_behind(): lax.ppermute(value, axis, [(i, (i + by) % size) for i in range(size)])  153 us
    psum x1, waiting for transfers between devices, on_device(): loss_total, second_total = lax.psum((loss_local, second_local), 'space')  115 us
    psum x1, blocking collectives, on_device(): loss_total, second_total = lax.psum((loss_local, second_local), 'space')  61.2 us
    add x15, other arithmetic, cycle_step(): return (moving, value_sum + smooth_abs, slope_sum + spread / smooth_abs)  39.7 us
  transfers between devices with their start and end apart: 17, of which 17 were waited for; matrix products, arithmetic and copies ran while one was open for 2% of the time, Pallas kernels for 0%

commit v1 on v0

v1 whole, which is shorter than its diff:
```python
import math

import jax
import jax.numpy as jnp
from jax import lax
from jax.experimental import pallas as pl
from jax.experimental.pallas import tpu as pltpu
from jax.sharding import Mesh
from jax.sharding import PartitionSpec as P

BF = jnp.bfloat16
F32 = jnp.float32
EPS = 0.01
C, H, H2 = 83, 1024, 1024
PTS = 1536
NPTS = 24576
MEMBERS = 16
GROUPS, USED, ROWS, LANES = 4, 21, 24, 384
PAD = GROUPS * ROWS
STEP = 512
HI, LO = 21, 22
VMEM = 60 * 1024 * 1024
NT = (((1,), (1,)), ((), ()))


def params(**more):
    return pltpu.CompilerParams(vmem_limit_bytes=VMEM, **more)


def whole(shape):
    return pl.BlockSpec(shape, lambda *_: (0,) * len(shape))


def forward_kernel(lat_ref, w1_ref, w2_ref, hid_ref, der_ref, blk_ref, w2t_ref, w2p, field):
    step = pl.program_id(0)

    @pl.when(step == 0)
    def _():
        w2 = jnp.concatenate([w2_ref[...].astype(F32), jnp.zeros((1, H2), F32)], 0)
        gap = jnp.zeros((ROWS - USED, H2), F32)
        parts = []
        for g in range(GROUPS):
            parts += [w2[g * USED : (g + 1) * USED], gap]
        padded = jnp.concatenate(parts, 0)
        w2p[...] = padded.astype(BF)
        tall = jnp.concatenate([padded, jnp.zeros((128 - PAD, H2), F32)], 0)
        w2t_ref[...] = tall.T.astype(BF)

    lat = lat_ref[0]
    total = jnp.zeros((PAD, STEP), F32)
    rows = 256
    for r in range(0, H2, rows):
        pre = jnp.dot(w1_ref[r : r + rows, :], lat, preferred_element_type=F32)
        sig = 0.5 * jnp.tanh(0.5 * pre) + 0.5
        act = pre * sig
        hid = act.astype(BF)
        hid_ref[r : r + rows, :] = hid
        der_ref[r : r + rows, :] = (sig + act * (1.0 - sig)).astype(BF)
        total += jnp.dot(w2p[:, r : r + rows], hid, preferred_element_type=F32)
    field[:, pl.ds(pl.multiple_of(step * STEP, STEP), STEP)] = total

    @pl.when(step == PTS // STEP - 1)
    def _():
        for g in range(GROUPS):
            for q in range(PTS // LANES):
                blk_ref[g * GROUPS + q] = field[
                    g * ROWS : (g + 1) * ROWS, q * LANES : (q + 1) * LANES
                ].astype(BF)


def forward(latent, w_first, w_second):
    return pl.pallas_call(
        forward_kernel,
        grid=(PTS // STEP,),
        in_specs=[
            pl.BlockSpec((1, H, STEP), lambda s: (0, 0, s)),
            whole((H2, H)),
            whole((C, H2)),
        ],
        out_specs=[
            pl.BlockSpec((H2, STEP), lambda s: (0, s)),
            pl.BlockSpec((H2, STEP), lambda s: (0, s)),
            whole((16, ROWS, LANES)),
            whole((H2, 128)),
        ],
        out_shape=[
            jax.ShapeDtypeStruct((H2, PTS), BF),
            jax.ShapeDtypeStruct((H2, PTS), BF),
            jax.ShapeDtypeStruct((16, ROWS, LANES), BF),
            jax.ShapeDtypeStruct((H2, 128), BF),
        ],
        scratch_shapes=[pltpu.VMEM((PAD, H2), BF), pltpu.VMEM((PAD, PTS), F32)],
        compiler_params=params(),
        name="forward",
    )(latent, w_first, w_second)


def pair_kernel(fields_ref, truth_ref, area_ref, out_ref, values, grads):
    lane_tiles = LANES // 128
    spots = (ROWS // 8) * lane_tiles
    for m in range(MEMBERS):
        block = fields_ref[m].astype(F32)
        for r in range(ROWS // 8):
            for l in range(lane_tiles):
                values[r * lane_tiles + l, m] = block[
                    r * 8 : (r + 1) * 8, l * 128 : (l + 1) * 128
                ]

    def spot(index, losses):
        v = [values[index, m] for m in range(MEMBERS)]
        truth = truth_ref[index]
        area = area_ref[index]
        value = [None] * MEMBERS
        slope = [None] * MEMBERS

        def add(store, m, term):
            store[m] = term if store[m] is None else store[m] + term

        for m in range(MEMBERS):
            for k in range(m + 1, MEMBERS):
                d = v[m] - v[k]
                square = d * d + EPS
                inverse = lax.rsqrt(square)
                s = square * inverse
                t = d * inverse
                add(value, m, s)
                add(value, k, s)
                add(slope, m, t)
                slope[k] = -t if slope[k] is None else slope[k] - t
        new = []
        for m in range(MEMBERS):
            gap = v[m] - truth
            square = gap * gap + EPS
            inverse = lax.rsqrt(square)
            grads[index, m] = area * (
                gap * inverse * (1.0 / MEMBERS)
                - slope[m] * (1.0 / (MEMBERS * (MEMBERS - 1)))
            )
            new.append(area * (square * inverse - value[m] * (1.0 / (2.0 * (MEMBERS - 1)))))
        return [a + b for a, b in zip(losses, new)]

    zero = [jnp.zeros((8, 128), F32) for _ in range(MEMBERS)]
    row = lax.broadcasted_iota(jnp.int32, (8, 128), 0)
    last = ROWS // 8 - 1
    for l in range(lane_tiles):
        losses = lax.fori_loop(
            0, ROWS // 8, lambda r, carry: spot(r * lane_tiles + l, carry), zero
        )
        for m in range(MEMBERS):
            loss = jnp.sum(losses[m], axis=0, keepdims=True)
            high = loss.astype(BF).astype(F32)
            low = loss - high
            at = last * lane_tiles + l
            kept = grads[at, m]
            grads[at, m] = jnp.where(
                row == HI - 8 * last, high, jnp.where(row == LO - 8 * last, low, kept)
            )
    for m in range(MEMBERS):
        out_ref[m] = jnp.concatenate(
            [
                jnp.concatenate([grads[r * lane_tiles + l, m] for l in range(lane_tiles)], 1)
                for r in range(ROWS // 8)
            ],
            0,
        ).astype(BF)


def pairs(fields, truth, area):
    spots = ROWS // 8 * (LANES // 128)
    return pl.pallas_call(
        pair_kernel,
        out_shape=jax.ShapeDtypeStruct((16, ROWS, LANES), BF),
        in_specs=[pl.BlockSpec(memory_space=pltpu.VMEM)] * 3,
        out_specs=pl.BlockSpec(memory_space=pltpu.VMEM),
        scratch_shapes=[
            pltpu.VMEM((spots, MEMBERS, 8, 128), F32),
            pltpu.VMEM((spots, MEMBERS, 8, 128), F32),
        ],
        compiler_params=params(),
        name="pairs",
    )(fields, truth, area)


def arrange(rows):
    out = []
    for x in range(4):
        for y in range(4):
            pick = [rows[x * 64 + zh * 32 + y * 8 : x * 64 + zh * 32 + y * 8 + 8] for zh in range(2)]
            out.append(jnp.concatenate(pick, 0))
    return out


def back_kernel(
    core_ref, blk_ref, hid_ref, der_ref, lat_ref, w2t_ref,
    grad_ref, bp_ref, send_ref, second_ref, low, first,
):
    step = pl.program_id(0)

    @pl.when(step == 0)
    def _():
        for q in range(PTS // LANES):
            cols = pl.ds(q * LANES, LANES)
            parts = [blk_ref[g * GROUPS + q].astype(F32) for g in range(GROUPS)]
            for g in range(GROUPS):
                used = min(USED, C - g * USED)
                grad_ref[0, g * USED : g * USED + used, cols] = parts[g][:used]
            low[:, cols] = jnp.concatenate(
                parts + [jnp.zeros((128 - PAD, LANES), F32)], 0
            ).astype(BF)

    low_now = low[:, pl.ds(pl.multiple_of(step * STEP, STEP), STEP)]
    back = jnp.dot(w2t_ref[...], low_now, preferred_element_type=F32)
    bp = (back * der_ref[...].astype(F32)).astype(BF)
    bp_ref[...] = bp
    second = lax.dot_general(low_now, hid_ref[...], NT, preferred_element_type=F32)[:PAD]
    part = lax.dot_general(bp, lat_ref[0], NT, preferred_element_type=F32)

    @pl.when(step == 0)
    def _():
        second_ref[...] = second
        first[...] = part

    @pl.when(step > 0)
    def _():
        second_ref[...] += second
        first[...] += part

    @pl.when(step == PTS // STEP - 1)
    def _():
        for z in range(4):
            for e, piece in enumerate(arrange(first[z * 256 : (z + 1) * 256, :])):
                send_ref[e, z * 16 : (z + 1) * 16, :] = piece.astype(BF)
        row = lax.broadcasted_iota(jnp.int32, (8, LANES), 0)
        total = jnp.zeros((1, LANES), F32)
        for e in range(16):
            block = blk_ref[e].astype(F32)
            total += block[HI : HI + 1] + block[LO : LO + 1]
        high = total.astype(BF).astype(F32)
        top = ROWS - 8
        second_ref[top:ROWS, :LANES] = jnp.where(
            row == HI - top, high, jnp.where(row == LO - top, total - high, second_ref[top:ROWS, :LANES])
        )


def backward(core, blocks, hidden, deriv, latent, w2t):
    half = H // 2
    return pl.pallas_call(
        back_kernel,
        grid_spec=pltpu.PrefetchScalarGridSpec(
            num_scalar_prefetch=1,
            grid=(PTS // STEP,),
            in_specs=[
                whole((16, ROWS, LANES)),
                pl.BlockSpec((H2, STEP), lambda s, c: (0, s)),
                pl.BlockSpec((H2, STEP), lambda s, c: (0, s)),
                pl.BlockSpec((1, half, STEP), lambda s, c: (0, 1 - c[0], s)),
                whole((H2, 128)),
            ],
            out_specs=[
                whole((1, C, PTS)),
                pl.BlockSpec((H2, STEP), lambda s, c: (0, s)),
                whole((16, 64, half)),
                whole((PAD, H2)),
            ],
            scratch_shapes=[pltpu.VMEM((128, PTS), BF), pltpu.VMEM((H2, half), F32)],
        ),
        out_shape=[
            jax.ShapeDtypeStruct((1, C, PTS), F32),
            jax.ShapeDtypeStruct((H2, PTS), BF),
            jax.ShapeDtypeStruct((16, 64, half), BF),
            jax.ShapeDtypeStruct((PAD, H2), F32),
        ],
        compiler_params=params(),
        name="backward",
    )(core, blocks, hidden, deriv, latent, w2t)


def own_kernel(core_ref, bp_ref, lat_ref, out_ref):
    part = lax.dot_general(bp_ref[...], lat_ref[0], NT, preferred_element_type=F32)
    for e, piece in enumerate(arrange(part)):
        out_ref[e] = piece


def own_half(core, bp, latent):
    half = H // 2
    return pl.pallas_call(
        own_kernel,
        grid_spec=pltpu.PrefetchScalarGridSpec(
            num_scalar_prefetch=1,
            grid=(4,),
            in_specs=[
                pl.BlockSpec((256, PTS), lambda z, c: (z, 0)),
                pl.BlockSpec((1, half, PTS), lambda z, c: (0, c[0], 0)),
            ],
            out_specs=pl.BlockSpec((16, 16, half), lambda z, c: (0, z, 0)),
        ),
        out_shape=jax.ShapeDtypeStruct((16, 64, half), F32),
        compiler_params=params(),
        cost_estimate=pl.CostEstimate(
            flops=2 * H2 * half * PTS, bytes_accessed=7 * 1024 * 1024, transcendentals=0
        ),
        name="own_half",
    )(core, bp, latent)


def swap(value, axis, by):
    size = lax.axis_size(axis)
    return lax.ppermute(value, axis, [(i, i ^ by) for i in range(size)])


def packed(total):
    row = lax.broadcasted_iota(jnp.int32, total.shape, 0)
    loss = total[HI : HI + 1] + total[LO : LO + 1]
    high = lax.reduce_precision(loss, 8, 7)
    return jnp.where(row == HI, high, jnp.where(row == LO, loss - high, total)).astype(BF)


def on_device(latent, truth, w_first, w_second):
    core = lax.axis_index("c").astype(jnp.int32)
    group, quarter = lax.axis_index("zl"), lax.axis_index("x")
    place = (lax.axis_index("zh") * 4 + lax.axis_index("y")) * 2 + lax.axis_index("c")

    hidden, deriv, blocks, w2t = forward(latent, w_first, w_second)

    position = (place * PTS + quarter * LANES + jnp.arange(LANES)).astype(F32)
    area = jnp.cos(math.pi * ((position + 0.5) / NPTS - 0.5))
    rows = jnp.arange(ROWS)
    valid = (rows < USED) & (group * USED + rows < C)
    area = jnp.where(valid[:, None], area[None], 0.0)
    truth_pad = jnp.pad(truth, ((0, GROUPS * USED + ROWS - USED - C), (0, 0)))
    truth_here = lax.dynamic_slice(truth_pad, (group * USED, quarter * LANES), (ROWS, LANES))

    def spots(value):
        value = value.reshape(ROWS // 8, 8, LANES // 128, 128)
        return value.transpose(0, 2, 1, 3).reshape(-1, 8, 128)

    area, truth_here = spots(area), spots(truth_here.astype(F32))

    gathered = lax.all_to_all(blocks, ("zl", "x"), 0, 0, tiled=True)
    grads = pairs(gathered, truth_here, area)
    grads = lax.all_to_all(grads, ("zl", "x"), 0, 0, tiled=True)

    field_grad, bp, send, second = backward(core[None], grads, hidden, deriv, latent, w2t)

    arrived = swap(send, "c", 1)
    own = own_half(core[None], bp, latent)
    first = (own + arrived.astype(F32)).astype(BF)

    first = lax.all_to_all(first, ("x", "y"), 0, 0, tiled=True)
    first = jnp.sum(first.astype(F32), 0).astype(BF).reshape(8, 8, H // 2)
    first = lax.all_to_all(first, ("zl", "zh"), 0, 0, tiled=True)
    first = jnp.sum(first.astype(F32), 0) * (1.0 / math.sqrt(MEMBERS * NPTS))
    low, high = first[:4], first[4:]
    mine = jnp.where(core == 0, low, high)
    other = swap(jnp.where(core == 0, high, low), "c", 1)
    first_out = jnp.concatenate(
        [jnp.where(core == 0, mine, other), jnp.where(core == 0, other, mine)], 1
    )

    total = packed(second)
    for axis, by in (("c", 1), ("y", 1), ("y", 2), ("zh", 1)):
        got = swap(total, axis, by)
        summed = total.astype(F32) + got.astype(F32)
        total = packed(summed)
    loss = (jnp.sum(summed[HI, :LANES] + summed[LO, :LANES]) / NPTS)[None]
    kept = summed.reshape(GROUPS, ROWS, H2)[:, :USED].reshape(GROUPS * USED, H2)[:C]
    second_out = (kept * (MEMBERS / math.sqrt(NPTS)))[None]
    return loss, field_grad, first_out, second_out


def solution(mesh):
    fine = Mesh(mesh.devices.reshape(4, 4, 2, 4, 2), ("zl", "x", "zh", "y", "c"))
    ens, space = ("zl", "x"), ("zh", "y", "c")
    in_specs = (P(ens, None, space), P(None, space), P(), P())
    out_specs = (P(ens), P(ens, None, space), P(ens + space, None), P(ens, None, None))
    return jax.shard_map(
        on_device, mesh=fine, in_specs=in_specs, out_specs=out_specs, check_vma=False
    )
```

time: 710 us -> 121 us (0.17)
  waiting for transfers between devices: 541 us -> 34.9 us
  blocking collectives: 61.2 us -> 0 us
  starting transfers between devices: 2.24 us -> 38.7 us
  other arithmetic: 44.6 us -> 11.1 us
  Pallas kernels: 0 us -> 28.8 us
  matrix products: 23 us -> 0 us
  local copies, waits for them, and re-layouts: 19.8 us -> 3.91 us
  between operations: 15.9 us -> 2.64 us
    unnamed x3 -> x0, waiting for transfers between devices: 273 us -> none
    ppermute x15 -> x6, waiting for transfers between devices: 153 us -> 6.9 us  [swap(): return lax.ppermute(value, axis, [(i, i ^ by) for i in range(size)])]
    psum x1 -> x0, waiting for transfers between devices: 115 us -> none  [on_device(): loss_total, second_total = lax.psum((loss_local, second_local), 'space')]
    psum x1 -> x0, blocking collectives: 61.2 us -> none  [on_device(): loss_total, second_total = lax.psum((loss_local, second_local), 'space')]
    add x15 -> x4, other arithmetic: 39.7 us -> 1.25 us  [on_device(): summed = total.astype(F32) + got.astype(F32)]
    pallas_call x0 -> x4, Pallas kernels: none -> 28.8 us  [the longest x1 10.4 us: forward(): pl.pallas_call(forward_kernel, grid=(PTS // STEP,), in_specs=[pl.BlockSpe...]
    all_to_all x0 -> x4, waiting for transfers between devices: none -> 28 us  [the longest x1 9.11 us: on_device(): grads = lax.all_to_all(grads, ('zl', 'x'), 0, 0, tiled=True)]
    dot_general x4 -> x0, matrix products: 23 us -> none  [the longest x1 10.3 us: on_device(): lax.dot_general(back_pre, latent_one, (((1,), (1,)), ((), ())), preferred...]
  transfers between devices with their start and end apart: 17 -> 10, of which waited for: 17 -> 6; matrix products, arithmetic and copies ran while one was open for 2% -> 8% of each run, Pallas kernels for 0% -> 5%
where the time goes in v1:
time: 121 us; the launch traced here: 120 us
  starting transfers between devices  38.7 us (32%)
  waiting for transfers between devices  34.9 us (29%)
  Pallas kernels  28.8 us (24%)
  other arithmetic  11.1 us (9%)
  local copies, waits for them, and re-layouts  3.91 us (3%)
  between operations  2.64 us (2%)
    ppermute x6, starting transfers between devices, swap(): return lax.ppermute(value, axis, [(i, i ^ by) for i in range(size)])  16.2 us
    pallas_call x1, Pallas kernels, forward(): pl.pallas_call(forward_kernel, grid=(PTS // STEP,), in_specs=[pl.BlockSpe...  10.4 us
    all_to_all x1, waiting for transfers between devices, on_device(): grads = lax.all_to_all(grads, ('zl', 'x'), 0, 0, tiled=True)  9.11 us
    pallas_call x1, Pallas kernels, backward(): pl.pallas_call(back_kernel, grid_spec=pltpu.PrefetchScalarGridSpec(num_sc...  9.07 us
    all_to_all x1, starting transfers between devices, on_device(): gathered = lax.all_to_all(blocks, ('zl', 'x'), 0, 0, tiled=True)  9.03 us
    all_to_all x1, waiting for transfers between devices, on_device(): gathered = lax.all_to_all(blocks, ('zl', 'x'), 0, 0, tiled=True)  8.55 us
    ppermute x6, waiting for transfers between devices, swap(): return lax.ppermute(value, axis, [(i, i ^ by) for i in range(size)])  6.9 us
    all_to_all x1, waiting for transfers between devices, on_device(): first = lax.all_to_all(first, ('zl', 'zh'), 0, 0, tiled=True)  6.58 us
  transfers between devices with their start and end apart: 10, of which 6 were waited for; matrix products, arithmetic and copies ran while one was open for 8% of the time, Pallas kernels for 5%

profile of v1, /device:TPU:1, one launch (start us, length us, event | category | flops | bytes accessed | tf_op | source)
XLA Modules:
  0.0 119.9 jit_solution(15145934010913507986)
XLA Ops:
  0.6 10.4 %forward.1 = (bf16[1024,1536]{1,0:T(8,128)(2,1)}, bf16[1024,1536]{1,0:T(8,128)(2,1)}, bf16[16,24,384]{2,1,0:T(8,128)(2,1)}, bf16[1024,128]{1,0:T(8,128)(2,1)}) custom-call(bf16[1,1024,1536]{2,1,0:T(8,128)(2,1)} %lat_ref.5, bf16[1024,1024]{1,0:T(8,128)(2,1)} %w1_ref.1, bf16[83,1024]{1,0:T(8,128)(2,1)} %w2_ref.1), custom_call_target="tpu_custom_call" | custom-call | tf_op jit(solution)/shard_map/forward/pallas_call | solution.py:72
  11.0 9.0 %all-to-all-start = ((bf16[16,24,384]{2,1,0:T(8,128)(2,1)}), bf16[16,24,384]{2,1,0:T(8,128)(2,1)S(1)}, u32[]{:S(2)}, u32[]{:S(2)}) async-start(bf16[16,24,384]{2,1,0:T(8,128)(2,1)} %get-tuple-element.12), calls=%async_computation | async-start | bytes 589824 | tf_op jit(solution)/shard_map/all_to_all | solution.py:339
  20.2 0.7 bitcast_convert_fusion
  20.9 0.7 broadcast_select_fusion.area_ref
  21.6 8.6 %all-to-all-done.fields_ref = bf16[16,24,384]{2,1,0:T(8,128)(2,1)S(1)} async-done(((bf16[16,24,384]{2,1,0:T(8,128)(2,1)}), bf16[16,24,384]{2,1,0:T(8,128)(2,1)S(1)}, u32[]{:S(2)}, u32[]{:S(2)}) %all-to-all-start) | async-done | bytes 294944 | tf_op jit(solution)/shard_map/all_to_all | solution.py:339
  30.1 0.7 copy-done.1
  30.8 3.7 %pairs.1 = bf16[16,24,384]{2,1,0:T(8,128)(2,1)} custom-call(bf16[16,24,384]{2,1,0:T(8,128)(2,1)} %copy-done.1, f32[9,8,128]{2,1,0:T(8,128)} %bitcast.22, f32[9,8,128]{2,1,0:T(8,128)} %broadcast_select_fusion.area_ref), custom_call_target="tpu_custom_call" | custom-call | tf_op jit(solution)/shard_map/pairs/pallas_call | solution.py:170
  34.6 4.2 %all-to-all-start.1 = ((bf16[16,24,384]{2,1,0:T(8,128)(2,1)}), bf16[16,24,384]{2,1,0:T(8,128)(2,1)S(1)}, u32[]{:S(2)}, u32[]{:S(2)}) async-start(bf16[16,24,384]{2,1,0:T(8,128)(2,1)} %pairs.1), calls=%async_computation.1 | async-start | bytes 589824 | tf_op jit(solution)/shard_map/all_to_all | solution.py:341
  38.8 9.1 %all-to-all-done.1.blk_ref = bf16[16,24,384]{2,1,0:T(8,128)(2,1)S(1)} async-done(((bf16[16,24,384]{2,1,0:T(8,128)(2,1)}), bf16[16,24,384]{2,1,0:T(8,128)(2,1)S(1)}, u32[]{:S(2)}, u32[]{:S(2)}) %all-to-all-start.1) | async-done | bytes 294944 | tf_op jit(solution)/shard_map/all_to_all | solution.py:341
  47.9 0.7 copy-done
  48.6 9.1 %backward.1 = (f32[1,83,1536]{2,1,0:T(8,128)}, bf16[1024,1536]{1,0:T(8,128)(2,1)}, bf16[16,64,512]{2,1,0:T(8,128)(2,1)}, f32[96,1024]{1,0:T(8,128)}) custom-call(s32[1]{0:T(128)} %bitcast.core_ref, bf16[16,24,384]{2,1,0:T(8,128)(2,1)} %copy-done, bf16[1024,1536]{1,0:T(8,128)(2,1)} %get-tuple-element.13.hid_ref, ...), custom_call_target="tpu_custom_call" | custom-call | tf_op jit(solution)/shard_map/backward/pallas_call | solution.py:247
  57.7 0.8 fusion.4
  58.5 1.1 select_convert_fusion.3
  59.6 3.1 %collective-permute-start = (bf16[96,1024]{1,0:T(8,128)(2,1)S(1)}, bf16[96,1024]{1,0:T(8,128)(2,1)S(1)}, u32[]{:S(2)}, u32[]{:S(2)}) collective-permute-start(bf16[96,1024]{1,0:T(8,128)(2,1)S(1)} %select_convert_fusion.3), channel_id=1, source_target_pairs={{0,1},{1,0},{2,3},{3,2},{4,5},{5,4},{6,7},{7,6},{8,9},{9,8},{10,11... | collective-permute-start | bytes 589832 | tf_op jit(solution)/shard_map/ppermute | solution.py:308
  62.8 1.0 collective-permute-done
  63.8 1.1 convert_add_fusion.3
  65.0 1.2 select_convert_fusion.2
  66.1 1.4 %collective-permute-start.1 = (bf16[96,1024]{1,0:T(8,128)(2,1)S(1)}, bf16[96,1024]{1,0:T(8,128)(2,1)S(1)}, u32[]{:S(2)}, u32[]{:S(2)}) collective-permute-start(bf16[96,1024]{1,0:T(8,128)(2,1)S(1)} %select_convert_fusion.2), channel_id=1, source_target_pairs={{0,2},{2,0},{4,6},{6,4},{1,3},{3,1},{5,7},{7,5},{8,10},{10,8},{12,... | collective-permute-start | bytes 589832 | tf_op jit(solution)/shard_map/ppermute | solution.py:308
  67.5 5.6 %own_half.1 = f32[16,64,512]{2,1,0:T(8,128)} custom-call(s32[1]{0:T(128)} %bitcast.core_ref, bf16[1024,1536]{1,0:T(8,128)(2,1)} %get-tuple-element.18.bp_ref, bf16[1,1024,1536]{2,1,0:T(8,128)(2,1)} %lat_ref.5), custom_call_target="tpu_custom_call" | custom-call | flops 1610612736 | bytes 7340032 | tf_op jit(solution)/shard_map/own_half/pallas_call | solution.py:286
  73.3 2.7 %collective-permute-start.2 = (bf16[96,1024]{1,0:T(8,128)(2,1)S(1)}, bf16[96,1024]{1,0:T(8,128)(2,1)S(1)}, u32[]{:S(2)}, u32[]{:S(2)}) collective-permute-start(bf16[96,1024]{1,0:T(8,128)(2,1)S(1)} %select_convert_fusion.1), channel_id=1, source_target_pairs={{0,4},{2,6},{4,0},{6,2},{1,5},{3,7},{5,1},{7,3},{8,12},{10,14},{12... | collective-permute-start | bytes 589832 | tf_op jit(solution)/shard_map/ppermute | solution.py:308
  76.1 2.9 %add_convert_fusion = bf16[16,64,512]{2,1,0:T(8,128)(2,1)} fusion(f32[16,64,512]{2,1,0:T(8,128)} %own_half.1, bf16[16,64,512]{2,1,0:T(8,128)(2,1)S(1)} %collective-permute-done.4), kind=kLoop, calls=%fused_computation | loop fusion | flops 1572864 | bytes 4194304 | tf_op jit(solution)/shard_map/convert_element_type | solution.py:347
  79.0 3.8 %all-to-all-start.2 = ((bf16[16,64,512]{2,1,0:T(8,128)(2,1)}), bf16[16,64,512]{2,1,0:T(8,128)(2,1)S(1)}, u32[]{:S(2)}, u32[]{:S(2)}) async-start(bf16[16,64,512]{2,1,0:T(8,128)(2,1)} %add_convert_fusion), calls=%async_computation.2 | async-start | bytes 2097152 | tf_op jit(solution)/shard_map/all_to_all | solution.py:349
  83.0 4.3 %collective-permute-start.3 = (bf16[96,1024]{1,0:T(8,128)(2,1)S(1)}, bf16[96,1024]{1,0:T(8,128)(2,1)S(1)}, u32[]{:S(2)}, u32[]{:S(2)}) collective-permute-start(bf16[96,1024]{1,0:T(8,128)(2,1)S(1)} %select_convert_fusion), channel_id=1, source_target_pairs={{0,8},{8,0},{1,9},{9,1},{2,10},{10,2},{3,11},{11,3},{4,12},{12,4},... | collective-permute-start | bytes 589832 | tf_op jit(solution)/shard_map/ppermute | solution.py:308
  87.3 1.3 %copy.11 = f32[1,83,1536]{2,0,1:T(1,128)} copy(f32[1,83,1536]{2,1,0:T(8,128)S(1)} %copy-done.2) | data formatting | bytes 1019904
  88.6 5.9 %collective-permute-done.3 = bf16[96,1024]{1,0:T(8,128)(2,1)S(1)} collective-permute-done((bf16[96,1024]{1,0:T(8,128)(2,1)S(1)}, bf16[96,1024]{1,0:T(8,128)(2,1)S(1)}, u32[]{:S(2)}, u32[]{:S(2)}) %collective-permute-start.3) | collective-permute-done | bytes 196640 | tf_op jit(solution)/shard_map/ppermute | solution.py:308
  94.6 3.7 %all-to-all-done.2 = bf16[16,64,512]{2,1,0:T(8,128)(2,1)S(1)} async-done(((bf16[16,64,512]{2,1,0:T(8,128)(2,1)}), bf16[16,64,512]{2,1,0:T(8,128)(2,1)S(1)}, u32[]{:S(2)}, u32[]{:S(2)}) %all-to-all-start.2) | async-done | bytes 1048608 | tf_op jit(solution)/shard_map/all_to_all | solution.py:349
  98.3 0.8 reduce_sum.31
  99.1 5.5 %all-to-all-start.3 = ((bf16[8,8,512]{2,1,0:T(8,128)(2,1)}), bf16[8,8,512]{2,1,0:T(8,128)(2,1)S(1)}, u32[]{:S(2)}, u32[]{:S(2)}) async-start(bf16[8,8,512]{2,1,0:T(8,128)(2,1)} %bitcast.13), calls=%async_computation.3 | async-start | bytes 131072 | tf_op jit(solution)/shard_map/all_to_all | solution.py:351
  104.6 6.6 %all-to-all-done.3 = bf16[8,8,512]{2,1,0:T(8,128)(2,1)S(1)} async-done(((bf16[8,8,512]{2,1,0:T(8,128)(2,1)}), bf16[8,8,512]{2,1,0:T(8,128)(2,1)S(1)}, u32[]{:S(2)}, u32[]{:S(2)}) %all-to-all-start.3) | async-done | bytes 65568 | tf_op jit(solution)/shard_map/all_to_all | solution.py:351
  111.2 4.6 %collective-permute-start.5 = (f32[4,512]{1,0:T(4,128)S(1)}, f32[4,512]{1,0:T(4,128)S(1)}, u32[]{:S(2)}, u32[]{:S(2)}) collective-permute-start(f32[4,512]{1,0:T(4,128)S(1)} %slice_select_fusion), channel_id=1, source_target_pairs={{0,1},{1,0},{2,3},{3,2},{4,5},{5,4},{6,7},{7,6},{8,9},{9,8},{10,11... | collective-permute-start | bytes 24584 | tf_op jit(solution)/shard_map/ppermute | solution.py:308
  116.4 1.1 copy.12
  118.2 0.6 pad_maximum_fusion
  (33 shorter events, 1.3 us)
Async XLA Ops:
  0.6 19.5 %copy-start.3 = (bf16[83,1536]{1,0:T(8,128)(2,1)S(1)}, bf16[83,1536]{1,0:T(8,128)(2,1)}, u32[]{:S(2)}) copy-start(bf16[83,1536]{1,0:T(8,128)(2,1)} %param.5) | copy-start | bytes 764932
  11.0 19.1 %all-to-all-start = ((bf16[16,24,384]{2,1,0:T(8,128)(2,1)}), bf16[16,24,384]{2,1,0:T(8,128)(2,1)S(1)}, u32[]{:S(2)}, u32[]{:S(2)}) async-start(bf16[16,24,384]{2,1,0:T(8,128)(2,1)} %get-tuple-element.12), calls=%async_computation | async-start | bytes 589824 | tf_op jit(solution)/shard_map/all_to_all | solution.py:339
  30.1 0.7 copy-start.1
  34.6 13.3 %all-to-all-start.1 = ((bf16[16,24,384]{2,1,0:T(8,128)(2,1)}), bf16[16,24,384]{2,1,0:T(8,128)(2,1)S(1)}, u32[]{:S(2)}, u32[]{:S(2)}) async-start(bf16[16,24,384]{2,1,0:T(8,128)(2,1)} %pairs.1), calls=%async_computation.1 | async-start | bytes 589824 | tf_op jit(solution)/shard_map/all_to_all | solution.py:341
  47.9 0.7 copy-start
  59.6 4.2 %collective-permute-start = (bf16[96,1024]{1,0:T(8,128)(2,1)S(1)}, bf16[96,1024]{1,0:T(8,128)(2,1)S(1)}, u32[]{:S(2)}, u32[]{:S(2)}) collective-permute-start(bf16[96,1024]{1,0:T(8,128)(2,1)S(1)} %select_convert_fusion.3), channel_id=1, source_target_pairs={{0,1},{1,0},{2,3},{3,2},{4,5},{5,4},{6,7},{7,6},{8,9},{9,8},{10,11... | collective-permute-start | bytes 589832 | tf_op jit(solution)/shard_map/ppermute | solution.py:308
  62.7 13.3 %collective-permute-start.4 = (bf16[16,64,512]{2,1,0:T(8,128)(2,1)}, bf16[16,64,512]{2,1,0:T(8,128)(2,1)S(1)}, u32[]{:S(2)}, u32[]{:S(2)}) collective-permute-start(bf16[16,64,512]{2,1,0:T(8,128)(2,1)} %get-tuple-element.19), channel_id=1, source_target_pairs={{0,1},{1,0},{2,3},{3,2},{4,5},{5,4},{6,7},{7,6},{8,9},{9,8},{10,11... | collective-permute-start | bytes 3145736 | tf_op jit(solution)/shard_map/ppermute | solution.py:308
  66.1 7.0 %collective-permute-start.1 = (bf16[96,1024]{1,0:T(8,128)(2,1)S(1)}, bf16[96,1024]{1,0:T(8,128)(2,1)S(1)}, u32[]{:S(2)}, u32[]{:S(2)}) collective-permute-start(bf16[96,1024]{1,0:T(8,128)(2,1)S(1)} %select_convert_fusion.2), channel_id=1, source_target_pairs={{0,2},{2,0},{4,6},{6,4},{1,3},{3,1},{5,7},{7,5},{8,10},{10,8},{12,... | collective-permute-start | bytes 589832 | tf_op jit(solution)/shard_map/ppermute | solution.py:308
  73.3 9.4 %collective-permute-start.2 = (bf16[96,1024]{1,0:T(8,128)(2,1)S(1)}, bf16[96,1024]{1,0:T(8,128)(2,1)S(1)}, u32[]{:S(2)}, u32[]{:S(2)}) collective-permute-start(bf16[96,1024]{1,0:T(8,128)(2,1)S(1)} %select_convert_fusion.1), channel_id=1, source_target_pairs={{0,4},{2,6},{4,0},{6,2},{1,5},{3,7},{5,1},{7,3},{8,12},{10,14},{12... | collective-permute-start | bytes 589832 | tf_op jit(solution)/shard_map/ppermute | solution.py:308
  79.0 8.3 %copy-start.2 = (f32[1,83,1536]{2,1,0:T(8,128)S(1)}, f32[1,83,1536]{2,1,0:T(8,128)}, u32[]{:S(2)}) copy-start(f32[1,83,1536]{2,1,0:T(8,128)} %get-tuple-element.29) | copy-start | bytes 1529860
  79.0 19.3 %all-to-all-start.2 = ((bf16[16,64,512]{2,1,0:T(8,128)(2,1)}), bf16[16,64,512]{2,1,0:T(8,128)(2,1)S(1)}, u32[]{:S(2)}, u32[]{:S(2)}) async-start(bf16[16,64,512]{2,1,0:T(8,128)(2,1)} %add_convert_fusion), calls=%async_computation.2 | async-start | bytes 2097152 | tf_op jit(solution)/shard_map/all_to_all | solution.py:349
  83.0 11.5 %collective-permute-start.3 = (bf16[96,1024]{1,0:T(8,128)(2,1)S(1)}, bf16[96,1024]{1,0:T(8,128)(2,1)S(1)}, u32[]{:S(2)}, u32[]{:S(2)}) collective-permute-start(bf16[96,1024]{1,0:T(8,128)(2,1)S(1)} %select_convert_fusion), channel_id=1, source_target_pairs={{0,8},{8,0},{1,9},{9,1},{2,10},{10,2},{3,11},{11,3},{4,12},{12,4},... | collective-permute-start | bytes 589832 | tf_op jit(solution)/shard_map/ppermute | solution.py:308
  99.1 12.1 %all-to-all-start.3 = ((bf16[8,8,512]{2,1,0:T(8,128)(2,1)}), bf16[8,8,512]{2,1,0:T(8,128)(2,1)S(1)}, u32[]{:S(2)}, u32[]{:S(2)}) async-start(bf16[8,8,512]{2,1,0:T(8,128)(2,1)} %bitcast.13), calls=%async_computation.3 | async-start | bytes 131072 | tf_op jit(solution)/shard_map/all_to_all | solution.py:351
  111.2 6.9 %collective-permute-start.5 = (f32[4,512]{1,0:T(4,128)S(1)}, f32[4,512]{1,0:T(4,128)S(1)}, u32[]{:S(2)}, u32[]{:S(2)}) collective-permute-start(f32[4,512]{1,0:T(4,128)S(1)} %slice_select_fusion), channel_id=1, source_target_pairs={{0,1},{1,0},{2,3},{3,2},{4,5},{5,4},{6,7},{7,6},{8,9},{9,8},{10,11... | collective-permute-start | bytes 24584 | tf_op jit(solution)/shard_map/ppermute | solution.py:308

commit v2 on v1

v2 whole, which is shorter than its diff:
```python
import functools
import math

import jax
import jax.numpy as jnp
from jax import lax
from jax.experimental import pallas as pl
from jax.experimental.pallas import tpu as pltpu
from jax.sharding import Mesh
from jax.sharding import PartitionSpec as P

BF = jnp.bfloat16
F32 = jnp.float32
EPS = 0.01
C, H, H2 = 83, 1024, 1024
PTS = 1536
NPTS = 24576
MEMBERS = 16
GROUPS, USED, ROWS, LANES = 4, 21, 24, 384
PAD = GROUPS * ROWS
WIDE = 512
HI, LO = 21, 22
FLOPS = 20_000_000_000
NT = (((1,), (1,)), ((), ()))
VM = pl.BlockSpec(memory_space=pltpu.VMEM)
HBM = pl.BlockSpec(memory_space=pltpu.HBM)
SCALAR = pl.BlockSpec(memory_space=pltpu.SMEM)


def params(mib=24):
    return pltpu.CompilerParams(vmem_limit_bytes=mib * 1024 * 1024)


def shape(dims, dtype=BF):
    return jax.ShapeDtypeStruct(dims, dtype)


def in_hbm(value):
    return pltpu.with_memory_space_constraint(value, pltpu.HBM)


def own_tiles(where_ref, all_truth_ref, truth_ref, area_ref):
    lane_tiles = LANES // 128
    group, quarter, place = where_ref[0], where_ref[1], where_ref[2]
    cols = pl.ds(pl.multiple_of(quarter * LANES, 128), LANES)
    all_truth = jnp.concatenate(
        [all_truth_ref[:, cols].astype(F32), jnp.zeros((GROUPS * USED + ROWS - USED - C, LANES), F32)], 0
    )
    truth_here = all_truth[:ROWS]
    for g in range(1, GROUPS):
        truth_here = jnp.where(group == g, all_truth[g * USED : g * USED + ROWS], truth_here)
    lane = lax.broadcasted_iota(jnp.int32, (ROWS, LANES), 1)
    row = lax.broadcasted_iota(jnp.int32, (ROWS, LANES), 0)
    position = (place * PTS + quarter * LANES + lane).astype(F32)
    area_here = jnp.cos(math.pi * ((position + 0.5) / NPTS - 0.5))
    area_here = jnp.where((row < USED) & (group * USED + row < C), area_here, 0.0)
    for r in range(ROWS // 8):
        for l in range(lane_tiles):
            tile = (slice(r * 8, (r + 1) * 8), slice(l * 128, (l + 1) * 128))
            truth_ref[r * lane_tiles + l] = truth_here[tile]
            area_ref[r * lane_tiles + l] = area_here[tile]


def forward_kernel(
    where_ref, lat_hbm, w1_hbm, w2_hbm, truth_hbm,
    hid_ref, der_ref, lat_ref, blk_ref, w2t_ref, truth_ref, area_ref,
    w1, w2_ref, all_truth, w2p, field, sems,
):
    halves, spans = 2, PTS // WIDE
    rows = H2 // halves
    w1_in = [
        pltpu.make_async_copy(
            w1_hbm.at[r * rows : (r + 1) * rows], w1.at[r * rows : (r + 1) * rows], sems.at[r]
        )
        for r in range(halves)
    ]
    lat_in = [
        pltpu.make_async_copy(
            lat_hbm.at[0, :, n * WIDE : (n + 1) * WIDE],
            lat_ref.at[:, n * WIDE : (n + 1) * WIDE],
            sems.at[halves + n],
        )
        for n in range(spans)
    ]
    w2_in = pltpu.make_async_copy(w2_hbm, w2_ref, sems.at[halves + spans])
    truth_in = pltpu.make_async_copy(truth_hbm, all_truth, sems.at[halves + spans + 1])
    for copy in [w2_in, truth_in, w1_in[0], lat_in[0]] + w1_in[1:] + lat_in[1:]:
        copy.start()
    w2_in.wait()
    w2 = jnp.concatenate([w2_ref[...].astype(F32), jnp.zeros((1, H2), F32)], 0)
    gap = jnp.zeros((ROWS - USED, H2), F32)
    parts = []
    for g in range(GROUPS):
        parts += [w2[g * USED : (g + 1) * USED], gap]
    padded = jnp.concatenate(parts, 0)
    w2p[...] = padded.astype(BF)
    w2t_ref[...] = jnp.concatenate([padded, jnp.zeros((128 - PAD, H2), F32)], 0).T.astype(BF)

    def decode(n):
        cols = slice(n * WIDE, (n + 1) * WIDE)
        field[:, cols] = jnp.dot(w2p[...], hid_ref[:, cols], preferred_element_type=F32)

    for n in range(spans):
        lat_in[n].wait()
        if n == 1:
            truth_in.wait()
            own_tiles(where_ref, all_truth, truth_ref, area_ref)
        cols = slice(n * WIDE, (n + 1) * WIDE)
        for r in range(halves):
            if n == 0:
                w1_in[r].wait()
            here = slice(r * rows, (r + 1) * rows)
            pre = jnp.dot(w1[here, :], lat_ref[:, cols], preferred_element_type=F32)
            sig = 0.5 * jnp.tanh(0.5 * pre) + 0.5
            act = pre * sig
            hid_ref[here, cols] = act.astype(BF)
            der_ref[here, cols] = (sig + act * (1.0 - sig)).astype(BF)
        if n > 0:
            decode(n - 1)
    decode(spans - 1)
    for g in range(GROUPS):
        for q in range(PTS // LANES):
            blk_ref[g * GROUPS + q] = field[
                g * ROWS : (g + 1) * ROWS, q * LANES : (q + 1) * LANES
            ].astype(BF)


def forward(where, latent, w_first, w_second, truth):
    spots = ROWS // 8 * (LANES // 128)
    return pl.pallas_call(
        forward_kernel,
        in_specs=[SCALAR, HBM, HBM, HBM, HBM],
        out_specs=[VM] * 7,
        out_shape=[
            shape((H2, PTS)),
            shape((H2, PTS)),
            shape((H, PTS)),
            shape((16, ROWS, LANES)),
            shape((H2, 128)),
            shape((spots, 8, 128), F32),
            shape((spots, 8, 128), F32),
        ],
        scratch_shapes=[
            pltpu.VMEM((H2, H), BF),
            pltpu.VMEM((C, H2), BF),
            pltpu.VMEM((C, PTS), BF),
            pltpu.VMEM((PAD, H2), BF),
            pltpu.VMEM((PAD, PTS), F32),
            pltpu.SemaphoreType.DMA((4 + PTS // WIDE,)),
        ],
        compiler_params=params(12),
        name="forward",
    )(where, in_hbm(latent), in_hbm(w_first), in_hbm(w_second), in_hbm(truth))


def pair_kernel(fields_ref, truth_ref, area_ref, out_ref, values, grads):
    lane_tiles = LANES // 128
    for m in range(MEMBERS):
        block = fields_ref[m].astype(F32)
        for r in range(ROWS // 8):
            for l in range(lane_tiles):
                values[r * lane_tiles + l, m] = block[
                    r * 8 : (r + 1) * 8, l * 128 : (l + 1) * 128
                ]

    def spot(index, losses):
        v = [values[index, m] for m in range(MEMBERS)]
        truth = truth_ref[index]
        area = area_ref[index]
        value = [None] * MEMBERS
        slope = [None] * MEMBERS

        def add(store, m, term):
            store[m] = term if store[m] is None else store[m] + term

        for m in range(MEMBERS):
            for k in range(m + 1, MEMBERS):
                d = v[m] - v[k]
                square = d * d + EPS
                inverse = lax.rsqrt(square)
                s = square * inverse
                t = d * inverse
                add(value, m, s)
                add(value, k, s)
                add(slope, m, t)
                slope[k] = -t if slope[k] is None else slope[k] - t
        new = []
        for m in range(MEMBERS):
            gap = v[m] - truth
            square = gap * gap + EPS
            inverse = lax.rsqrt(square)
            grads[index, m] = area * (
                gap * inverse * (1.0 / MEMBERS)
                - slope[m] * (1.0 / (MEMBERS * (MEMBERS - 1)))
            )
            new.append(area * (square * inverse - value[m] * (1.0 / (2.0 * (MEMBERS - 1)))))
        return [a + b for a, b in zip(losses, new)]

    zero = [jnp.zeros((8, 128), F32) for _ in range(MEMBERS)]
    row = lax.broadcasted_iota(jnp.int32, (8, 128), 0)
    last = ROWS // 8 - 1
    for l in range(lane_tiles):
        losses = lax.fori_loop(
            0, ROWS // 8, lambda r, carry: spot(r * lane_tiles + l, carry), zero
        )
        for m in range(MEMBERS):
            loss = jnp.sum(losses[m], axis=0, keepdims=True)
            high = loss.astype(BF).astype(F32)
            low = loss - high
            at = last * lane_tiles + l
            kept = grads[at, m]
            grads[at, m] = jnp.where(
                row == HI - 8 * last, high, jnp.where(row == LO - 8 * last, low, kept)
            )
    for m in range(MEMBERS):
        out_ref[m] = jnp.concatenate(
            [
                jnp.concatenate([grads[r * lane_tiles + l, m] for l in range(lane_tiles)], 1)
                for r in range(ROWS // 8)
            ],
            0,
        ).astype(BF)


def pairs(fields, truth, area):
    spots = ROWS // 8 * (LANES // 128)
    return pl.pallas_call(
        pair_kernel,
        out_shape=shape((16, ROWS, LANES)),
        in_specs=[VM] * 3,
        out_specs=VM,
        scratch_shapes=[
            pltpu.VMEM((spots, MEMBERS, 8, 128), F32),
            pltpu.VMEM((spots, MEMBERS, 8, 128), F32),
        ],
        compiler_params=params(6),
        name="pairs",
    )(fields, truth, area)


def arrange(rows):
    out = []
    for x in range(4):
        for y in range(4):
            pick = [rows[x * 64 + zh * 32 + y * 8 : x * 64 + zh * 32 + y * 8 + 8] for zh in range(2)]
            out.append(jnp.concatenate(pick, 0))
    return out


def half_of_first(bp_ref, lat_ref, half, out_ref):
    lat = lat_ref[pl.ds(pl.multiple_of(half * (H // 2), H // 2), H // 2), :]
    for z in range(4):
        part = lax.dot_general(
            bp_ref[z * 256 : (z + 1) * 256, :], lat, NT, preferred_element_type=F32
        )
        for e, piece in enumerate(arrange(part)):
            out_ref[e, z * 16 : (z + 1) * 16, :] = piece.astype(out_ref.dtype)


def back_kernel(
    core_ref, blk_ref, der_ref, lat_ref, w2t_ref, hid_ref,
    bp_ref, send_ref, keep2_ref, send2_ref, low, second,
):
    half = H // 2
    for q in range(PTS // LANES):
        parts = [blk_ref[g * GROUPS + q].astype(F32) for g in range(GROUPS)]
        parts.append(jnp.zeros((128 - PAD, LANES), F32))
        low[:, q * LANES : (q + 1) * LANES] = jnp.concatenate(parts, 0).astype(BF)
    for n in range(PTS // WIDE):
        cols = slice(n * WIDE, (n + 1) * WIDE)
        back = jnp.dot(w2t_ref[...], low[:, cols], preferred_element_type=F32)
        bp_ref[:, cols] = (back * der_ref[:, cols].astype(F32)).astype(BF)
    half_of_first(bp_ref, lat_ref, 1 - core_ref[0], send_ref)

    second[...] = lax.dot_general(low[:PAD, :], hid_ref[...], NT, preferred_element_type=F32)
    row = lax.broadcasted_iota(jnp.int32, (8, LANES), 0)
    total = jnp.zeros((1, LANES), F32)
    for e in range(16):
        block = blk_ref[e].astype(F32)
        total += block[HI : HI + 1] + block[LO : LO + 1]
    high = total.astype(BF).astype(F32)
    top = ROWS - 8
    second[top:ROWS, :LANES] = jnp.where(
        row == HI - top,
        high,
        jnp.where(row == LO - top, total - high, second[top:ROWS, :LANES]),
    )
    keep2_ref[...] = second[:, pl.ds(pl.multiple_of(core_ref[0] * half, half), half)]
    send2_ref[...] = second[:, pl.ds(pl.multiple_of((1 - core_ref[0]) * half, half), half)].astype(BF)


def backward(core, blocks, deriv, latent, w2t, hidden):
    return pl.pallas_call(
        back_kernel,
        in_specs=[SCALAR, VM, VM, VM, VM, VM],
        out_specs=[VM] * 4,
        out_shape=[
            shape((H2, PTS)),
            shape((16, 64, H // 2)),
            shape((PAD, H2 // 2), F32),
            shape((PAD, H2 // 2)),
        ],
        scratch_shapes=[pltpu.VMEM((128, PTS), BF), pltpu.VMEM((PAD, H2), F32)],
        compiler_params=params(12),
        name="backward",
    )(core, blocks, deriv, latent, w2t, hidden)


def own_kernel(core_ref, bp_ref, lat_ref, blk_ref, out_ref, grad_ref):
    half_of_first(bp_ref, lat_ref, core_ref[0], out_ref)
    for q in range(PTS // LANES):
        cols = slice(q * LANES, (q + 1) * LANES)
        for g in range(GROUPS):
            used = min(USED, C - g * USED)
            part = blk_ref[g * GROUPS + q].astype(F32)
            grad_ref[g * USED : g * USED + used, :, cols] = part[:used].reshape(used, 1, LANES)


def own_half(core, bp, latent, blocks):
    return pl.pallas_call(
        own_kernel,
        in_specs=[SCALAR, VM, VM, VM],
        out_specs=[VM] * 2,
        out_shape=[shape((16, 64, H // 2), F32), shape((C, 1, PTS), F32)],
        compiler_params=params(12),
        cost_estimate=pl.CostEstimate(
            flops=2 * H2 * (H // 2) * PTS, bytes_accessed=8 * 1024 * 1024, transcendentals=0
        ),
        name="own_half",
    )(core, bp, latent, blocks)


def sum_kernel(scale, parts_ref, out_ref):
    total = parts_ref[0].astype(F32)
    for e in range(1, parts_ref.shape[0]):
        total += parts_ref[e].astype(F32)
    out_ref[...] = (total * scale).astype(out_ref.dtype)


def sum_parts(parts, scale, dtype, flops):
    return pl.pallas_call(
        functools.partial(sum_kernel, scale),
        in_specs=[VM],
        out_specs=VM,
        out_shape=shape(parts.shape[1:], dtype),
        compiler_params=params(6),
        cost_estimate=pl.CostEstimate(flops=flops, bytes_accessed=parts.size * 2, transcendentals=0),
        name="sum_parts",
    )(parts)


def finish_kernel(core_ref, mine_ref, other_ref, second_ref, loss_ref):
    first_core = core_ref[0] == 0
    mine, other = mine_ref[...].astype(F32), other_ref[...].astype(F32)
    left, right = jnp.where(first_core, mine, other), jnp.where(first_core, other, mine)
    loss = left[HI : HI + 1, :LANES] + left[LO : LO + 1, :LANES]
    loss_ref[...] = jnp.sum(loss, axis=1, keepdims=True) / NPTS
    scale = MEMBERS / math.sqrt(NPTS)
    for g in range(GROUPS):
        used = min(USED, C - g * USED)
        for cols, part in ((slice(0, H2 // 2), left), (slice(H2 // 2, H2), right)):
            rows = part[g * ROWS : g * ROWS + used] * scale
            second_ref[g * USED : g * USED + used, :, cols] = rows.reshape(used, 1, H2 // 2)


def finish(core, mine, other):
    return pl.pallas_call(
        finish_kernel,
        in_specs=[SCALAR, VM, VM],
        out_specs=[VM, VM],
        out_shape=[shape((C, 1, H2), F32), shape((1, 1), F32)],
        compiler_params=params(6),
        name="finish",
    )(core, mine, other)


def swap(value, axis, by):
    size = lax.axis_size(axis)
    return lax.ppermute(value, axis, [(i, i ^ by) for i in range(size)])


def turn(value, axis, by):
    size = lax.axis_size(axis)
    return lax.ppermute(value, axis, [(i, (i + by) % size) for i in range(size)])


def packed(total):
    row = lax.broadcasted_iota(jnp.int32, total.shape, 0)
    loss = total[HI : HI + 1] + total[LO : LO + 1]
    high = lax.reduce_precision(loss, 8, 7)
    return jnp.where(row == HI, high, jnp.where(row == LO, loss - high, total)).astype(BF)


def on_device(latent, truth, w_first, w_second):
    core = lax.axis_index("c").astype(jnp.int32)
    group, quarter = lax.axis_index("zl"), lax.axis_index("x")
    place = (lax.axis_index("zh") * 4 + lax.axis_index("y")) * 2 + lax.axis_index("c")
    where = jnp.stack([group, quarter, place]).astype(jnp.int32)
    latent, where, core = lax.optimization_barrier((latent, where, core[None]))

    hidden, deriv, kept_latent, blocks, w2t, truth_here, area = forward(
        where, latent, w_first, w_second, truth
    )

    gathered = lax.all_to_all(blocks, ("zl", "x"), 0, 0, tiled=True)
    grads = pairs(gathered, truth_here, area)
    grads = lax.all_to_all(grads, ("zl", "x"), 0, 0, tiled=True)

    bp, send, keep2, send2 = backward(core, grads, deriv, kept_latent, w2t, hidden)
    arrived, arrived2 = swap(send, "c", 1), swap(send2, "c", 1)
    own, field_grad = own_half(core, bp, kept_latent, grads)
    first = (own + arrived.astype(F32)).astype(BF)
    total = packed(keep2 + arrived2.astype(F32))
    first, total = lax.optimization_barrier((first, total))

    total = packed(total.astype(F32) + swap(total, "zh", 1).astype(F32))
    first = lax.all_to_all(first, ("x", "y"), 0, 0, tiled=True)
    first = sum_parts(first, 1.0, BF, FLOPS).reshape(8, 8, H // 2)
    first, total = lax.optimization_barrier((first, total))
    ring = [turn(total, "y", by).astype(F32) for by in (1, 2, 3)]
    total = packed((total.astype(F32) + ring[1]) + (ring[0] + ring[2]))
    other2 = swap(total, "c", 1)
    first = lax.all_to_all(first, ("zl", "zh"), 0, 0, tiled=True)
    first, total, other2 = lax.optimization_barrier((first, total, other2))
    first = sum_parts(first, 1.0 / math.sqrt(MEMBERS * NPTS), F32, FLOPS)
    upper, under = first[:4], first[4:]
    mine = jnp.where(core[0] == 0, upper, under)
    other = swap(jnp.where(core[0] == 0, under, upper), "c", 1)
    first_out = jnp.concatenate(
        [jnp.where(core[0] == 0, mine, other), jnp.where(core[0] == 0, other, mine)], 1
    )
    second_out, loss = finish(core, total, other2)
    return loss[0], field_grad.transpose(1, 0, 2), first_out, second_out.transpose(1, 0, 2)


def solution(mesh):
    fine = Mesh(mesh.devices.reshape(4, 4, 2, 4, 2), ("zl", "x", "zh", "y", "c"))
    ens, space = ("zl", "x"), ("zh", "y", "c")
    in_specs = (P(ens, None, space), P(None, space), P(), P())
    out_specs = (P(ens), P(ens, None, space), P(ens + space, None), P(ens, None, None))
    return jax.shard_map(
        on_device, mesh=fine, in_specs=in_specs, out_specs=out_specs, check_vma=False
    )
```

time: 121 us -> 97.8 us (0.81)
  blocking collectives: 0 us -> 32 us
  waiting for transfers between devices: 34.9 us -> 13.4 us
  Pallas kernels: 28.8 us -> 17.8 us
  other arithmetic: 11.1 us -> 2.49 us
  starting transfers between devices: 38.7 us -> 31.1 us
  local copies, waits for them, and re-layouts: 3.91 us -> 0 us
  between operations: 2.64 us -> 0.79 us
    all_to_all x0 -> x2, blocking collectives: none -> 32 us  [the longest x1 18.9 us: on_device(): gathered = lax.all_to_all(blocks, ('zl', 'x'), 0, 0, tiled=True)]
    all_to_all x2 -> x0, waiting for transfers between devices: 17.7 us -> none  [the longest x1 9.11 us: on_device(): grads = lax.all_to_all(grads, ('zl', 'x'), 0, 0, tiled=True)]
    all_to_all x2 -> x0, starting transfers between devices: 13.2 us -> none  [the longest x1 9.03 us: on_device(): gathered = lax.all_to_all(blocks, ('zl', 'x'), 0, 0, tiled=True)]
    pallas_call x4 -> x7, Pallas kernels: 28.8 us -> 17.8 us  [the longest x1 7.91 us: forward(): pl.pallas_call(forward_kernel, in_specs=[SCALAR, HBM, HBM, HBM, HBM], out...]
    ppermute x0 -> x3, starting transfers between devices: none -> 4.61 us  [turn(): lax.ppermute(value, axis, [(i, (i + by) % size) for i in range(size)])]
    unnamed x10 -> x0, local copies, waits for them, and re-layouts: 3.82 us -> none
    all_to_all x1, waiting for transfers between devices: 6.58 us -> 2.96 us  [on_device(): first = lax.all_to_all(first, ('zl', 'zh'), 0, 0, tiled=True)]
    ppermute x6 -> x5, waiting for transfers between devices: 6.9 us -> 3.28 us  [swap(): return lax.ppermute(value, axis, [(i, i ^ by) for i in range(size)])]
  transfers between devices with their start and end apart: 10 -> 10, of which waited for: 6 -> 3; matrix products, arithmetic and copies ran while one was open for 8% -> 0% of each run, Pallas kernels for 5% -> 4%
where the time goes in v2:
time: 97.8 us; the launch traced here: 97.5 us
  blocking collectives  32 us (33%)
  starting transfers between devices  31.1 us (32%)
  Pallas kernels  17.8 us (18%)
  waiting for transfers between devices  13.4 us (14%)
  other arithmetic  2.49 us (3%)
    all_to_all x1, blocking collectives, on_device(): gathered = lax.all_to_all(blocks, ('zl', 'x'), 0, 0, tiled=True)  18.9 us
    ppermute x5, starting transfers between devices, swap(): return lax.ppermute(value, axis, [(i, i ^ by) for i in range(size)])  15.8 us
    all_to_all x1, blocking collectives, on_device(): grads = lax.all_to_all(grads, ('zl', 'x'), 0, 0, tiled=True)  13.1 us
    pallas_call x1, Pallas kernels, forward(): pl.pallas_call(forward_kernel, in_specs=[SCALAR, HBM, HBM, HBM, HBM], out...  7.91 us
    all_to_all x1, waiting for transfers between devices, on_device(): first = lax.all_to_all(first, ('x', 'y'), 0, 0, tiled=True)  7.16 us
    all_to_all x1, starting transfers between devices, on_device(): first = lax.all_to_all(first, ('zl', 'zh'), 0, 0, tiled=True)  5.49 us
    all_to_all x1, starting transfers between devices, on_device(): first = lax.all_to_all(first, ('x', 'y'), 0, 0, tiled=True)  5.18 us
    ppermute x3, starting transfers between devices, turn(): lax.ppermute(value, axis, [(i, (i + by) % size) for i in range(size)])  4.61 us
  transfers between devices with their start and end apart: 10, of which 3 were waited for; matrix products, arithmetic and copies ran while one was open for 0% of the time, Pallas kernels for 4%

profile of v2, /device:TPU:1, one launch (start us, length us, event | category | flops | bytes accessed | tf_op | source)
XLA Modules:
  0.0 97.5 jit_solution(10127646721667557134)
XLA Ops:
  0.6 0.1 pad_add_fusion.where_ref
  0.7 7.9 %forward.1 = (bf16[1024,1536]{1,0:T(8,128)(2,1)S(1)}, bf16[1024,1536]{1,0:T(8,128)(2,1)S(1)}, bf16[1024,1536]{1,0:T(8,128)(2,1)S(1)}, bf16[16,24,384]{2,1,0:T(8,...) custom-call(s32[3]{0:T(128)S(1)} %pad_add_fusion.where_ref, ...), custom_call_target="tpu_custom_call" | custom-call | tf_op jit(solution)/shard_map/forward/pallas_call | solution.py:130
  8.6 18.9 %all_to_all.20.fields_ref = bf16[16,24,384]{2,1,0:T(8,128)(2,1)S(1)} all-to-all(bf16[16,24,384]{2,1,0:T(8,128)(2,1)S(1)} %get-tuple-element.32), channel_id=1, replica_groups=mesh['zl'=4,'x'=4,'zh'=2,'y'=4,'c'=2] {'zl','x'}, dimensions={0} | all-to-all | bytes 589824 | tf_op jit(solution)/shard_map/all_to_all | solution.py:405
  27.6 2.0 %pairs.1 = bf16[16,24,384]{2,1,0:T(8,128)(2,1)S(1)} custom-call(bf16[16,24,384]{2,1,0:T(8,128)(2,1)S(1)} %all_to_all.20.fields_ref, f32[9,8,128]{2,1,0:T(8,128)S(1)} %get-tuple-element.33.truth_ref, f32[9,8,128]{2,1,0:T(8,128)S(1)} %get-tuple-element.34.area_ref), custom_call_target="tpu_custom_call" | custom-call | tf_op jit(solution)/shard_map/pairs/pallas_call | solution.py:227
  29.6 13.1 %all_to_all.21.blk_ref = bf16[16,24,384]{2,1,0:T(8,128)(2,1)S(1)} all-to-all(bf16[16,24,384]{2,1,0:T(8,128)(2,1)S(1)} %pairs.1), channel_id=1, replica_groups=mesh['zl'=4,'x'=4,'zh'=2,'y'=4,'c'=2] {'zl','x'}, dimensions={0} | all-to-all | bytes 589824 | tf_op jit(solution)/shard_map/all_to_all | solution.py:407
  42.7 3.5 %backward.1 = (bf16[1024,1536]{1,0:T(8,128)(2,1)S(1)}, bf16[16,64,512]{2,1,0:T(8,128)(2,1)S(1)}, f32[96,512]{1,0:T(8,128)S(1)}, bf16[96,512]{1,0:T(8,128)(2,1)S(1)}) custom-call(s32[1]{0:T(128)} %bitcast.3.core_ref, bf16[16,24,384]{2,1,0:T(8,128)(2,1)S(1)} %all_to_all.21.blk_ref, bf16[1024,1536]{1,0:T(8,128)(2,1)S(1)} %get-tuple-element.35.der_ref, ...), custom_call_target="tpu_custom_call" | custom-call | tf_op jit(solution)/shard_map/backward/pallas_call | solution.py:293
  46.2 3.1 %collective-permute-start = (bf16[16,64,512]{2,1,0:T(8,128)(2,1)S(1)}, bf16[16,64,512]{2,1,0:T(8,128)(2,1)S(1)}, u32[]{:S(2)}, u32[]{:S(2)}) collective-permute-start(bf16[16,64,512]{2,1,0:T(8,128)(2,1)S(1)} %get-tuple-element.41), channel_id=1, source_target_pairs={{0,1},{1,0},{2,3},{3,2},{4,5},{5,4},{6,7},{7,6},{8,9},{9,8},{10,11... | collective-permute-start | bytes 3145736 | tf_op jit(solution)/shard_map/ppermute | solution.py:379
  49.3 0.1 collective-permute-start.1
  49.4 2.7 %own_half.1 = (f32[16,64,512]{2,1,0:T(8,128)S(1)}, f32[83,1,1536]{2,1,0:T(1,128)}) custom-call(s32[1]{0:T(128)} %bitcast.3.core_ref, bf16[1024,1536]{1,0:T(8,128)(2,1)S(1)} %get-tuple-element.39.bp_ref, bf16[1024,1536]{1,0:T(8,128)(2,1)S(1)} %get-tuple-element.36.lat_ref, bf16[16,24,384]{2,1,0:T(8,128)(2,1)S(1)} %all_to_all.21.blk_ref), custom_call_target="tpu_custom_call" | custom-call | flops 1610612736 | bytes 8388608 | tf_op jit(solution)/shard_map/own_half/pallas_call | solution.py:320
  52.1 0.0 collective-permute-done.1
  52.2 0.1 select_convert_fusion.2
  52.3 0.0 collective-permute-done
  52.3 1.4 %add_convert_fusion = bf16[16,64,512]{2,1,0:T(8,128)(2,1)} fusion(f32[16,64,512]{2,1,0:T(8,128)S(1)} %get-tuple-element.40, bf16[16,64,512]{2,1,0:T(8,128)(2,1)S(1)} %collective-permute-done), kind=kLoop, calls=%fused_computation | loop fusion | flops 1572864 | bytes 4194304 | tf_op jit(solution)/shard_map/convert_element_type | solution.py:412
  53.6 5.2 %all-to-all-start.2 = ((bf16[16,64,512]{2,1,0:T(8,128)(2,1)}), bf16[16,64,512]{2,1,0:T(8,128)(2,1)S(1)}, u32[]{:S(2)}, u32[]{:S(2)}) async-start(bf16[16,64,512]{2,1,0:T(8,128)(2,1)} %add_convert_fusion), calls=%async_computation.2 | async-start | bytes 2097152 | tf_op jit(solution)/shard_map/all_to_all | solution.py:417
  58.8 4.5 %collective-permute-start.2 = (bf16[96,512]{1,0:T(8,128)(2,1)S(1)}, bf16[96,512]{1,0:T(8,128)(2,1)S(1)}, u32[]{:S(2)}, u32[]{:S(2)}) collective-permute-start(bf16[96,512]{1,0:T(8,128)(2,1)S(1)} %select_convert_fusion.2), channel_id=1, source_target_pairs={{0,8},{8,0},{1,9},{9,1},{2,10},{10,2},{3,11},{11,3},{4,12},{12,4},... | collective-permute-start | bytes 294920 | tf_op jit(solution)/shard_map/ppermute | solution.py:379
  63.3 3.3 %collective-permute-done.2 = bf16[96,512]{1,0:T(8,128)(2,1)S(1)} collective-permute-done((bf16[96,512]{1,0:T(8,128)(2,1)S(1)}, bf16[96,512]{1,0:T(8,128)(2,1)S(1)}, u32[]{:S(2)}, u32[]{:S(2)}) %collective-permute-start.2) | collective-permute-done | bytes 98336 | tf_op jit(solution)/shard_map/ppermute | solution.py:379
  66.6 0.1 select_convert_fusion.1
  66.7 7.2 %all-to-all-done.2.parts_ref = bf16[16,64,512]{2,1,0:T(8,128)(2,1)S(1)} async-done(((bf16[16,64,512]{2,1,0:T(8,128)(2,1)}), bf16[16,64,512]{2,1,0:T(8,128)(2,1)S(1)}, u32[]{:S(2)}, u32[]{:S(2)}) %all-to-all-start.2) | async-done | bytes 1048608 | tf_op jit(solution)/shard_map/all_to_all | solution.py:417
  73.9 0.8 sum_parts.2
  74.7 1.9 %collective-permute-start.3 = (bf16[96,512]{1,0:T(8,128)(2,1)S(1)}, bf16[96,512]{1,0:T(8,128)(2,1)S(1)}, u32[]{:S(2)}, u32[]{:S(2)}) collective-permute-start(bf16[96,512]{1,0:T(8,128)(2,1)S(1)} %select_convert_fusion.1), channel_id=1, source_target_pairs={{0,4},{2,6},{4,0},{6,2},{1,5},{3,7},{5,1},{7,3},{8,12},{10,14},{12... | collective-permute-start | bytes 294920 | tf_op jit(solution)/shard_map/ppermute | solution.py:384
  76.6 0.4 collective-permute-start.4
  77.0 2.3 %collective-permute-start.5 = (bf16[96,512]{1,0:T(8,128)(2,1)S(1)}, bf16[96,512]{1,0:T(8,128)(2,1)S(1)}, u32[]{:S(2)}, u32[]{:S(2)}) collective-permute-start(bf16[96,512]{1,0:T(8,128)(2,1)S(1)} %select_convert_fusion.1), channel_id=1, source_target_pairs={{0,6},{2,0},{4,2},{6,4},{1,7},{3,1},{5,3},{7,5},{8,14},{10,8},{12,... | collective-permute-start | bytes 294920 | tf_op jit(solution)/shard_map/ppermute | solution.py:384
  79.3 5.5 %all-to-all-start.3 = ((bf16[8,8,512]{2,1,0:T(8,128)(2,1)}), bf16[8,8,512]{2,1,0:T(8,128)(2,1)S(1)}, u32[]{:S(2)}, u32[]{:S(2)}) async-start(bf16[8,8,512]{2,1,0:T(8,128)(2,1)} %bitcast.6), calls=%async_computation.3 | async-start | bytes 131072 | tf_op jit(solution)/shard_map/all_to_all | solution.py:423
  84.8 0.0 collective-permute-done.3
  84.8 0.0 collective-permute-done.5
  84.8 0.1 add_add_fusion
  84.9 0.1 select_convert_fusion.mine_ref
  85.0 3.5 %collective-permute-start.6 = (bf16[96,512]{1,0:T(8,128)(2,1)S(1)}, bf16[96,512]{1,0:T(8,128)(2,1)S(1)}, u32[]{:S(2)}, u32[]{:S(2)}) collective-permute-start(bf16[96,512]{1,0:T(8,128)(2,1)S(1)} %select_convert_fusion.mine_ref), channel_id=1, source_target_pairs={{0,1},{1,0},{2,3},{3,2},{4,5},{5,4},{6,7},{7,6},{8,9},{9,8},{10,11... | collective-permute-start | bytes 294920 | tf_op jit(solution)/shard_map/ppermute | solution.py:379
  88.4 3.0 %all-to-all-done.3.parts_ref = bf16[8,8,512]{2,1,0:T(8,128)(2,1)S(1)} async-done(((bf16[8,8,512]{2,1,0:T(8,128)(2,1)}), bf16[8,8,512]{2,1,0:T(8,128)(2,1)S(1)}, u32[]{:S(2)}, u32[]{:S(2)}) %all-to-all-start.3) | async-done | bytes 65568 | tf_op jit(solution)/shard_map/all_to_all | solution.py:423
  91.4 4.6 %collective-permute-start.7 = (f32[4,512]{1,0:T(4,128)S(1)}, f32[4,512]{1,0:T(4,128)S(1)}, u32[]{:S(2)}, u32[]{:S(2)}) collective-permute-start(f32[4,512]{1,0:T(4,128)S(1)} %slice_select_fusion), channel_id=1, source_target_pairs={{0,1},{1,0},{2,3},{3,2},{4,5},{5,4},{6,7},{7,6},{8,9},{9,8},{10,11... | collective-permute-start | bytes 24584 | tf_op jit(solution)/shard_map/ppermute | solution.py:379
  96.0 0.9 finish.1
  96.9 0.6 pad_maximum_fusion
  (12 shorter events, 0.1 us)
Async XLA Ops:
  46.2 6.1 %collective-permute-start = (bf16[16,64,512]{2,1,0:T(8,128)(2,1)S(1)}, bf16[16,64,512]{2,1,0:T(8,128)(2,1)S(1)}, u32[]{:S(2)}, u32[]{:S(2)}) collective-permute-start(bf16[16,64,512]{2,1,0:T(8,128)(2,1)S(1)} %get-tuple-element.41), channel_id=1, source_target_pairs={{0,1},{1,0},{2,3},{3,2},{4,5},{5,4},{6,7},{7,6},{8,9},{9,8},{10,11... | collective-permute-start | bytes 3145736 | tf_op jit(solution)/shard_map/ppermute | solution.py:379
  49.3 2.8 %collective-permute-start.1 = (bf16[96,512]{1,0:T(8,128)(2,1)S(1)}, bf16[96,512]{1,0:T(8,128)(2,1)S(1)}, u32[]{:S(2)}, u32[]{:S(2)}) collective-permute-start(bf16[96,512]{1,0:T(8,128)(2,1)S(1)} %get-tuple-element.43), channel_id=1, source_target_pairs={{0,1},{1,0},{2,3},{3,2},{4,5},{5,4},{6,7},{7,6},{8,9},{9,8},{10,11... | collective-permute-start | bytes 294920 | tf_op jit(solution)/shard_map/ppermute | solution.py:379
  53.6 20.2 %all-to-all-start.2 = ((bf16[16,64,512]{2,1,0:T(8,128)(2,1)}), bf16[16,64,512]{2,1,0:T(8,128)(2,1)S(1)}, u32[]{:S(2)}, u32[]{:S(2)}) async-start(bf16[16,64,512]{2,1,0:T(8,128)(2,1)} %add_convert_fusion), calls=%async_computation.2 | async-start | bytes 2097152 | tf_op jit(solution)/shard_map/all_to_all | solution.py:417
  58.8 7.7 %collective-permute-start.2 = (bf16[96,512]{1,0:T(8,128)(2,1)S(1)}, bf16[96,512]{1,0:T(8,128)(2,1)S(1)}, u32[]{:S(2)}, u32[]{:S(2)}) collective-permute-start(bf16[96,512]{1,0:T(8,128)(2,1)S(1)} %select_convert_fusion.2), channel_id=1, source_target_pairs={{0,8},{8,0},{1,9},{9,1},{2,10},{10,2},{3,11},{11,3},{4,12},{12,4},... | collective-permute-start | bytes 294920 | tf_op jit(solution)/shard_map/ppermute | solution.py:379
  74.7 10.1 %collective-permute-start.3 = (bf16[96,512]{1,0:T(8,128)(2,1)S(1)}, bf16[96,512]{1,0:T(8,128)(2,1)S(1)}, u32[]{:S(2)}, u32[]{:S(2)}) collective-permute-start(bf16[96,512]{1,0:T(8,128)(2,1)S(1)} %select_convert_fusion.1), channel_id=1, source_target_pairs={{0,4},{2,6},{4,0},{6,2},{1,5},{3,7},{5,1},{7,3},{8,12},{10,14},{12... | collective-permute-start | bytes 294920 | tf_op jit(solution)/shard_map/ppermute | solution.py:384
  76.6 8.2 %collective-permute-start.4 = (bf16[96,512]{1,0:T(8,128)(2,1)S(1)}, bf16[96,512]{1,0:T(8,128)(2,1)S(1)}, u32[]{:S(2)}, u32[]{:S(2)}) collective-permute-start(bf16[96,512]{1,0:T(8,128)(2,1)S(1)} %select_convert_fusion.1), channel_id=1, source_target_pairs={{0,2},{2,4},{4,6},{6,0},{1,3},{3,5},{5,7},{7,1},{8,10},{10,12},{12... | collective-permute-start | bytes 294920 | tf_op jit(solution)/shard_map/ppermute | solution.py:384
  77.0 7.8 %collective-permute-start.5 = (bf16[96,512]{1,0:T(8,128)(2,1)S(1)}, bf16[96,512]{1,0:T(8,128)(2,1)S(1)}, u32[]{:S(2)}, u32[]{:S(2)}) collective-permute-start(bf16[96,512]{1,0:T(8,128)(2,1)S(1)} %select_convert_fusion.1), channel_id=1, source_target_pairs={{0,6},{2,0},{4,2},{6,4},{1,7},{3,1},{5,3},{7,5},{8,14},{10,8},{12,... | collective-permute-start | bytes 294920 | tf_op jit(solution)/shard_map/ppermute | solution.py:384
  79.3 12.1 %all-to-all-start.3 = ((bf16[8,8,512]{2,1,0:T(8,128)(2,1)}), bf16[8,8,512]{2,1,0:T(8,128)(2,1)S(1)}, u32[]{:S(2)}, u32[]{:S(2)}) async-start(bf16[8,8,512]{2,1,0:T(8,128)(2,1)} %bitcast.6), calls=%async_computation.3 | async-start | bytes 131072 | tf_op jit(solution)/shard_map/all_to_all | solution.py:423
  85.0 6.4 %collective-permute-start.6 = (bf16[96,512]{1,0:T(8,128)(2,1)S(1)}, bf16[96,512]{1,0:T(8,128)(2,1)S(1)}, u32[]{:S(2)}, u32[]{:S(2)}) collective-permute-start(bf16[96,512]{1,0:T(8,128)(2,1)S(1)} %select_convert_fusion.mine_ref), channel_id=1, source_target_pairs={{0,1},{1,0},{2,3},{3,2},{4,5},{5,4},{6,7},{7,6},{8,9},{9,8},{10,11... | collective-permute-start | bytes 294920 | tf_op jit(solution)/shard_map/ppermute | solution.py:379
  91.4 5.5 %collective-permute-start.7 = (f32[4,512]{1,0:T(4,128)S(1)}, f32[4,512]{1,0:T(4,128)S(1)}, u32[]{:S(2)}, u32[]{:S(2)}) collective-permute-start(f32[4,512]{1,0:T(4,128)S(1)} %slice_select_fusion), channel_id=1, source_target_pairs={{0,1},{1,0},{2,3},{3,2},{4,5},{5,4},{6,7},{7,6},{8,9},{9,8},{10,11... | collective-permute-start | bytes 24584 | tf_op jit(solution)/shard_map/ppermute | solution.py:379

commit v3 on v2

--- a/solution.py
+++ b/solution.py
@@ -94,29 +94,41 @@
         parts += [w2[g * USED : (g + 1) * USED], gap]
     padded = jnp.concatenate(parts, 0)
     w2p[...] = padded.astype(BF)
-    w2t_ref[...] = jnp.concatenate([padded, jnp.zeros((128 - PAD, H2), F32)], 0).T.astype(BF)
+    w2t_ref[...] = (0.5 * jnp.concatenate([padded, jnp.zeros((128 - PAD, H2), F32)], 0)).T.astype(BF)
 
     def decode(n):
         cols = slice(n * WIDE, (n + 1) * WIDE)
         field[:, cols] = jnp.dot(w2p[...], hid_ref[:, cols], preferred_element_type=F32)
 
+    def gate(pre, here, cols):
+        half = 0.5 * pre
+        t = jnp.tanh(half)
+        twice = 1.0 + t
+        act = half * twice
+        hid_ref[here, cols] = act.astype(BF)
+        der_ref[here, cols] = (twice + act * (1.0 - t)).astype(BF)
+
+    held = None
     for n in range(spans):
-        lat_in[n].wait()
+        if n == 0:
+            lat_in[0].wait()
         if n == 1:
             truth_in.wait()
+            for copy in lat_in[1:]:
+                copy.wait()
             own_tiles(where_ref, all_truth, truth_ref, area_ref)
         cols = slice(n * WIDE, (n + 1) * WIDE)
-        for r in range(halves):
-            if n == 0:
-                w1_in[r].wait()
-            here = slice(r * rows, (r + 1) * rows)
+        for r in range(0, H2, 128):
+            if n == 0 and r % rows == 0:
+                w1_in[r // rows].wait()
+            here = slice(r, r + 128)
             pre = jnp.dot(w1[here, :], lat_ref[:, cols], preferred_element_type=F32)
-            sig = 0.5 * jnp.tanh(0.5 * pre) + 0.5
-            act = pre * sig
-            hid_ref[here, cols] = act.astype(BF)
-            der_ref[here, cols] = (sig + act * (1.0 - sig)).astype(BF)
+            if held is not None:
+                gate(*held)
+            held = (pre, here, cols)
         if n > 0:
             decode(n - 1)
+    gate(*held)
     decode(spans - 1)
     for g in range(GROUPS):
         for q in range(PTS // LANES):
@@ -257,27 +269,76 @@
             out_ref[e, z * 16 : (z + 1) * 16, :] = piece.astype(out_ref.dtype)
 
 
-def back_kernel(
-    core_ref, blk_ref, der_ref, lat_ref, w2t_ref, hid_ref,
-    bp_ref, send_ref, keep2_ref, send2_ref, low, second,
-):
-    half = H // 2
+def back_kernel(core_ref, blk_ref, der_ref, lat_ref, w2t_ref, bp_ref, send_ref, low_ref):
     for q in range(PTS // LANES):
         parts = [blk_ref[g * GROUPS + q].astype(F32) for g in range(GROUPS)]
         parts.append(jnp.zeros((128 - PAD, LANES), F32))
-        low[:, q * LANES : (q + 1) * LANES] = jnp.concatenate(parts, 0).astype(BF)
+        low_ref[:, q * LANES : (q + 1) * LANES] = jnp.concatenate(parts, 0).astype(BF)
     for n in range(PTS // WIDE):
         cols = slice(n * WIDE, (n + 1) * WIDE)
-        back = jnp.dot(w2t_ref[...], low[:, cols], preferred_element_type=F32)
+        back = jnp.dot(w2t_ref[...], low_ref[:, cols], preferred_element_type=F32)
         bp_ref[:, cols] = (back * der_ref[:, cols].astype(F32)).astype(BF)
     half_of_first(bp_ref, lat_ref, 1 - core_ref[0], send_ref)
 
-    second[...] = lax.dot_general(low[:PAD, :], hid_ref[...], NT, preferred_element_type=F32)
+
+def backward(core, blocks, deriv, latent, w2t):
+    return pl.pallas_call(
+        back_kernel,
+        in_specs=[SCALAR, VM, VM, VM, VM],
+        out_specs=[VM] * 3,
+        out_shape=[shape((H2, PTS)), shape((16, 64, H // 2)), shape((128, PTS))],
+        compiler_params=params(12),
+        name="backward",
+    )(core, blocks, deriv, latent, w2t)
+
+
+def own_kernel(core_ref, bp_ref, lat_ref, out_ref):
+    half_of_first(bp_ref, lat_ref, core_ref[0], out_ref)
+
+
+def own_half(core, bp, latent):
+    return pl.pallas_call(
+        own_kernel,
+        in_specs=[SCALAR, VM, VM],
+        out_specs=VM,
+        out_shape=shape((16, 64, H // 2), F32),
+        compiler_params=params(12),
+        cost_estimate=pl.CostEstimate(
+            flops=2 * H2 * (H // 2) * PTS, bytes_accessed=8 * 1024 * 1024, transcendentals=0
+        ),
+        name="own_half",
+    )(core, bp, latent)
+
+
+def emit_kernel(low_ref, grad_ref):
+    for g in range(GROUPS):
+        used = min(USED, C - g * USED)
+        part = low_ref[g * ROWS : (g + 1) * ROWS, :].astype(F32)
+        grad_ref[g * USED : g * USED + used] = part[:used].reshape(used, 1, PTS)
+
+
+def emit(low):
+    return pl.pallas_call(
+        emit_kernel,
+        in_specs=[VM],
+        out_specs=VM,
+        out_shape=shape((C, 1, PTS), F32),
+        compiler_params=params(6),
+        cost_estimate=pl.CostEstimate(flops=0, bytes_accessed=PTS, transcendentals=0),
+        name="emit",
+    )(low)
+
+
+def second_kernel(core_ref, low_ref, hid_ref, keep_ref, send_ref, second):
+    half = H2 // 2
+    second[...] = lax.dot_general(low_ref[...], hid_ref[...], NT, preferred_element_type=F32)[:PAD]
     row = lax.broadcasted_iota(jnp.int32, (8, LANES), 0)
     total = jnp.zeros((1, LANES), F32)
-    for e in range(16):
-        block = blk_ref[e].astype(F32)
-        total += block[HI : HI + 1] + block[LO : LO + 1]
+    for g in range(GROUPS):
+        block = low_ref[g * ROWS : (g + 1) * ROWS, :].astype(F32)
+        for q in range(PTS // LANES):
+            cols = slice(q * LANES, (q + 1) * LANES)
+            total += block[HI : HI + 1, cols] + block[LO : LO + 1, cols]
     high = total.astype(BF).astype(F32)
     top = ROWS - 8
     second[top:ROWS, :LANES] = jnp.where(
@@ -285,49 +346,20 @@
         high,
         jnp.where(row == LO - top, total - high, second[top:ROWS, :LANES]),
     )
-    keep2_ref[...] = second[:, pl.ds(pl.multiple_of(core_ref[0] * half, half), half)]
-    send2_ref[...] = second[:, pl.ds(pl.multiple_of((1 - core_ref[0]) * half, half), half)].astype(BF)
-
-
-def backward(core, blocks, deriv, latent, w2t, hidden):
-    return pl.pallas_call(
-        back_kernel,
-        in_specs=[SCALAR, VM, VM, VM, VM, VM],
-        out_specs=[VM] * 4,
-        out_shape=[
-            shape((H2, PTS)),
-            shape((16, 64, H // 2)),
-            shape((PAD, H2 // 2), F32),
-            shape((PAD, H2 // 2)),
-        ],
-        scratch_shapes=[pltpu.VMEM((128, PTS), BF), pltpu.VMEM((PAD, H2), F32)],
+    keep_ref[...] = second[:, pl.ds(pl.multiple_of(core_ref[0] * half, half), half)]
+    send_ref[...] = second[:, pl.ds(pl.multiple_of((1 - core_ref[0]) * half, half), half)].astype(BF)
+
+
+def second_halves(core, low, hidden):
+    return pl.pallas_call(
+        second_kernel,
+        in_specs=[SCALAR, VM, VM],
+        out_specs=[VM] * 2,
+        out_shape=[shape((PAD, H2 // 2), F32), shape((PAD, H2 // 2))],
+        scratch_shapes=[pltpu.VMEM((PAD, H2), F32)],
         compiler_params=params(12),
-        name="backward",
-    )(core, blocks, deriv, latent, w2t, hidden)
-
-
-def own_kernel(core_ref, bp_ref, lat_ref, blk_ref, out_ref, grad_ref):
-    half_of_first(bp_ref, lat_ref, core_ref[0], out_ref)
-    for q in range(PTS // LANES):
-        cols = slice(q * LANES, (q + 1) * LANES)
-        for g in range(GROUPS):
-            used = min(USED, C - g * USED)
-            part = blk_ref[g * GROUPS + q].astype(F32)
-            grad_ref[g * USED : g * USED + used, :, cols] = part[:used].reshape(used, 1, LANES)
-
-
-def own_half(core, bp, latent, blocks):
-    return pl.pallas_call(
-        own_kernel,
-        in_specs=[SCALAR, VM, VM, VM],
-        out_specs=[VM] * 2,
-        out_shape=[shape((16, 64, H // 2), F32), shape((C, 1, PTS), F32)],
-        compiler_params=params(12),
-        cost_estimate=pl.CostEstimate(
-            flops=2 * H2 * (H // 2) * PTS, bytes_accessed=8 * 1024 * 1024, transcendentals=0
-        ),
-        name="own_half",
-    )(core, bp, latent, blocks)
+        name="second",
+    )(core, low, hidden)
 
 
 def sum_kernel(scale, parts_ref, out_ref):
@@ -349,8 +381,35 @@
     )(parts)
 
 
-def finish_kernel(core_ref, mine_ref, other_ref, second_ref, loss_ref):
+def halves_kernel(core_ref, parts_ref, keep_ref, give_ref):
+    total = parts_ref[0].astype(F32)
+    for e in range(1, parts_ref.shape[0]):
+        total += parts_ref[e].astype(F32)
+    total *= 1.0 / math.sqrt(MEMBERS * NPTS)
+    upper, under = total[:4], total[4:]
     first_core = core_ref[0] == 0
+    keep_ref[...] = jnp.where(first_core, upper, under)
+    give_ref[...] = jnp.where(first_core, under, upper)
+
+
+def sum_halves(core, parts):
+    return pl.pallas_call(
+        halves_kernel,
+        in_specs=[SCALAR, VM],
+        out_specs=[VM, VM],
+        out_shape=[shape((4, H // 2), F32)] * 2,
+        compiler_params=params(6),
+        cost_estimate=pl.CostEstimate(flops=FLOPS, bytes_accessed=parts.size * 2, transcendentals=0),
+        name="sum_halves",
+    )(core, parts)
+
+
+def finish_kernel(core_ref, keep_ref, got_ref, mine_ref, other_ref, first_ref, second_ref, loss_ref):
+    half = H // 2
+    first_core = core_ref[0] == 0
+    keep, got = keep_ref[...], got_ref[...]
+    first_ref[:, :half] = jnp.where(first_core, keep, got)
+    first_ref[:, half:] = jnp.where(first_core, got, keep)
     mine, other = mine_ref[...].astype(F32), other_ref[...].astype(F32)
     left, right = jnp.where(first_core, mine, other), jnp.where(first_core, other, mine)
     loss = left[HI : HI + 1, :LANES] + left[LO : LO + 1, :LANES]
@@ -358,20 +417,20 @@
     scale = MEMBERS / math.sqrt(NPTS)
     for g in range(GROUPS):
         used = min(USED, C - g * USED)
-        for cols, part in ((slice(0, H2 // 2), left), (slice(H2 // 2, H2), right)):
+        for cols, part in ((slice(0, half), left), (slice(half, H2), right)):
             rows = part[g * ROWS : g * ROWS + used] * scale
-            second_ref[g * USED : g * USED + used, :, cols] = rows.reshape(used, 1, H2 // 2)
-
-
-def finish(core, mine, other):
+            second_ref[g * USED : g * USED + used, :, cols] = rows.reshape(used, 1, half)
+
+
+def finish(core, keep, got, mine, other):
     return pl.pallas_call(
         finish_kernel,
-        in_specs=[SCALAR, VM, VM],
-        out_specs=[VM, VM],
-        out_shape=[shape((C, 1, H2), F32), shape((1, 1), F32)],
+        in_specs=[SCALAR, VM, VM, VM, VM],
+        out_specs=[VM] * 3,
+        out_shape=[shape((4, H), F32), shape((C, 1, H2), F32), shape((1, 1), F32)],
         compiler_params=params(6),
         name="finish",
-    )(core, mine, other)
+    )(core, keep, got, mine, other)
 
 
 def swap(value, axis, by):
@@ -379,9 +438,9 @@
     return lax.ppermute(value, axis, [(i, i ^ by) for i in range(size)])
 
 
-def turn(value, axis, by):
-    size = lax.axis_size(axis)
-    return lax.ppermute(value, axis, [(i, (i + by) % size) for i in range(size)])
+def cross(value, h, y):
+    pairs = [(zh * 4 + k, (zh ^ h) * 4 + (k ^ y)) for zh in range(2) for k in range(4)]
+    return lax.ppermute(value, ("zh", "y"), pairs)
 
 
 def packed(total):
@@ -406,30 +465,30 @@
     grads = pairs(gathered, truth_here, area)
     grads = lax.all_to_all(grads, ("zl", "x"), 0, 0, tiled=True)
 
-    bp, send, keep2, send2 = backward(core, grads, deriv, kept_latent, w2t, hidden)
-    arrived, arrived2 = swap(send, "c", 1), swap(send2, "c", 1)
-    own, field_grad = own_half(core, bp, kept_latent, grads)
+    bp, send, low = backward(core, grads, deriv, kept_latent, w2t)
+    arrived = swap(send, "c", 1)
+    keep2, send2 = second_halves(core, low, hidden)
+    arrived2 = swap(send2, "c", 1)
+    own = own_half(core, bp, kept_latent)
     first = (own + arrived.astype(F32)).astype(BF)
     total = packed(keep2 + arrived2.astype(F32))
-    first, total = lax.optimization_barrier((first, total))
-
-    total = packed(total.astype(F32) + swap(total, "zh", 1).astype(F32))
+    first, total, low = lax.optimization_barrier((first, total, low))
+
+    field_grad = emit(low)
+    near, far, both = (cross(total, h, y).astype(F32) for h, y in ((0, 1), (1, 0), (1, 1)))
+    total = packed((total.astype(F32) + both) + (near + far))
     first = lax.all_to_all(first, ("x", "y"), 0, 0, tiled=True)
     first = sum_parts(first, 1.0, BF, FLOPS).reshape(8, 8, H // 2)
+    first, total, field_grad = lax.optimization_barrier((first, total, field_grad))
+
+    total = packed(total.astype(F32) + swap(total, "y", 2).astype(F32))
+    first = lax.all_to_all(first, ("zl", "zh"), 0, 0, tiled=True)
     first, total = lax.optimization_barrier((first, total))
-    ring = [turn(total, "y", by).astype(F32) for by in (1, 2, 3)]
-    total = packed((total.astype(F32) + ring[1]) + (ring[0] + ring[2]))
-    other2 = swap(total, "c", 1)
-    first = lax.all_to_all(first, ("zl", "zh"), 0, 0, tiled=True)
-    first, total, other2 = lax.optimization_barrier((first, total, other2))
-    first = sum_parts(first, 1.0 / math.sqrt(MEMBERS * NPTS), F32, FLOPS)
-    upper, under = first[:4], first[4:]
-    mine = jnp.where(core[0] == 0, upper, under)
-    other = swap(jnp.where(core[0] == 0, under, upper), "c", 1)
-    first_out = jnp.concatenate(
-        [jnp.where(core[0] == 0, mine, other), jnp.where(core[0] == 0, other, mine)], 1
-    )
-    second_out, loss = finish(core, total, other2)
+
+    other = swap(total, "c", 1)
+    keep, give = sum_halves(core, first)
+    got = swap(give, "c", 1)
+    first_out, second_out, loss = finish(core, keep, got, total, other)
     return loss[0], field_grad.transpose(1, 0, 2), first_out, second_out.transpose(1, 0, 2)
 
 

time: 97.8 us -> 96 us (0.982)
  starting transfers between devices: 31.1 us -> 24.8 us
  waiting for transfers between devices: 13.4 us -> 18.6 us
    ppermute x3, waiting for transfers between devices: 0.01 us -> 11 us  [cross(): return lax.ppermute(value, ('zh', 'y'), pairs)]
    all_to_all x1, waiting for transfers between devices: 7.16 us -> 0.01 us  [on_device(): first = lax.all_to_all(first, ('x', 'y'), 0, 0, tiled=True)]
    ppermute x5, starting transfers between devices: 15.8 us -> 8.71 us  [swap(): return lax.ppermute(value, axis, [(i, i ^ by) for i in range(size)])]
    all_to_all x1, waiting for transfers between devices: 2.96 us -> 6.46 us  [on_device(): first = lax.all_to_all(first, ('zl', 'zh'), 0, 0, tiled=True)]
    ppermute x3, starting transfers between devices: 4.61 us -> 6.82 us  [cross(): return lax.ppermute(value, ('zh', 'y'), pairs)]
    ppermute x5, waiting for transfers between devices: 3.28 us -> 1.17 us  [swap(): return lax.ppermute(value, axis, [(i, i ^ by) for i in range(size)])]
    all_to_all x1, starting transfers between devices: 5.49 us -> 4.1 us  [on_device(): first = lax.all_to_all(first, ('zl', 'zh'), 0, 0, tiled=True)]
    pallas_call x3 -> x6, Pallas kernels: 7.05 us -> 7.35 us  [the longest x1 2.6 us: backward(): pl.pallas_call(back_kernel, in_specs=[SCALAR, VM, VM, VM, VM], out_specs=...]
  transfers between devices with their start and end apart: 10 -> 10, of which waited for: 3 -> 4; matrix products, arithmetic and copies ran while one was open for 0% -> 0% of each run, Pallas kernels for 4% -> 4%
where the time goes in v3:
time: 96 us; the launch traced here: 95.7 us
  blocking collectives  32 us (33%)
  starting transfers between devices  24.8 us (26%)
  waiting for transfers between devices  18.6 us (19%)
  Pallas kernels  17.5 us (18%)
  other arithmetic  1.87 us (2%)
    all_to_all x1, blocking collectives, on_device(): gathered = lax.all_to_all(blocks, ('zl', 'x'), 0, 0, tiled=True)  18.9 us
    all_to_all x1, blocking collectives, on_device(): grads = lax.all_to_all(grads, ('zl', 'x'), 0, 0, tiled=True)  13.1 us
    ppermute x3, waiting for transfers between devices, cross(): return lax.ppermute(value, ('zh', 'y'), pairs)  11 us
    ppermute x5, starting transfers between devices, swap(): return lax.ppermute(value, axis, [(i, i ^ by) for i in range(size)])  8.71 us
    pallas_call x1, Pallas kernels, forward(): pl.pallas_call(forward_kernel, in_specs=[SCALAR, HBM, HBM, HBM, HBM], out...  7.4 us
    ppermute x3, starting transfers between devices, cross(): return lax.ppermute(value, ('zh', 'y'), pairs)  6.82 us
    all_to_all x1, waiting for transfers between devices, on_device(): first = lax.all_to_all(first, ('zl', 'zh'), 0, 0, tiled=True)  6.46 us
    all_to_all x1, starting transfers between devices, on_device(): first = lax.all_to_all(first, ('x', 'y'), 0, 0, tiled=True)  5.17 us
  transfers between devices with their start and end apart: 10, of which 4 were waited for; matrix products, arithmetic and copies ran while one was open for 0% of the time, Pallas kernels for 4%

profile of v3, /device:TPU:1, one launch (start us, length us, event | category | flops | bytes accessed | tf_op | source)
XLA Modules:
  0.0 95.7 jit_solution(11752275521441369799)
XLA Ops:
  0.6 0.1 pad_add_fusion.where_ref
  0.7 7.4 %forward.1 = (bf16[1024,1536]{1,0:T(8,128)(2,1)S(1)}, bf16[1024,1536]{1,0:T(8,128)(2,1)S(1)}, bf16[1024,1536]{1,0:T(8,128)(2,1)S(1)}, bf16[16,24,384]{2,1,0:T(8,...) custom-call(s32[3]{0:T(128)S(1)} %pad_add_fusion.where_ref, ...), custom_call_target="tpu_custom_call" | custom-call | tf_op jit(solution)/shard_map/forward/pallas_call | solution.py:142
  8.1 18.9 %all_to_all.20.fields_ref = bf16[16,24,384]{2,1,0:T(8,128)(2,1)S(1)} all-to-all(bf16[16,24,384]{2,1,0:T(8,128)(2,1)S(1)} %get-tuple-element.35), channel_id=1, replica_groups=mesh['zl'=4,'x'=4,'zh'=2,'y'=4,'c'=2] {'zl','x'}, dimensions={0} | all-to-all | bytes 589824 | tf_op jit(solution)/shard_map/all_to_all | solution.py:464
  27.1 2.0 %pairs.1 = bf16[16,24,384]{2,1,0:T(8,128)(2,1)S(1)} custom-call(bf16[16,24,384]{2,1,0:T(8,128)(2,1)S(1)} %all_to_all.20.fields_ref, f32[9,8,128]{2,1,0:T(8,128)S(1)} %get-tuple-element.36.truth_ref, f32[9,8,128]{2,1,0:T(8,128)S(1)} %get-tuple-element.37.area_ref), custom_call_target="tpu_custom_call" | custom-call | tf_op jit(solution)/shard_map/pairs/pallas_call | solution.py:239
  29.1 13.1 %all_to_all.21.blk_ref = bf16[16,24,384]{2,1,0:T(8,128)(2,1)S(1)} all-to-all(bf16[16,24,384]{2,1,0:T(8,128)(2,1)S(1)} %pairs.1), channel_id=1, replica_groups=mesh['zl'=4,'x'=4,'zh'=2,'y'=4,'c'=2] {'zl','x'}, dimensions={0} | all-to-all | bytes 589824 | tf_op jit(solution)/shard_map/all_to_all | solution.py:466
  42.2 2.6 %backward.1 = (bf16[1024,1536]{1,0:T(8,128)(2,1)S(1)}, bf16[16,64,512]{2,1,0:T(8,128)(2,1)S(1)}, bf16[128,1536]{1,0:T(8,128)(2,1)S(1)}) custom-call(s32[1]{0:T(128)} %bitcast.3.core_ref, bf16[16,24,384]{2,1,0:T(8,128)(2,1)S(1)} %all_to_all.21.blk_ref, bf16[1024,1536]{1,0:T(8,128)(2,1)S(1)} %get-tuple-element.38.der_ref, ...), custom_call_target="tpu_custom_call" | custom-call | tf_op jit(solution)/shard_map/backward/pallas_call | solution.py:285
  44.8 3.1 %collective-permute-start = (bf16[16,64,512]{2,1,0:T(8,128)(2,1)S(1)}, bf16[16,64,512]{2,1,0:T(8,128)(2,1)S(1)}, u32[]{:S(2)}, u32[]{:S(2)}) collective-permute-start(bf16[16,64,512]{2,1,0:T(8,128)(2,1)S(1)} %get-tuple-element.42), channel_id=1, source_target_pairs={{0,1},{1,0},{2,3},{3,2},{4,5},{5,4},{6,7},{7,6},{8,9},{9,8},{10,11... | collective-permute-start | bytes 3145736 | tf_op jit(solution)/shard_map/ppermute | solution.py:438
  47.9 1.2 %second.1 = (f32[96,512]{1,0:T(8,128)S(1)}, bf16[96,512]{1,0:T(8,128)(2,1)S(1)}) custom-call(s32[1]{0:T(128)} %bitcast.3.core_ref, bf16[128,1536]{1,0:T(8,128)(2,1)S(1)} %get-tuple-element.49.low_ref, bf16[1024,1536]{1,0:T(8,128)(2,1)S(1)} %get-tuple-element.44.hid_ref), custom_call_target="tpu_custom_call" | custom-call | tf_op jit(solution)/shard_map/second/pallas_call | solution.py:354
  49.1 0.1 collective-permute-start.1
  49.2 1.8 %own_half.1 = f32[16,64,512]{2,1,0:T(8,128)S(1)} custom-call(s32[1]{0:T(128)} %bitcast.3.core_ref, bf16[1024,1536]{1,0:T(8,128)(2,1)S(1)} %get-tuple-element.41.bp_ref, bf16[1024,1536]{1,0:T(8,128)(2,1)S(1)} %get-tuple-element.39.lat_ref), custom_call_target="tpu_custom_call" | custom-call | flops 1610612736 | bytes 8388608 | tf_op jit(solution)/shard_map/own_half/pallas_call | solution.py:300
  51.0 0.0 collective-permute-done.1
  51.1 0.1 select_convert_fusion.2
  51.2 0.0 collective-permute-done
  51.2 1.4 %add_convert_fusion = bf16[16,64,512]{2,1,0:T(8,128)(2,1)} fusion(f32[16,64,512]{2,1,0:T(8,128)S(1)} %own_half.1, bf16[16,64,512]{2,1,0:T(8,128)(2,1)S(1)} %collective-permute-done), kind=kLoop, calls=%fused_computation | loop fusion | flops 1572864 | bytes 4194304 | tf_op jit(solution)/shard_map/convert_element_type | solution.py:473
  52.6 5.2 %all-to-all-start.2 = ((bf16[16,64,512]{2,1,0:T(8,128)(2,1)}), bf16[16,64,512]{2,1,0:T(8,128)(2,1)S(1)}, u32[]{:S(2)}, u32[]{:S(2)}) async-start(bf16[16,64,512]{2,1,0:T(8,128)(2,1)} %add_convert_fusion), calls=%async_computation.2 | async-start | bytes 2097152 | tf_op jit(solution)/shard_map/all_to_all | solution.py:480
  57.8 5.3 %collective-permute-start.2 = (bf16[96,512]{1,0:T(8,128)(2,1)S(1)}, bf16[96,512]{1,0:T(8,128)(2,1)S(1)}, u32[]{:S(2)}, u32[]{:S(2)}) collective-permute-start(bf16[96,512]{1,0:T(8,128)(2,1)S(1)} %select_convert_fusion.2), channel_id=1, source_target_pairs={{0,10},{2,8},{4,14},{6,12},{8,2},{10,0},{12,6},{14,4},{1,11},{3,9}... | collective-permute-start | bytes 294920 | tf_op jit(solution)/shard_map/ppermute | solution.py:443
  63.0 0.4 collective-permute-start.3
  63.4 1.2 %collective-permute-start.4 = (bf16[96,512]{1,0:T(8,128)(2,1)S(1)}, bf16[96,512]{1,0:T(8,128)(2,1)S(1)}, u32[]{:S(2)}, u32[]{:S(2)}) collective-permute-start(bf16[96,512]{1,0:T(8,128)(2,1)S(1)} %select_convert_fusion.2), channel_id=1, source_target_pairs={{0,8},{2,10},{4,12},{6,14},{8,0},{10,2},{12,4},{14,6},{1,9},{3,11}... | collective-permute-start | bytes 294920 | tf_op jit(solution)/shard_map/ppermute | solution.py:443
  64.6 0.9 emit.1
  65.5 1.9 %collective-permute-done.2 = bf16[96,512]{1,0:T(8,128)(2,1)S(1)} collective-permute-done((bf16[96,512]{1,0:T(8,128)(2,1)S(1)}, bf16[96,512]{1,0:T(8,128)(2,1)S(1)}, u32[]{:S(2)}, u32[]{:S(2)}) %collective-permute-start.2) | collective-permute-done | bytes 98336 | tf_op jit(solution)/shard_map/ppermute | solution.py:443
  67.4 9.1 %collective-permute-done.3 = bf16[96,512]{1,0:T(8,128)(2,1)S(1)} collective-permute-done((bf16[96,512]{1,0:T(8,128)(2,1)S(1)}, bf16[96,512]{1,0:T(8,128)(2,1)S(1)}, u32[]{:S(2)}, u32[]{:S(2)}) %collective-permute-start.3) | collective-permute-done | bytes 98336 | tf_op jit(solution)/shard_map/ppermute | solution.py:443
  76.6 0.1 select_convert_fusion.1
  76.7 0.0 all-to-all-done.2.parts_ref
  76.7 0.8 sum_parts.1
  77.4 2.6 %collective-permute-start.5 = (bf16[96,512]{1,0:T(8,128)(2,1)S(1)}, bf16[96,512]{1,0:T(8,128)(2,1)S(1)}, u32[]{:S(2)}, u32[]{:S(2)}) collective-permute-start(bf16[96,512]{1,0:T(8,128)(2,1)S(1)} %select_convert_fusion.1), channel_id=1, source_target_pairs={{0,4},{2,6},{4,0},{6,2},{1,5},{3,7},{5,1},{7,3},{8,12},{10,14},{12... | collective-permute-start | bytes 294920 | tf_op jit(solution)/shard_map/ppermute | solution.py:438
  80.1 4.1 %all-to-all-start.3 = ((bf16[8,8,512]{2,1,0:T(8,128)(2,1)}), bf16[8,8,512]{2,1,0:T(8,128)(2,1)S(1)}, u32[]{:S(2)}, u32[]{:S(2)}) async-start(bf16[8,8,512]{2,1,0:T(8,128)(2,1)} %bitcast.6), calls=%async_computation.3 | async-start | bytes 131072 | tf_op jit(solution)/shard_map/all_to_all | solution.py:485
  84.2 0.1 select_convert_fusion.mine_ref
  84.3 6.5 %all-to-all-done.3.parts_ref = bf16[8,8,512]{2,1,0:T(8,128)(2,1)S(1)} async-done(((bf16[8,8,512]{2,1,0:T(8,128)(2,1)}), bf16[8,8,512]{2,1,0:T(8,128)(2,1)S(1)}, u32[]{:S(2)}, u32[]{:S(2)}) %all-to-all-start.3) | async-done | bytes 65568 | tf_op jit(solution)/shard_map/all_to_all | solution.py:485
  90.8 2.8 %collective-permute-start.7 = (bf16[96,512]{1,0:T(8,128)(2,1)S(1)}, bf16[96,512]{1,0:T(8,128)(2,1)S(1)}, u32[]{:S(2)}, u32[]{:S(2)}) collective-permute-start(bf16[96,512]{1,0:T(8,128)(2,1)S(1)} %select_convert_fusion.mine_ref), channel_id=1, source_target_pairs={{0,1},{1,0},{2,3},{3,2},{4,5},{5,4},{6,7},{7,6},{8,9},{9,8},{10,11... | collective-permute-start | bytes 294920 | tf_op jit(solution)/shard_map/ppermute | solution.py:438
  93.6 0.1 collective-permute-start.6
  93.7 1.2 %collective-permute-done.6.got_ref = f32[4,512]{1,0:T(4,128)S(1)} collective-permute-done((f32[4,512]{1,0:T(4,128)S(1)}, f32[4,512]{1,0:T(4,128)S(1)}, u32[]{:S(2)}, u32[]{:S(2)}) %collective-permute-start.6) | collective-permute-done | bytes 8224 | tf_op jit(solution)/shard_map/ppermute | solution.py:438
  94.8 0.9 finish.1
  (11 shorter events, 0.2 us)
Async XLA Ops:
  44.8 6.4 %collective-permute-start = (bf16[16,64,512]{2,1,0:T(8,128)(2,1)S(1)}, bf16[16,64,512]{2,1,0:T(8,128)(2,1)S(1)}, u32[]{:S(2)}, u32[]{:S(2)}) collective-permute-start(bf16[16,64,512]{2,1,0:T(8,128)(2,1)S(1)} %get-tuple-element.42), channel_id=1, source_target_pairs={{0,1},{1,0},{2,3},{3,2},{4,5},{5,4},{6,7},{7,6},{8,9},{9,8},{10,11... | collective-permute-start | bytes 3145736 | tf_op jit(solution)/shard_map/ppermute | solution.py:438
  49.1 1.9 %collective-permute-start.1 = (bf16[96,512]{1,0:T(8,128)(2,1)S(1)}, bf16[96,512]{1,0:T(8,128)(2,1)S(1)}, u32[]{:S(2)}, u32[]{:S(2)}) collective-permute-start(bf16[96,512]{1,0:T(8,128)(2,1)S(1)} %get-tuple-element.46), channel_id=1, source_target_pairs={{0,1},{1,0},{2,3},{3,2},{4,5},{5,4},{6,7},{7,6},{8,9},{9,8},{10,11... | collective-permute-start | bytes 294920 | tf_op jit(solution)/shard_map/ppermute | solution.py:438
  52.6 24.1 %all-to-all-start.2 = ((bf16[16,64,512]{2,1,0:T(8,128)(2,1)}), bf16[16,64,512]{2,1,0:T(8,128)(2,1)S(1)}, u32[]{:S(2)}, u32[]{:S(2)}) async-start(bf16[16,64,512]{2,1,0:T(8,128)(2,1)} %add_convert_fusion), calls=%async_computation.2 | async-start | bytes 2097152 | tf_op jit(solution)/shard_map/all_to_all | solution.py:480
  57.8 9.6 %collective-permute-start.2 = (bf16[96,512]{1,0:T(8,128)(2,1)S(1)}, bf16[96,512]{1,0:T(8,128)(2,1)S(1)}, u32[]{:S(2)}, u32[]{:S(2)}) collective-permute-start(bf16[96,512]{1,0:T(8,128)(2,1)S(1)} %select_convert_fusion.2), channel_id=1, source_target_pairs={{0,10},{2,8},{4,14},{6,12},{8,2},{10,0},{12,6},{14,4},{1,11},{3,9}... | collective-permute-start | bytes 294920 | tf_op jit(solution)/shard_map/ppermute | solution.py:443
  63.0 13.5 %collective-permute-start.3 = (bf16[96,512]{1,0:T(8,128)(2,1)S(1)}, bf16[96,512]{1,0:T(8,128)(2,1)S(1)}, u32[]{:S(2)}, u32[]{:S(2)}) collective-permute-start(bf16[96,512]{1,0:T(8,128)(2,1)S(1)} %select_convert_fusion.2), channel_id=1, source_target_pairs={{0,2},{2,0},{4,6},{6,4},{8,10},{10,8},{12,14},{14,12},{1,3},{3,1},... | collective-permute-start | bytes 294920 | tf_op jit(solution)/shard_map/ppermute | solution.py:443
  63.4 13.1 %collective-permute-start.4 = (bf16[96,512]{1,0:T(8,128)(2,1)S(1)}, bf16[96,512]{1,0:T(8,128)(2,1)S(1)}, u32[]{:S(2)}, u32[]{:S(2)}) collective-permute-start(bf16[96,512]{1,0:T(8,128)(2,1)S(1)} %select_convert_fusion.2), channel_id=1, source_target_pairs={{0,8},{2,10},{4,12},{6,14},{8,0},{10,2},{12,4},{14,6},{1,9},{3,11}... | collective-permute-start | bytes 294920 | tf_op jit(solution)/shard_map/ppermute | solution.py:443
  77.4 6.7 %collective-permute-start.5 = (bf16[96,512]{1,0:T(8,128)(2,1)S(1)}, bf16[96,512]{1,0:T(8,128)(2,1)S(1)}, u32[]{:S(2)}, u32[]{:S(2)}) collective-permute-start(bf16[96,512]{1,0:T(8,128)(2,1)S(1)} %select_convert_fusion.1), channel_id=1, source_target_pairs={{0,4},{2,6},{4,0},{6,2},{1,5},{3,7},{5,1},{7,3},{8,12},{10,14},{12... | collective-permute-start | bytes 294920 | tf_op jit(solution)/shard_map/ppermute | solution.py:438
  80.1 10.7 %all-to-all-start.3 = ((bf16[8,8,512]{2,1,0:T(8,128)(2,1)}), bf16[8,8,512]{2,1,0:T(8,128)(2,1)S(1)}, u32[]{:S(2)}, u32[]{:S(2)}) async-start(bf16[8,8,512]{2,1,0:T(8,128)(2,1)} %bitcast.6), calls=%async_computation.3 | async-start | bytes 131072 | tf_op jit(solution)/shard_map/all_to_all | solution.py:485
  90.8 4.0 %collective-permute-start.7 = (bf16[96,512]{1,0:T(8,128)(2,1)S(1)}, bf16[96,512]{1,0:T(8,128)(2,1)S(1)}, u32[]{:S(2)}, u32[]{:S(2)}) collective-permute-start(bf16[96,512]{1,0:T(8,128)(2,1)S(1)} %select_convert_fusion.mine_ref), channel_id=1, source_target_pairs={{0,1},{1,0},{2,3},{3,2},{4,5},{5,4},{6,7},{7,6},{8,9},{9,8},{10,11... | collective-permute-start | bytes 294920 | tf_op jit(solution)/shard_map/ppermute | solution.py:438
  93.6 1.3 %collective-permute-start.6 = (f32[4,512]{1,0:T(4,128)S(1)}, f32[4,512]{1,0:T(4,128)S(1)}, u32[]{:S(2)}, u32[]{:S(2)}) collective-permute-start(f32[4,512]{1,0:T(4,128)S(1)} %get-tuple-element.54), channel_id=1, source_target_pairs={{0,1},{1,0},{2,3},{3,2},{4,5},{5,4},{6,7},{7,6},{8,9},{9,8},{10,11... | collective-permute-start | bytes 24584 | tf_op jit(solution)/shard_map/ppermute | solution.py:438

commit v4 on v3

--- a/solution.py
+++ b/solution.py
@@ -132,7 +132,7 @@
     decode(spans - 1)
     for g in range(GROUPS):
         for q in range(PTS // LANES):
-            blk_ref[g * GROUPS + q] = field[
+            blk_ref[q * GROUPS + g] = field[
                 g * ROWS : (g + 1) * ROWS, q * LANES : (q + 1) * LANES
             ].astype(BF)
 
@@ -252,8 +252,8 @@
 
 def arrange(rows):
     out = []
-    for x in range(4):
-        for y in range(4):
+    for y in range(4):
+        for x in range(4):
             pick = [rows[x * 64 + zh * 32 + y * 8 : x * 64 + zh * 32 + y * 8 + 8] for zh in range(2)]
             out.append(jnp.concatenate(pick, 0))
     return out
@@ -271,7 +271,7 @@
 
 def back_kernel(core_ref, blk_ref, der_ref, lat_ref, w2t_ref, bp_ref, send_ref, low_ref):
     for q in range(PTS // LANES):
-        parts = [blk_ref[g * GROUPS + q].astype(F32) for g in range(GROUPS)]
+        parts = [blk_ref[q * GROUPS + g].astype(F32) for g in range(GROUPS)]
         parts.append(jnp.zeros((128 - PAD, LANES), F32))
         low_ref[:, q * LANES : (q + 1) * LANES] = jnp.concatenate(parts, 0).astype(BF)
     for n in range(PTS // WIDE):
@@ -362,54 +362,55 @@
     )(core, low, hidden)
 
 
-def sum_kernel(scale, parts_ref, out_ref):
-    total = parts_ref[0].astype(F32)
-    for e in range(1, parts_ref.shape[0]):
+def total_of(parts_ref, which):
+    total = parts_ref[which[0]].astype(F32)
+    for e in which[1:]:
         total += parts_ref[e].astype(F32)
-    out_ref[...] = (total * scale).astype(out_ref.dtype)
-
-
-def sum_parts(parts, scale, dtype, flops):
-    return pl.pallas_call(
-        functools.partial(sum_kernel, scale),
+    return total
+
+
+def sum_chips_kernel(parts_ref, out_ref):
+    total = total_of(parts_ref, range(16))
+    for z in range(8):
+        for c in range(2):
+            at = z * 8 + c * 4
+            out_ref[c * 8 + z] = total[at : at + 4].astype(BF)
+
+
+def sum_chips(parts):
+    return pl.pallas_call(
+        sum_chips_kernel,
         in_specs=[VM],
         out_specs=VM,
-        out_shape=shape(parts.shape[1:], dtype),
-        compiler_params=params(6),
-        cost_estimate=pl.CostEstimate(flops=flops, bytes_accessed=parts.size * 2, transcendentals=0),
-        name="sum_parts",
-    )(parts)
-
-
-def halves_kernel(core_ref, parts_ref, keep_ref, give_ref):
-    total = parts_ref[0].astype(F32)
-    for e in range(1, parts_ref.shape[0]):
-        total += parts_ref[e].astype(F32)
-    total *= 1.0 / math.sqrt(MEMBERS * NPTS)
-    upper, under = total[:4], total[4:]
-    first_core = core_ref[0] == 0
-    keep_ref[...] = jnp.where(first_core, upper, under)
-    give_ref[...] = jnp.where(first_core, under, upper)
-
-
-def sum_halves(core, parts):
-    return pl.pallas_call(
-        halves_kernel,
-        in_specs=[SCALAR, VM],
-        out_specs=[VM, VM],
-        out_shape=[shape((4, H // 2), F32)] * 2,
+        out_shape=shape((16, 4, H // 2)),
         compiler_params=params(6),
         cost_estimate=pl.CostEstimate(flops=FLOPS, bytes_accessed=parts.size * 2, transcendentals=0),
-        name="sum_halves",
-    )(core, parts)
-
-
-def finish_kernel(core_ref, keep_ref, got_ref, mine_ref, other_ref, first_ref, second_ref, loss_ref):
+        name="sum_chips",
+    )(parts)
+
+
+def sum_last_kernel(parts_ref, out_ref):
+    half = H // 2
+    for c in range(2):
+        total = total_of(parts_ref, range(c * 8, c * 8 + 8))
+        out_ref[:, c * half : (c + 1) * half] = total * (1.0 / math.sqrt(MEMBERS * NPTS))
+
+
+def sum_last(parts):
+    return pl.pallas_call(
+        sum_last_kernel,
+        in_specs=[VM],
+        out_specs=VM,
+        out_shape=shape((4, H), F32),
+        compiler_params=params(6),
+        cost_estimate=pl.CostEstimate(flops=FLOPS, bytes_accessed=parts.size * 2, transcendentals=0),
+        name="sum_last",
+    )(parts)
+
+
+def finish_kernel(core_ref, mine_ref, other_ref, second_ref, loss_ref):
     half = H // 2
     first_core = core_ref[0] == 0
-    keep, got = keep_ref[...], got_ref[...]
-    first_ref[:, :half] = jnp.where(first_core, keep, got)
-    first_ref[:, half:] = jnp.where(first_core, got, keep)
     mine, other = mine_ref[...].astype(F32), other_ref[...].astype(F32)
     left, right = jnp.where(first_core, mine, other), jnp.where(first_core, other, mine)
     loss = left[HI : HI + 1, :LANES] + left[LO : LO + 1, :LANES]
@@ -422,15 +423,16 @@
             second_ref[g * USED : g * USED + used, :, cols] = rows.reshape(used, 1, half)
 
 
-def finish(core, keep, got, mine, other):
+def finish(core, mine, other):
     return pl.pallas_call(
         finish_kernel,
-        in_specs=[SCALAR, VM, VM, VM, VM],
-        out_specs=[VM] * 3,
-        out_shape=[shape((4, H), F32), shape((C, 1, H2), F32), shape((1, 1), F32)],
+        in_specs=[SCALAR, VM, VM],
+        out_specs=[VM] * 2,
+        out_shape=[shape((C, 1, H2), F32), shape((1, 1), F32)],
         compiler_params=params(6),
+        cost_estimate=pl.CostEstimate(flops=0, bytes_accessed=PTS, transcendentals=0),
         name="finish",
-    )(core, keep, got, mine, other)
+    )(core, mine, other)
 
 
 def swap(value, axis, by):
@@ -461,9 +463,9 @@
         where, latent, w_first, w_second, truth
     )
 
-    gathered = lax.all_to_all(blocks, ("zl", "x"), 0, 0, tiled=True)
+    gathered = lax.all_to_all(blocks, ("x", "zl"), 0, 0, tiled=True)
     grads = pairs(gathered, truth_here, area)
-    grads = lax.all_to_all(grads, ("zl", "x"), 0, 0, tiled=True)
+    grads = lax.all_to_all(grads, ("x", "zl"), 0, 0, tiled=True)
 
     bp, send, low = backward(core, grads, deriv, kept_latent, w2t)
     arrived = swap(send, "c", 1)
@@ -477,19 +479,15 @@
     field_grad = emit(low)
     near, far, both = (cross(total, h, y).astype(F32) for h, y in ((0, 1), (1, 0), (1, 1)))
     total = packed((total.astype(F32) + both) + (near + far))
-    first = lax.all_to_all(first, ("x", "y"), 0, 0, tiled=True)
-    first = sum_parts(first, 1.0, BF, FLOPS).reshape(8, 8, H // 2)
+    first = lax.all_to_all(first, ("y", "x"), 0, 0, tiled=True)
+    first = sum_chips(first)
     first, total, field_grad = lax.optimization_barrier((first, total, field_grad))
 
     total = packed(total.astype(F32) + swap(total, "y", 2).astype(F32))
-    first = lax.all_to_all(first, ("zl", "zh"), 0, 0, tiled=True)
-    first, total = lax.optimization_barrier((first, total))
-
-    other = swap(total, "c", 1)
-    keep, give = sum_halves(core, first)
-    got = swap(give, "c", 1)
-    first_out, second_out, loss = finish(core, keep, got, total, other)
-    return loss[0], field_grad.transpose(1, 0, 2), first_out, second_out.transpose(1, 0, 2)
+    second_out, loss = finish(core, total, swap(total, "c", 1))
+    first = lax.all_to_all(first, ("c", "zl", "zh"), 0, 0, tiled=True)
+    first, second_out, loss = lax.optimization_barrier((first, second_out, loss))
+    return loss[0], field_grad.transpose(1, 0, 2), sum_last(first), second_out.transpose(1, 0, 2)
 
 
 def solution(mesh):

time: 96 us -> 94 us (0.979)
  starting transfers between devices: 24.8 us -> 22.6 us
  waiting for transfers between devices: 18.6 us -> 17 us
  blocking collectives: 32 us -> 33.3 us
    ppermute x5 -> x4, starting transfers between devices: 8.71 us -> 4.95 us  [swap(): return lax.ppermute(value, axis, [(i, i ^ by) for i in range(size)])]
    all_to_all x2, starting transfers between devices: 9.27 us -> 10.8 us  [the longest x1 6.26 us: on_device(): first = lax.all_to_all(first, ('c', 'zl', 'zh'), 0, 0, tiled=True)]
    all_to_all x2, waiting for transfers between devices: 6.47 us -> 5.07 us  [the longest x1 5.07 us: on_device(): first = lax.all_to_all(first, ('c', 'zl', 'zh'), 0, 0, tiled=True)]
    all_to_all x2, blocking collectives: 32 us -> 33.3 us  [the longest x1 19.4 us: on_device(): gathered = lax.all_to_all(blocks, ('x', 'zl'), 0, 0, tiled=True)]
  transfers between devices with their start and end apart: 10 -> 9, of which waited for: 4 -> 4; matrix products, arithmetic and copies ran while one was open for 0% -> 0% of each run, Pallas kernels for 4% -> 5%
where the time goes in v4:
time: 94 us; the launch traced here: 93.7 us
  blocking collectives  33.3 us (35%)
  starting transfers between devices  22.6 us (24%)
  Pallas kernels  18.1 us (19%)
  waiting for transfers between devices  17 us (18%)
  other arithmetic  1.86 us (2%)
    all_to_all x1, blocking collectives, on_device(): gathered = lax.all_to_all(blocks, ('x', 'zl'), 0, 0, tiled=True)  19.4 us
    all_to_all x1, blocking collectives, on_device(): grads = lax.all_to_all(grads, ('x', 'zl'), 0, 0, tiled=True)  13.8 us
    ppermute x3, waiting for transfers between devices, cross(): return lax.ppermute(value, ('zh', 'y'), pairs)  10.7 us
    pallas_call x1, Pallas kernels, forward(): pl.pallas_call(forward_kernel, in_specs=[SCALAR, HBM, HBM, HBM, HBM], out...  7.4 us
    ppermute x3, starting transfers between devices, cross(): return lax.ppermute(value, ('zh', 'y'), pairs)  6.82 us
    all_to_all x1, starting transfers between devices, on_device(): first = lax.all_to_all(first, ('c', 'zl', 'zh'), 0, 0, tiled=True)  6.26 us
    all_to_all x1, waiting for transfers between devices, on_device(): first = lax.all_to_all(first, ('c', 'zl', 'zh'), 0, 0, tiled=True)  5.07 us
    ppermute x4, starting transfers between devices, swap(): return lax.ppermute(value, axis, [(i, i ^ by) for i in range(size)])  4.95 us
  transfers between devices with their start and end apart: 9, of which 4 were waited for; matrix products, arithmetic and copies ran while one was open for 0% of the time, Pallas kernels for 5%

profile of v4, /device:TPU:1, one launch (start us, length us, event | category | flops | bytes accessed | tf_op | source)
XLA Modules:
  0.0 93.7 jit_solution(17987691430039847907)
XLA Ops:
  0.6 0.1 pad_add_fusion.where_ref
  0.7 7.4 %forward.1 = (bf16[1024,1536]{1,0:T(8,128)(2,1)S(1)}, bf16[1024,1536]{1,0:T(8,128)(2,1)S(1)}, bf16[1024,1536]{1,0:T(8,128)(2,1)S(1)}, bf16[16,24,384]{2,1,0:T(8,...) custom-call(s32[3]{0:T(128)S(1)} %pad_add_fusion.where_ref, ...), custom_call_target="tpu_custom_call" | custom-call | tf_op jit(solution)/shard_map/forward/pallas_call | solution.py:142
  8.1 19.4 %all_to_all.20.fields_ref = bf16[16,24,384]{2,1,0:T(8,128)(2,1)S(1)} all-to-all(bf16[16,24,384]{2,1,0:T(8,128)(2,1)S(1)} %get-tuple-element.33), channel_id=1, replica_groups=mesh['zl'=4,'x'=4,'zh'=2,'y'=4,'c'=2] {'x','zl'}, dimensions={0} | all-to-all | bytes 589824 | tf_op jit(solution)/shard_map/all_to_all | solution.py:466
  27.5 2.0 %pairs.1 = bf16[16,24,384]{2,1,0:T(8,128)(2,1)S(1)} custom-call(bf16[16,24,384]{2,1,0:T(8,128)(2,1)S(1)} %all_to_all.20.fields_ref, f32[9,8,128]{2,1,0:T(8,128)S(1)} %get-tuple-element.34.truth_ref, f32[9,8,128]{2,1,0:T(8,128)S(1)} %get-tuple-element.35.area_ref), custom_call_target="tpu_custom_call" | custom-call | tf_op jit(solution)/shard_map/pairs/pallas_call | solution.py:239
  29.6 13.8 %all_to_all.21.blk_ref = bf16[16,24,384]{2,1,0:T(8,128)(2,1)S(1)} all-to-all(bf16[16,24,384]{2,1,0:T(8,128)(2,1)S(1)} %pairs.1), channel_id=1, replica_groups=mesh['zl'=4,'x'=4,'zh'=2,'y'=4,'c'=2] {'x','zl'}, dimensions={0} | all-to-all | bytes 589824 | tf_op jit(solution)/shard_map/all_to_all | solution.py:468
  43.4 2.6 %backward.1 = (bf16[1024,1536]{1,0:T(8,128)(2,1)S(1)}, bf16[16,64,512]{2,1,0:T(8,128)(2,1)S(1)}, bf16[128,1536]{1,0:T(8,128)(2,1)S(1)}) custom-call(s32[1]{0:T(128)} %bitcast.3.core_ref, bf16[16,24,384]{2,1,0:T(8,128)(2,1)S(1)} %all_to_all.21.blk_ref, bf16[1024,1536]{1,0:T(8,128)(2,1)S(1)} %get-tuple-element.36.der_ref, ...), custom_call_target="tpu_custom_call" | custom-call | tf_op jit(solution)/shard_map/backward/pallas_call | solution.py:285
  46.0 2.2 %collective-permute-start = (bf16[16,64,512]{2,1,0:T(8,128)(2,1)S(1)}, bf16[16,64,512]{2,1,0:T(8,128)(2,1)S(1)}, u32[]{:S(2)}, u32[]{:S(2)}) collective-permute-start(bf16[16,64,512]{2,1,0:T(8,128)(2,1)S(1)} %get-tuple-element.40), channel_id=1, source_target_pairs={{0,1},{1,0},{2,3},{3,2},{4,5},{5,4},{6,7},{7,6},{8,9},{9,8},{10,11... | collective-permute-start | bytes 3145736 | tf_op jit(solution)/shard_map/ppermute | solution.py:440
  48.3 1.2 %second.1 = (f32[96,512]{1,0:T(8,128)S(1)}, bf16[96,512]{1,0:T(8,128)(2,1)S(1)}) custom-call(s32[1]{0:T(128)} %bitcast.3.core_ref, bf16[128,1536]{1,0:T(8,128)(2,1)S(1)} %get-tuple-element.47.low_ref, bf16[1024,1536]{1,0:T(8,128)(2,1)S(1)} %get-tuple-element.42.hid_ref), custom_call_target="tpu_custom_call" | custom-call | tf_op jit(solution)/shard_map/second/pallas_call | solution.py:354
  49.4 0.1 collective-permute-start.1
  49.6 1.8 %own_half.1 = f32[16,64,512]{2,1,0:T(8,128)S(1)} custom-call(s32[1]{0:T(128)} %bitcast.3.core_ref, bf16[1024,1536]{1,0:T(8,128)(2,1)S(1)} %get-tuple-element.39.bp_ref, bf16[1024,1536]{1,0:T(8,128)(2,1)S(1)} %get-tuple-element.37.lat_ref), custom_call_target="tpu_custom_call" | custom-call | flops 1610612736 | bytes 8388608 | tf_op jit(solution)/shard_map/own_half/pallas_call | solution.py:300
  51.4 0.0 collective-permute-done.1
  51.4 0.1 select_convert_fusion.2
  51.5 1.4 %add_convert_fusion = bf16[16,64,512]{2,1,0:T(8,128)(2,1)} fusion(f32[16,64,512]{2,1,0:T(8,128)S(1)} %own_half.1, bf16[16,64,512]{2,1,0:T(8,128)(2,1)S(1)} %collective-permute-done), kind=kLoop, calls=%fused_computation | loop fusion | flops 1572864 | bytes 4194304 | tf_op jit(solution)/shard_map/convert_element_type | solution.py:475
  52.9 4.6 %all-to-all-start.2 = ((bf16[16,64,512]{2,1,0:T(8,128)(2,1)}), bf16[16,64,512]{2,1,0:T(8,128)(2,1)S(1)}, u32[]{:S(2)}, u32[]{:S(2)}) async-start(bf16[16,64,512]{2,1,0:T(8,128)(2,1)} %add_convert_fusion), calls=%async_computation.2 | async-start | bytes 2097152 | tf_op jit(solution)/shard_map/all_to_all | solution.py:482
  57.5 5.2 %collective-permute-start.2 = (bf16[96,512]{1,0:T(8,128)(2,1)S(1)}, bf16[96,512]{1,0:T(8,128)(2,1)S(1)}, u32[]{:S(2)}, u32[]{:S(2)}) collective-permute-start(bf16[96,512]{1,0:T(8,128)(2,1)S(1)} %select_convert_fusion.2), channel_id=1, source_target_pairs={{0,10},{2,8},{4,14},{6,12},{8,2},{10,0},{12,6},{14,4},{1,11},{3,9}... | collective-permute-start | bytes 294920 | tf_op jit(solution)/shard_map/ppermute | solution.py:445
  62.7 0.4 collective-permute-start.3
  63.1 1.2 %collective-permute-start.4 = (bf16[96,512]{1,0:T(8,128)(2,1)S(1)}, bf16[96,512]{1,0:T(8,128)(2,1)S(1)}, u32[]{:S(2)}, u32[]{:S(2)}) collective-permute-start(bf16[96,512]{1,0:T(8,128)(2,1)S(1)} %select_convert_fusion.2), channel_id=1, source_target_pairs={{0,8},{2,10},{4,12},{6,14},{8,0},{10,2},{12,4},{14,6},{1,9},{3,11}... | collective-permute-start | bytes 294920 | tf_op jit(solution)/shard_map/ppermute | solution.py:445
  64.3 0.9 emit.1
  65.2 1.8 %collective-permute-done.2 = bf16[96,512]{1,0:T(8,128)(2,1)S(1)} collective-permute-done((bf16[96,512]{1,0:T(8,128)(2,1)S(1)}, bf16[96,512]{1,0:T(8,128)(2,1)S(1)}, u32[]{:S(2)}, u32[]{:S(2)}) %collective-permute-start.2) | collective-permute-done | bytes 98336 | tf_op jit(solution)/shard_map/ppermute | solution.py:445
  67.0 8.9 %collective-permute-done.3 = bf16[96,512]{1,0:T(8,128)(2,1)S(1)} collective-permute-done((bf16[96,512]{1,0:T(8,128)(2,1)S(1)}, bf16[96,512]{1,0:T(8,128)(2,1)S(1)}, u32[]{:S(2)}, u32[]{:S(2)}) %collective-permute-start.3) | collective-permute-done | bytes 98336 | tf_op jit(solution)/shard_map/ppermute | solution.py:445
  75.9 0.0 collective-permute-done.4
  76.0 0.1 select_convert_fusion.1
  76.1 0.0 all-to-all-done.2.parts_ref
  76.1 0.8 sum_chips.1
  76.9 2.4 %collective-permute-start.5 = (bf16[96,512]{1,0:T(8,128)(2,1)S(1)}, bf16[96,512]{1,0:T(8,128)(2,1)S(1)}, u32[]{:S(2)}, u32[]{:S(2)}) collective-permute-start(bf16[96,512]{1,0:T(8,128)(2,1)S(1)} %select_convert_fusion.1), channel_id=1, source_target_pairs={{0,4},{2,6},{4,0},{6,2},{1,5},{3,7},{5,1},{7,3},{8,12},{10,14},{12... | collective-permute-start | bytes 294920 | tf_op jit(solution)/shard_map/ppermute | solution.py:440
  79.3 6.3 %all-to-all-start.3 = ((bf16[16,4,512]{2,1,0:T(4,128)(2,1)}), bf16[16,4,512]{2,1,0:T(4,128)(2,1)S(1)}, u32[]{:S(2)}, u32[]{:S(2)}) async-start(bf16[16,4,512]{2,1,0:T(4,128)(2,1)} %sum_chips.1), calls=%async_computation.3 | async-start | bytes 131072 | tf_op jit(solution)/shard_map/all_to_all | solution.py:488
  85.6 0.1 select_convert_fusion.mine_ref
  85.7 0.2 collective-permute-start.6
  85.9 1.2 %collective-permute-done.6.other_ref = bf16[96,512]{1,0:T(8,128)(2,1)S(1)} collective-permute-done((bf16[96,512]{1,0:T(8,128)(2,1)S(1)}, bf16[96,512]{1,0:T(8,128)(2,1)S(1)}, u32[]{:S(2)}, u32[]{:S(2)}) %collective-permute-start.6) | collective-permute-done | bytes 98336 | tf_op jit(solution)/shard_map/ppermute | solution.py:440
  87.1 0.9 finish.1
  88.0 5.1 %all-to-all-done.3.parts_ref = bf16[16,4,512]{2,1,0:T(4,128)(2,1)S(1)} async-done(((bf16[16,4,512]{2,1,0:T(4,128)(2,1)}), bf16[16,4,512]{2,1,0:T(4,128)(2,1)S(1)}, u32[]{:S(2)}, u32[]{:S(2)}) %all-to-all-start.3) | async-done | bytes 65568 | tf_op jit(solution)/shard_map/all_to_all | solution.py:488
  93.1 0.6 sum_last.1
  (9 shorter events, 0.1 us)
Async XLA Ops:
  46.0 5.5 %collective-permute-start = (bf16[16,64,512]{2,1,0:T(8,128)(2,1)S(1)}, bf16[16,64,512]{2,1,0:T(8,128)(2,1)S(1)}, u32[]{:S(2)}, u32[]{:S(2)}) collective-permute-start(bf16[16,64,512]{2,1,0:T(8,128)(2,1)S(1)} %get-tuple-element.40), channel_id=1, source_target_pairs={{0,1},{1,0},{2,3},{3,2},{4,5},{5,4},{6,7},{7,6},{8,9},{9,8},{10,11... | collective-permute-start | bytes 3145736 | tf_op jit(solution)/shard_map/ppermute | solution.py:440
  49.4 1.9 %collective-permute-start.1 = (bf16[96,512]{1,0:T(8,128)(2,1)S(1)}, bf16[96,512]{1,0:T(8,128)(2,1)S(1)}, u32[]{:S(2)}, u32[]{:S(2)}) collective-permute-start(bf16[96,512]{1,0:T(8,128)(2,1)S(1)} %get-tuple-element.44), channel_id=1, source_target_pairs={{0,1},{1,0},{2,3},{3,2},{4,5},{5,4},{6,7},{7,6},{8,9},{9,8},{10,11... | collective-permute-start | bytes 294920 | tf_op jit(solution)/shard_map/ppermute | solution.py:440
  52.9 23.2 %all-to-all-start.2 = ((bf16[16,64,512]{2,1,0:T(8,128)(2,1)}), bf16[16,64,512]{2,1,0:T(8,128)(2,1)S(1)}, u32[]{:S(2)}, u32[]{:S(2)}) async-start(bf16[16,64,512]{2,1,0:T(8,128)(2,1)} %add_convert_fusion), calls=%async_computation.2 | async-start | bytes 2097152 | tf_op jit(solution)/shard_map/all_to_all | solution.py:482
  57.5 9.5 %collective-permute-start.2 = (bf16[96,512]{1,0:T(8,128)(2,1)S(1)}, bf16[96,512]{1,0:T(8,128)(2,1)S(1)}, u32[]{:S(2)}, u32[]{:S(2)}) collective-permute-start(bf16[96,512]{1,0:T(8,128)(2,1)S(1)} %select_convert_fusion.2), channel_id=1, source_target_pairs={{0,10},{2,8},{4,14},{6,12},{8,2},{10,0},{12,6},{14,4},{1,11},{3,9}... | collective-permute-start | bytes 294920 | tf_op jit(solution)/shard_map/ppermute | solution.py:445
  62.7 13.2 %collective-permute-start.3 = (bf16[96,512]{1,0:T(8,128)(2,1)S(1)}, bf16[96,512]{1,0:T(8,128)(2,1)S(1)}, u32[]{:S(2)}, u32[]{:S(2)}) collective-permute-start(bf16[96,512]{1,0:T(8,128)(2,1)S(1)} %select_convert_fusion.2), channel_id=1, source_target_pairs={{0,2},{2,0},{4,6},{6,4},{8,10},{10,8},{12,14},{14,12},{1,3},{3,1},... | collective-permute-start | bytes 294920 | tf_op jit(solution)/shard_map/ppermute | solution.py:445
  63.1 12.8 %collective-permute-start.4 = (bf16[96,512]{1,0:T(8,128)(2,1)S(1)}, bf16[96,512]{1,0:T(8,128)(2,1)S(1)}, u32[]{:S(2)}, u32[]{:S(2)}) collective-permute-start(bf16[96,512]{1,0:T(8,128)(2,1)S(1)} %select_convert_fusion.2), channel_id=1, source_target_pairs={{0,8},{2,10},{4,12},{6,14},{8,0},{10,2},{12,4},{14,6},{1,9},{3,11}... | collective-permute-start | bytes 294920 | tf_op jit(solution)/shard_map/ppermute | solution.py:445
  76.9 8.7 %collective-permute-start.5 = (bf16[96,512]{1,0:T(8,128)(2,1)S(1)}, bf16[96,512]{1,0:T(8,128)(2,1)S(1)}, u32[]{:S(2)}, u32[]{:S(2)}) collective-permute-start(bf16[96,512]{1,0:T(8,128)(2,1)S(1)} %select_convert_fusion.1), channel_id=1, source_target_pairs={{0,4},{2,6},{4,0},{6,2},{1,5},{3,7},{5,1},{7,3},{8,12},{10,14},{12... | collective-permute-start | bytes 294920 | tf_op jit(solution)/shard_map/ppermute | solution.py:440
  79.3 13.7 %all-to-all-start.3 = ((bf16[16,4,512]{2,1,0:T(4,128)(2,1)}), bf16[16,4,512]{2,1,0:T(4,128)(2,1)S(1)}, u32[]{:S(2)}, u32[]{:S(2)}) async-start(bf16[16,4,512]{2,1,0:T(4,128)(2,1)} %sum_chips.1), calls=%async_computation.3 | async-start | bytes 131072 | tf_op jit(solution)/shard_map/all_to_all | solution.py:488
  85.7 1.4 %collective-permute-start.6 = (bf16[96,512]{1,0:T(8,128)(2,1)S(1)}, bf16[96,512]{1,0:T(8,128)(2,1)S(1)}, u32[]{:S(2)}, u32[]{:S(2)}) collective-permute-start(bf16[96,512]{1,0:T(8,128)(2,1)S(1)} %select_convert_fusion.mine_ref), channel_id=1, source_target_pairs={{0,1},{1,0},{2,3},{3,2},{4,5},{5,4},{6,7},{7,6},{8,9},{9,8},{10,11... | collective-permute-start | bytes 294920 | tf_op jit(solution)/shard_map/ppermute | solution.py:440

commit v5 on v4

--- a/solution.py
+++ b/solution.py
@@ -441,8 +441,13 @@
 
 
 def cross(value, h, y):
-    pairs = [(zh * 4 + k, (zh ^ h) * 4 + (k ^ y)) for zh in range(2) for k in range(4)]
-    return lax.ppermute(value, ("zh", "y"), pairs)
+    pairs = []
+    for zh in range(2):
+        for k in range(4):
+            for c in range(2):
+                mate = (k + (1 if k % 2 == c else 3)) % 4 if y else k
+                pairs.append(((zh * 4 + k) * 2 + c, ((zh ^ h) * 4 + mate) * 2 + c))
+    return lax.ppermute(value, ("zh", "y", "c"), pairs)
 
 
 def packed(total):

time: 94 us -> 93 us (0.989)
  waiting for transfers between devices: 17 us -> 14 us
  starting transfers between devices: 22.6 us -> 24.7 us
    ppermute x3, waiting for transfers between devices: 10.7 us -> 7.68 us  [cross(): return lax.ppermute(value, ('zh', 'y', 'c'), pairs)]
    all_to_all x1, starting transfers between devices: 6.26 us -> 8.4 us  [on_device(): first = lax.all_to_all(first, ('c', 'zl', 'zh'), 0, 0, tiled=True)]
    ppermute x4, starting transfers between devices: 4.95 us -> 3.64 us  [swap(): return lax.ppermute(value, axis, [(i, i ^ by) for i in range(size)])]
    ppermute x3, starting transfers between devices: 6.82 us -> 8.03 us  [cross(): return lax.ppermute(value, ('zh', 'y', 'c'), pairs)]
where the time goes in v5:
time: 93 us; the launch traced here: 92.7 us
  blocking collectives  33.3 us (36%)
  starting transfers between devices  24.7 us (27%)
  Pallas kernels  18.1 us (19%)
  waiting for transfers between devices  14 us (15%)
  other arithmetic  1.86 us (2%)
    all_to_all x1, blocking collectives, on_device(): gathered = lax.all_to_all(blocks, ('x', 'zl'), 0, 0, tiled=True)  19.4 us
    all_to_all x1, blocking collectives, on_device(): grads = lax.all_to_all(grads, ('x', 'zl'), 0, 0, tiled=True)  13.8 us
    all_to_all x1, starting transfers between devices, on_device(): first = lax.all_to_all(first, ('c', 'zl', 'zh'), 0, 0, tiled=True)  8.4 us
    ppermute x3, starting transfers between devices, cross(): return lax.ppermute(value, ('zh', 'y', 'c'), pairs)  8.03 us
    ppermute x3, waiting for transfers between devices, cross(): return lax.ppermute(value, ('zh', 'y', 'c'), pairs)  7.68 us
    pallas_call x1, Pallas kernels, forward(): pl.pallas_call(forward_kernel, in_specs=[SCALAR, HBM, HBM, HBM, HBM], out...  7.4 us
    all_to_all x1, waiting for transfers between devices, on_device(): first = lax.all_to_all(first, ('c', 'zl', 'zh'), 0, 0, tiled=True)  5.07 us
    all_to_all x1, starting transfers between devices, on_device(): first = lax.all_to_all(first, ('y', 'x'), 0, 0, tiled=True)  4.58 us
  transfers between devices with their start and end apart: 9, of which 4 were waited for; matrix products, arithmetic and copies ran while one was open for 0% of the time, Pallas kernels for 5%

profile of v5, /device:TPU:1, one launch (start us, length us, event | category | flops | bytes accessed | tf_op | source)
XLA Modules:
  0.0 92.7 jit_solution(11562732651736466661)
XLA Ops:
  0.6 0.1 pad_add_fusion.where_ref
  0.7 7.4 %forward.1 = (bf16[1024,1536]{1,0:T(8,128)(2,1)S(1)}, bf16[1024,1536]{1,0:T(8,128)(2,1)S(1)}, bf16[1024,1536]{1,0:T(8,128)(2,1)S(1)}, bf16[16,24,384]{2,1,0:T(8,...) custom-call(s32[3]{0:T(128)S(1)} %pad_add_fusion.where_ref, ...), custom_call_target="tpu_custom_call" | custom-call | tf_op jit(solution)/shard_map/forward/pallas_call | solution.py:142
  8.1 19.4 %all_to_all.20.fields_ref = bf16[16,24,384]{2,1,0:T(8,128)(2,1)S(1)} all-to-all(bf16[16,24,384]{2,1,0:T(8,128)(2,1)S(1)} %get-tuple-element.33), channel_id=1, replica_groups=mesh['zl'=4,'x'=4,'zh'=2,'y'=4,'c'=2] {'x','zl'}, dimensions={0} | all-to-all | bytes 589824 | tf_op jit(solution)/shard_map/all_to_all | solution.py:471
  27.5 2.0 %pairs.1 = bf16[16,24,384]{2,1,0:T(8,128)(2,1)S(1)} custom-call(bf16[16,24,384]{2,1,0:T(8,128)(2,1)S(1)} %all_to_all.20.fields_ref, f32[9,8,128]{2,1,0:T(8,128)S(1)} %get-tuple-element.34.truth_ref, f32[9,8,128]{2,1,0:T(8,128)S(1)} %get-tuple-element.35.area_ref), custom_call_target="tpu_custom_call" | custom-call | tf_op jit(solution)/shard_map/pairs/pallas_call | solution.py:239
  29.6 13.8 %all_to_all.21.blk_ref = bf16[16,24,384]{2,1,0:T(8,128)(2,1)S(1)} all-to-all(bf16[16,24,384]{2,1,0:T(8,128)(2,1)S(1)} %pairs.1), channel_id=1, replica_groups=mesh['zl'=4,'x'=4,'zh'=2,'y'=4,'c'=2] {'x','zl'}, dimensions={0} | all-to-all | bytes 589824 | tf_op jit(solution)/shard_map/all_to_all | solution.py:473
  43.4 2.6 %backward.1 = (bf16[1024,1536]{1,0:T(8,128)(2,1)S(1)}, bf16[16,64,512]{2,1,0:T(8,128)(2,1)S(1)}, bf16[128,1536]{1,0:T(8,128)(2,1)S(1)}) custom-call(s32[1]{0:T(128)} %bitcast.3.core_ref, bf16[16,24,384]{2,1,0:T(8,128)(2,1)S(1)} %all_to_all.21.blk_ref, bf16[1024,1536]{1,0:T(8,128)(2,1)S(1)} %get-tuple-element.36.der_ref, ...), custom_call_target="tpu_custom_call" | custom-call | tf_op jit(solution)/shard_map/backward/pallas_call | solution.py:285
  46.0 2.2 %collective-permute-start = (bf16[16,64,512]{2,1,0:T(8,128)(2,1)S(1)}, bf16[16,64,512]{2,1,0:T(8,128)(2,1)S(1)}, u32[]{:S(2)}, u32[]{:S(2)}) collective-permute-start(bf16[16,64,512]{2,1,0:T(8,128)(2,1)S(1)} %get-tuple-element.40), channel_id=1, source_target_pairs={{0,1},{1,0},{2,3},{3,2},{4,5},{5,4},{6,7},{7,6},{8,9},{9,8},{10,11... | collective-permute-start | bytes 3145736 | tf_op jit(solution)/shard_map/ppermute | solution.py:440
  48.3 1.2 %second.1 = (f32[96,512]{1,0:T(8,128)S(1)}, bf16[96,512]{1,0:T(8,128)(2,1)S(1)}) custom-call(s32[1]{0:T(128)} %bitcast.3.core_ref, bf16[128,1536]{1,0:T(8,128)(2,1)S(1)} %get-tuple-element.47.low_ref, bf16[1024,1536]{1,0:T(8,128)(2,1)S(1)} %get-tuple-element.42.hid_ref), custom_call_target="tpu_custom_call" | custom-call | tf_op jit(solution)/shard_map/second/pallas_call | solution.py:354
  49.4 0.1 collective-permute-start.1
  49.6 1.8 %own_half.1 = f32[16,64,512]{2,1,0:T(8,128)S(1)} custom-call(s32[1]{0:T(128)} %bitcast.3.core_ref, bf16[1024,1536]{1,0:T(8,128)(2,1)S(1)} %get-tuple-element.39.bp_ref, bf16[1024,1536]{1,0:T(8,128)(2,1)S(1)} %get-tuple-element.37.lat_ref), custom_call_target="tpu_custom_call" | custom-call | flops 1610612736 | bytes 8388608 | tf_op jit(solution)/shard_map/own_half/pallas_call | solution.py:300
  51.4 0.0 collective-permute-done.1
  51.4 0.1 select_convert_fusion.2
  51.5 0.0 collective-permute-done
  51.5 1.4 %add_convert_fusion = bf16[16,64,512]{2,1,0:T(8,128)(2,1)} fusion(f32[16,64,512]{2,1,0:T(8,128)S(1)} %own_half.1, bf16[16,64,512]{2,1,0:T(8,128)(2,1)S(1)} %collective-permute-done), kind=kLoop, calls=%fused_computation | loop fusion | flops 1572864 | bytes 4194304 | tf_op jit(solution)/shard_map/convert_element_type | solution.py:480
  52.9 4.6 %all-to-all-start.2 = ((bf16[16,64,512]{2,1,0:T(8,128)(2,1)}), bf16[16,64,512]{2,1,0:T(8,128)(2,1)S(1)}, u32[]{:S(2)}, u32[]{:S(2)}) async-start(bf16[16,64,512]{2,1,0:T(8,128)(2,1)} %add_convert_fusion), calls=%async_computation.2 | async-start | bytes 2097152 | tf_op jit(solution)/shard_map/all_to_all | solution.py:487
  57.5 6.5 %collective-permute-start.2 = (bf16[96,512]{1,0:T(8,128)(2,1)S(1)}, bf16[96,512]{1,0:T(8,128)(2,1)S(1)}, u32[]{:S(2)}, u32[]{:S(2)}) collective-permute-start(bf16[96,512]{1,0:T(8,128)(2,1)S(1)} %select_convert_fusion.2), channel_id=1, source_target_pairs={{0,10},{1,15},{2,8},{3,13},{4,14},{5,11},{6,12},{7,9},{8,2},{9,7},... | collective-permute-start | bytes 294920 | tf_op jit(solution)/shard_map/ppermute | solution.py:450
  64.0 0.4 collective-permute-start.3
  64.3 1.2 %collective-permute-start.4 = (bf16[96,512]{1,0:T(8,128)(2,1)S(1)}, bf16[96,512]{1,0:T(8,128)(2,1)S(1)}, u32[]{:S(2)}, u32[]{:S(2)}) collective-permute-start(bf16[96,512]{1,0:T(8,128)(2,1)S(1)} %select_convert_fusion.2), channel_id=1, source_target_pairs={{0,8},{1,9},{2,10},{3,11},{4,12},{5,13},{6,14},{7,15},{8,0},{9,1},... | collective-permute-start | bytes 294920 | tf_op jit(solution)/shard_map/ppermute | solution.py:450
  65.5 0.9 emit.1
  66.4 1.9 %collective-permute-done.2 = bf16[96,512]{1,0:T(8,128)(2,1)S(1)} collective-permute-done((bf16[96,512]{1,0:T(8,128)(2,1)S(1)}, bf16[96,512]{1,0:T(8,128)(2,1)S(1)}, u32[]{:S(2)}, u32[]{:S(2)}) %collective-permute-start.2) | collective-permute-done | bytes 98336 | tf_op jit(solution)/shard_map/ppermute | solution.py:450
  68.3 5.8 %collective-permute-done.3 = bf16[96,512]{1,0:T(8,128)(2,1)S(1)} collective-permute-done((bf16[96,512]{1,0:T(8,128)(2,1)S(1)}, bf16[96,512]{1,0:T(8,128)(2,1)S(1)}, u32[]{:S(2)}, u32[]{:S(2)}) %collective-permute-start.3) | collective-permute-done | bytes 98336 | tf_op jit(solution)/shard_map/ppermute | solution.py:450
  74.2 0.1 select_convert_fusion.1
  74.3 0.8 sum_chips.1
  75.1 1.1 %collective-permute-start.5 = (bf16[96,512]{1,0:T(8,128)(2,1)S(1)}, bf16[96,512]{1,0:T(8,128)(2,1)S(1)}, u32[]{:S(2)}, u32[]{:S(2)}) collective-permute-start(bf16[96,512]{1,0:T(8,128)(2,1)S(1)} %select_convert_fusion.1), channel_id=1, source_target_pairs={{0,4},{2,6},{4,0},{6,2},{1,5},{3,7},{5,1},{7,3},{8,12},{10,14},{12... | collective-permute-start | bytes 294920 | tf_op jit(solution)/shard_map/ppermute | solution.py:440
  76.2 8.4 %all-to-all-start.3 = ((bf16[16,4,512]{2,1,0:T(4,128)(2,1)}), bf16[16,4,512]{2,1,0:T(4,128)(2,1)S(1)}, u32[]{:S(2)}, u32[]{:S(2)}) async-start(bf16[16,4,512]{2,1,0:T(4,128)(2,1)} %sum_chips.1), calls=%async_computation.3 | async-start | bytes 131072 | tf_op jit(solution)/shard_map/all_to_all | solution.py:493
  84.6 0.0 collective-permute-done.5
  84.6 0.1 select_convert_fusion.mine_ref
  84.7 0.2 collective-permute-start.6
  84.9 1.2 %collective-permute-done.6.other_ref = bf16[96,512]{1,0:T(8,128)(2,1)S(1)} collective-permute-done((bf16[96,512]{1,0:T(8,128)(2,1)S(1)}, bf16[96,512]{1,0:T(8,128)(2,1)S(1)}, u32[]{:S(2)}, u32[]{:S(2)}) %collective-permute-start.6) | collective-permute-done | bytes 98336 | tf_op jit(solution)/shard_map/ppermute | solution.py:440
  86.1 0.9 finish.1
  87.0 5.1 %all-to-all-done.3.parts_ref = bf16[16,4,512]{2,1,0:T(4,128)(2,1)S(1)} async-done(((bf16[16,4,512]{2,1,0:T(4,128)(2,1)}), bf16[16,4,512]{2,1,0:T(4,128)(2,1)S(1)}, u32[]{:S(2)}, u32[]{:S(2)}) %all-to-all-start.3) | async-done | bytes 65568 | tf_op jit(solution)/shard_map/all_to_all | solution.py:493
  92.0 0.6 sum_last.1
  (9 shorter events, 0.1 us)
Async XLA Ops:
  46.0 5.5 %collective-permute-start = (bf16[16,64,512]{2,1,0:T(8,128)(2,1)S(1)}, bf16[16,64,512]{2,1,0:T(8,128)(2,1)S(1)}, u32[]{:S(2)}, u32[]{:S(2)}) collective-permute-start(bf16[16,64,512]{2,1,0:T(8,128)(2,1)S(1)} %get-tuple-element.40), channel_id=1, source_target_pairs={{0,1},{1,0},{2,3},{3,2},{4,5},{5,4},{6,7},{7,6},{8,9},{9,8},{10,11... | collective-permute-start | bytes 3145736 | tf_op jit(solution)/shard_map/ppermute | solution.py:440
  49.4 1.9 %collective-permute-start.1 = (bf16[96,512]{1,0:T(8,128)(2,1)S(1)}, bf16[96,512]{1,0:T(8,128)(2,1)S(1)}, u32[]{:S(2)}, u32[]{:S(2)}) collective-permute-start(bf16[96,512]{1,0:T(8,128)(2,1)S(1)} %get-tuple-element.44), channel_id=1, source_target_pairs={{0,1},{1,0},{2,3},{3,2},{4,5},{5,4},{6,7},{7,6},{8,9},{9,8},{10,11... | collective-permute-start | bytes 294920 | tf_op jit(solution)/shard_map/ppermute | solution.py:440
  52.9 21.4 %all-to-all-start.2 = ((bf16[16,64,512]{2,1,0:T(8,128)(2,1)}), bf16[16,64,512]{2,1,0:T(8,128)(2,1)S(1)}, u32[]{:S(2)}, u32[]{:S(2)}) async-start(bf16[16,64,512]{2,1,0:T(8,128)(2,1)} %add_convert_fusion), calls=%async_computation.2 | async-start | bytes 2097152 | tf_op jit(solution)/shard_map/all_to_all | solution.py:487
  57.5 10.8 %collective-permute-start.2 = (bf16[96,512]{1,0:T(8,128)(2,1)S(1)}, bf16[96,512]{1,0:T(8,128)(2,1)S(1)}, u32[]{:S(2)}, u32[]{:S(2)}) collective-permute-start(bf16[96,512]{1,0:T(8,128)(2,1)S(1)} %select_convert_fusion.2), channel_id=1, source_target_pairs={{0,10},{1,15},{2,8},{3,13},{4,14},{5,11},{6,12},{7,9},{8,2},{9,7},... | collective-permute-start | bytes 294920 | tf_op jit(solution)/shard_map/ppermute | solution.py:450
  64.0 10.1 %collective-permute-start.3 = (bf16[96,512]{1,0:T(8,128)(2,1)S(1)}, bf16[96,512]{1,0:T(8,128)(2,1)S(1)}, u32[]{:S(2)}, u32[]{:S(2)}) collective-permute-start(bf16[96,512]{1,0:T(8,128)(2,1)S(1)} %select_convert_fusion.2), channel_id=1, source_target_pairs={{0,2},{1,7},{2,0},{3,5},{4,6},{5,3},{6,4},{7,1},{8,10},{9,15},{10,... | collective-permute-start | bytes 294920 | tf_op jit(solution)/shard_map/ppermute | solution.py:450
  64.3 9.8 %collective-permute-start.4 = (bf16[96,512]{1,0:T(8,128)(2,1)S(1)}, bf16[96,512]{1,0:T(8,128)(2,1)S(1)}, u32[]{:S(2)}, u32[]{:S(2)}) collective-permute-start(bf16[96,512]{1,0:T(8,128)(2,1)S(1)} %select_convert_fusion.2), channel_id=1, source_target_pairs={{0,8},{1,9},{2,10},{3,11},{4,12},{5,13},{6,14},{7,15},{8,0},{9,1},... | collective-permute-start | bytes 294920 | tf_op jit(solution)/shard_map/ppermute | solution.py:450
  75.1 9.5 %collective-permute-start.5 = (bf16[96,512]{1,0:T(8,128)(2,1)S(1)}, bf16[96,512]{1,0:T(8,128)(2,1)S(1)}, u32[]{:S(2)}, u32[]{:S(2)}) collective-permute-start(bf16[96,512]{1,0:T(8,128)(2,1)S(1)} %select_convert_fusion.1), channel_id=1, source_target_pairs={{0,4},{2,6},{4,0},{6,2},{1,5},{3,7},{5,1},{7,3},{8,12},{10,14},{12... | collective-permute-start | bytes 294920 | tf_op jit(solution)/shard_map/ppermute | solution.py:440
  76.2 15.9 %all-to-all-start.3 = ((bf16[16,4,512]{2,1,0:T(4,128)(2,1)}), bf16[16,4,512]{2,1,0:T(4,128)(2,1)S(1)}, u32[]{:S(2)}, u32[]{:S(2)}) async-start(bf16[16,4,512]{2,1,0:T(4,128)(2,1)} %sum_chips.1), calls=%async_computation.3 | async-start | bytes 131072 | tf_op jit(solution)/shard_map/all_to_all | solution.py:493
  84.7 1.4 %collective-permute-start.6 = (bf16[96,512]{1,0:T(8,128)(2,1)S(1)}, bf16[96,512]{1,0:T(8,128)(2,1)S(1)}, u32[]{:S(2)}, u32[]{:S(2)}) collective-permute-start(bf16[96,512]{1,0:T(8,128)(2,1)S(1)} %select_convert_fusion.mine_ref), channel_id=1, source_target_pairs={{0,1},{1,0},{2,3},{3,2},{4,5},{5,4},{6,7},{7,6},{8,9},{9,8},{10,11... | collective-permute-start | bytes 294920 | tf_op jit(solution)/shard_map/ppermute | solution.py:440

commit v6 on v5

--- a/solution.py
+++ b/solution.py
@@ -374,7 +374,7 @@
     for z in range(8):
         for c in range(2):
             at = z * 8 + c * 4
-            out_ref[c * 8 + z] = total[at : at + 4].astype(BF)
+            out_ref[c * 8 + z % 2 * 4 + z // 2] = total[at : at + 4].astype(BF)
 
 
 def sum_chips(parts):
@@ -490,7 +490,7 @@
 
     total = packed(total.astype(F32) + swap(total, "y", 2).astype(F32))
     second_out, loss = finish(core, total, swap(total, "c", 1))
-    first = lax.all_to_all(first, ("c", "zl", "zh"), 0, 0, tiled=True)
+    first = lax.all_to_all(first, ("c", "zh", "zl"), 0, 0, tiled=True)
     first, second_out, loss = lax.optimization_barrier((first, second_out, loss))
     return loss[0], field_grad.transpose(1, 0, 2), sum_last(first), second_out.transpose(1, 0, 2)
 

time: 93 us -> 92.7 us (level)
  no operation moved by 1% of the time
where the time goes in v6:
time: 92.7 us; the launch traced here: 92.4 us
  blocking collectives  33.3 us (36%)
  starting transfers between devices  24.7 us (27%)
  Pallas kernels  18.1 us (20%)
  waiting for transfers between devices  13.6 us (15%)
  other arithmetic  1.86 us (2%)
    all_to_all x1, blocking collectives, on_device(): gathered = lax.all_to_all(blocks, ('x', 'zl'), 0, 0, tiled=True)  19.4 us
    all_to_all x1, blocking collectives, on_device(): grads = lax.all_to_all(grads, ('x', 'zl'), 0, 0, tiled=True)  13.8 us
    all_to_all x1, starting transfers between devices, on_device(): first = lax.all_to_all(first, ('c', 'zh', 'zl'), 0, 0, tiled=True)  8.4 us
    ppermute x3, starting transfers between devices, cross(): return lax.ppermute(value, ('zh', 'y', 'c'), pairs)  8.03 us
    ppermute x3, waiting for transfers between devices, cross(): return lax.ppermute(value, ('zh', 'y', 'c'), pairs)  7.68 us
    pallas_call x1, Pallas kernels, forward(): pl.pallas_call(forward_kernel, in_specs=[SCALAR, HBM, HBM, HBM, HBM], out...  7.4 us
    all_to_all x1, waiting for transfers between devices, on_device(): first = lax.all_to_all(first, ('c', 'zh', 'zl'), 0, 0, tiled=True)  4.76 us
    all_to_all x1, starting transfers between devices, on_device(): first = lax.all_to_all(first, ('y', 'x'), 0, 0, tiled=True)  4.58 us
  transfers between devices with their start and end apart: 9, of which 4 were waited for; matrix products, arithmetic and copies ran while one was open for 0% of the time, Pallas kernels for 5%

profile of v6, /device:TPU:1, one launch (start us, length us, event | category | flops | bytes accessed | tf_op | source)
XLA Modules:
  0.0 92.4 jit_solution(17939667251297651125)
XLA Ops:
  0.6 0.1 pad_add_fusion.where_ref
  0.7 7.4 %forward.1 = (bf16[1024,1536]{1,0:T(8,128)(2,1)S(1)}, bf16[1024,1536]{1,0:T(8,128)(2,1)S(1)}, bf16[1024,1536]{1,0:T(8,128)(2,1)S(1)}, bf16[16,24,384]{2,1,0:T(8,...) custom-call(s32[3]{0:T(128)S(1)} %pad_add_fusion.where_ref, ...), custom_call_target="tpu_custom_call" | custom-call | tf_op jit(solution)/shard_map/forward/pallas_call | solution.py:142
  8.1 19.4 %all_to_all.20.fields_ref = bf16[16,24,384]{2,1,0:T(8,128)(2,1)S(1)} all-to-all(bf16[16,24,384]{2,1,0:T(8,128)(2,1)S(1)} %get-tuple-element.33), channel_id=1, replica_groups=mesh['zl'=4,'x'=4,'zh'=2,'y'=4,'c'=2] {'x','zl'}, dimensions={0} | all-to-all | bytes 589824 | tf_op jit(solution)/shard_map/all_to_all | solution.py:471
  27.5 2.0 %pairs.1 = bf16[16,24,384]{2,1,0:T(8,128)(2,1)S(1)} custom-call(bf16[16,24,384]{2,1,0:T(8,128)(2,1)S(1)} %all_to_all.20.fields_ref, f32[9,8,128]{2,1,0:T(8,128)S(1)} %get-tuple-element.34.truth_ref, f32[9,8,128]{2,1,0:T(8,128)S(1)} %get-tuple-element.35.area_ref), custom_call_target="tpu_custom_call" | custom-call | tf_op jit(solution)/shard_map/pairs/pallas_call | solution.py:239
  29.6 13.8 %all_to_all.21.blk_ref = bf16[16,24,384]{2,1,0:T(8,128)(2,1)S(1)} all-to-all(bf16[16,24,384]{2,1,0:T(8,128)(2,1)S(1)} %pairs.1), channel_id=1, replica_groups=mesh['zl'=4,'x'=4,'zh'=2,'y'=4,'c'=2] {'x','zl'}, dimensions={0} | all-to-all | bytes 589824 | tf_op jit(solution)/shard_map/all_to_all | solution.py:473
  43.4 2.6 %backward.1 = (bf16[1024,1536]{1,0:T(8,128)(2,1)S(1)}, bf16[16,64,512]{2,1,0:T(8,128)(2,1)S(1)}, bf16[128,1536]{1,0:T(8,128)(2,1)S(1)}) custom-call(s32[1]{0:T(128)} %bitcast.3.core_ref, bf16[16,24,384]{2,1,0:T(8,128)(2,1)S(1)} %all_to_all.21.blk_ref, bf16[1024,1536]{1,0:T(8,128)(2,1)S(1)} %get-tuple-element.36.der_ref, ...), custom_call_target="tpu_custom_call" | custom-call | tf_op jit(solution)/shard_map/backward/pallas_call | solution.py:285
  46.0 2.2 %collective-permute-start = (bf16[16,64,512]{2,1,0:T(8,128)(2,1)S(1)}, bf16[16,64,512]{2,1,0:T(8,128)(2,1)S(1)}, u32[]{:S(2)}, u32[]{:S(2)}) collective-permute-start(bf16[16,64,512]{2,1,0:T(8,128)(2,1)S(1)} %get-tuple-element.40), channel_id=1, source_target_pairs={{0,1},{1,0},{2,3},{3,2},{4,5},{5,4},{6,7},{7,6},{8,9},{9,8},{10,11... | collective-permute-start | bytes 3145736 | tf_op jit(solution)/shard_map/ppermute | solution.py:440
  48.3 1.2 %second.1 = (f32[96,512]{1,0:T(8,128)S(1)}, bf16[96,512]{1,0:T(8,128)(2,1)S(1)}) custom-call(s32[1]{0:T(128)} %bitcast.3.core_ref, bf16[128,1536]{1,0:T(8,128)(2,1)S(1)} %get-tuple-element.47.low_ref, bf16[1024,1536]{1,0:T(8,128)(2,1)S(1)} %get-tuple-element.42.hid_ref), custom_call_target="tpu_custom_call" | custom-call | tf_op jit(solution)/shard_map/second/pallas_call | solution.py:354
  49.4 0.1 collective-permute-start.1
  49.6 1.8 %own_half.1 = f32[16,64,512]{2,1,0:T(8,128)S(1)} custom-call(s32[1]{0:T(128)} %bitcast.3.core_ref, bf16[1024,1536]{1,0:T(8,128)(2,1)S(1)} %get-tuple-element.39.bp_ref, bf16[1024,1536]{1,0:T(8,128)(2,1)S(1)} %get-tuple-element.37.lat_ref), custom_call_target="tpu_custom_call" | custom-call | flops 1610612736 | bytes 8388608 | tf_op jit(solution)/shard_map/own_half/pallas_call | solution.py:300
  51.4 0.0 collective-permute-done.1
  51.4 0.1 select_convert_fusion.2
  51.5 0.0 collective-permute-done
  51.5 1.4 %add_convert_fusion = bf16[16,64,512]{2,1,0:T(8,128)(2,1)} fusion(f32[16,64,512]{2,1,0:T(8,128)S(1)} %own_half.1, bf16[16,64,512]{2,1,0:T(8,128)(2,1)S(1)} %collective-permute-done), kind=kLoop, calls=%fused_computation | loop fusion | flops 1572864 | bytes 4194304 | tf_op jit(solution)/shard_map/convert_element_type | solution.py:480
  52.9 4.6 %all-to-all-start.2 = ((bf16[16,64,512]{2,1,0:T(8,128)(2,1)}), bf16[16,64,512]{2,1,0:T(8,128)(2,1)S(1)}, u32[]{:S(2)}, u32[]{:S(2)}) async-start(bf16[16,64,512]{2,1,0:T(8,128)(2,1)} %add_convert_fusion), calls=%async_computation.2 | async-start | bytes 2097152 | tf_op jit(solution)/shard_map/all_to_all | solution.py:487
  57.5 6.5 %collective-permute-start.2 = (bf16[96,512]{1,0:T(8,128)(2,1)S(1)}, bf16[96,512]{1,0:T(8,128)(2,1)S(1)}, u32[]{:S(2)}, u32[]{:S(2)}) collective-permute-start(bf16[96,512]{1,0:T(8,128)(2,1)S(1)} %select_convert_fusion.2), channel_id=1, source_target_pairs={{0,10},{1,15},{2,8},{3,13},{4,14},{5,11},{6,12},{7,9},{8,2},{9,7},... | collective-permute-start | bytes 294920 | tf_op jit(solution)/shard_map/ppermute | solution.py:450
  64.0 0.4 collective-permute-start.3
  64.3 1.2 %collective-permute-start.4 = (bf16[96,512]{1,0:T(8,128)(2,1)S(1)}, bf16[96,512]{1,0:T(8,128)(2,1)S(1)}, u32[]{:S(2)}, u32[]{:S(2)}) collective-permute-start(bf16[96,512]{1,0:T(8,128)(2,1)S(1)} %select_convert_fusion.2), channel_id=1, source_target_pairs={{0,8},{1,9},{2,10},{3,11},{4,12},{5,13},{6,14},{7,15},{8,0},{9,1},... | collective-permute-start | bytes 294920 | tf_op jit(solution)/shard_map/ppermute | solution.py:450
  65.5 0.9 emit.1
  66.4 1.9 %collective-permute-done.2 = bf16[96,512]{1,0:T(8,128)(2,1)S(1)} collective-permute-done((bf16[96,512]{1,0:T(8,128)(2,1)S(1)}, bf16[96,512]{1,0:T(8,128)(2,1)S(1)}, u32[]{:S(2)}, u32[]{:S(2)}) %collective-permute-start.2) | collective-permute-done | bytes 98336 | tf_op jit(solution)/shard_map/ppermute | solution.py:450
  68.3 5.8 %collective-permute-done.3 = bf16[96,512]{1,0:T(8,128)(2,1)S(1)} collective-permute-done((bf16[96,512]{1,0:T(8,128)(2,1)S(1)}, bf16[96,512]{1,0:T(8,128)(2,1)S(1)}, u32[]{:S(2)}, u32[]{:S(2)}) %collective-permute-start.3) | collective-permute-done | bytes 98336 | tf_op jit(solution)/shard_map/ppermute | solution.py:450
  74.2 0.1 select_convert_fusion.1
  74.3 0.8 sum_chips.1
  75.1 1.1 %collective-permute-start.5 = (bf16[96,512]{1,0:T(8,128)(2,1)S(1)}, bf16[96,512]{1,0:T(8,128)(2,1)S(1)}, u32[]{:S(2)}, u32[]{:S(2)}) collective-permute-start(bf16[96,512]{1,0:T(8,128)(2,1)S(1)} %select_convert_fusion.1), channel_id=1, source_target_pairs={{0,4},{2,6},{4,0},{6,2},{1,5},{3,7},{5,1},{7,3},{8,12},{10,14},{12... | collective-permute-start | bytes 294920 | tf_op jit(solution)/shard_map/ppermute | solution.py:440
  76.2 8.4 %all-to-all-start.3 = ((bf16[16,4,512]{2,1,0:T(4,128)(2,1)}), bf16[16,4,512]{2,1,0:T(4,128)(2,1)S(1)}, u32[]{:S(2)}, u32[]{:S(2)}) async-start(bf16[16,4,512]{2,1,0:T(4,128)(2,1)} %sum_chips.1), calls=%async_computation.3 | async-start | bytes 131072 | tf_op jit(solution)/shard_map/all_to_all | solution.py:493
  84.6 0.0 collective-permute-done.5
  84.6 0.1 select_convert_fusion.mine_ref
  84.7 0.2 collective-permute-start.6
  84.9 1.2 %collective-permute-done.6.other_ref = bf16[96,512]{1,0:T(8,128)(2,1)S(1)} collective-permute-done((bf16[96,512]{1,0:T(8,128)(2,1)S(1)}, bf16[96,512]{1,0:T(8,128)(2,1)S(1)}, u32[]{:S(2)}, u32[]{:S(2)}) %collective-permute-start.6) | collective-permute-done | bytes 98336 | tf_op jit(solution)/shard_map/ppermute | solution.py:440
  86.1 0.9 finish.1
  87.0 4.8 %all-to-all-done.3.parts_ref = bf16[16,4,512]{2,1,0:T(4,128)(2,1)S(1)} async-done(((bf16[16,4,512]{2,1,0:T(4,128)(2,1)}), bf16[16,4,512]{2,1,0:T(4,128)(2,1)S(1)}, u32[]{:S(2)}, u32[]{:S(2)}) %all-to-all-start.3) | async-done | bytes 65568 | tf_op jit(solution)/shard_map/all_to_all | solution.py:493
  91.7 0.6 sum_last.1
  (9 shorter events, 0.1 us)
Async XLA Ops:
  46.0 5.5 %collective-permute-start = (bf16[16,64,512]{2,1,0:T(8,128)(2,1)S(1)}, bf16[16,64,512]{2,1,0:T(8,128)(2,1)S(1)}, u32[]{:S(2)}, u32[]{:S(2)}) collective-permute-start(bf16[16,64,512]{2,1,0:T(8,128)(2,1)S(1)} %get-tuple-element.40), channel_id=1, source_target_pairs={{0,1},{1,0},{2,3},{3,2},{4,5},{5,4},{6,7},{7,6},{8,9},{9,8},{10,11... | collective-permute-start | bytes 3145736 | tf_op jit(solution)/shard_map/ppermute | solution.py:440
  49.4 1.9 %collective-permute-start.1 = (bf16[96,512]{1,0:T(8,128)(2,1)S(1)}, bf16[96,512]{1,0:T(8,128)(2,1)S(1)}, u32[]{:S(2)}, u32[]{:S(2)}) collective-permute-start(bf16[96,512]{1,0:T(8,128)(2,1)S(1)} %get-tuple-element.44), channel_id=1, source_target_pairs={{0,1},{1,0},{2,3},{3,2},{4,5},{5,4},{6,7},{7,6},{8,9},{9,8},{10,11... | collective-permute-start | bytes 294920 | tf_op jit(solution)/shard_map/ppermute | solution.py:440
  52.9 21.4 %all-to-all-start.2 = ((bf16[16,64,512]{2,1,0:T(8,128)(2,1)}), bf16[16,64,512]{2,1,0:T(8,128)(2,1)S(1)}, u32[]{:S(2)}, u32[]{:S(2)}) async-start(bf16[16,64,512]{2,1,0:T(8,128)(2,1)} %add_convert_fusion), calls=%async_computation.2 | async-start | bytes 2097152 | tf_op jit(solution)/shard_map/all_to_all | solution.py:487
  57.5 10.8 %collective-permute-start.2 = (bf16[96,512]{1,0:T(8,128)(2,1)S(1)}, bf16[96,512]{1,0:T(8,128)(2,1)S(1)}, u32[]{:S(2)}, u32[]{:S(2)}) collective-permute-start(bf16[96,512]{1,0:T(8,128)(2,1)S(1)} %select_convert_fusion.2), channel_id=1, source_target_pairs={{0,10},{1,15},{2,8},{3,13},{4,14},{5,11},{6,12},{7,9},{8,2},{9,7},... | collective-permute-start | bytes 294920 | tf_op jit(solution)/shard_map/ppermute | solution.py:450
  64.0 10.1 %collective-permute-start.3 = (bf16[96,512]{1,0:T(8,128)(2,1)S(1)}, bf16[96,512]{1,0:T(8,128)(2,1)S(1)}, u32[]{:S(2)}, u32[]{:S(2)}) collective-permute-start(bf16[96,512]{1,0:T(8,128)(2,1)S(1)} %select_convert_fusion.2), channel_id=1, source_target_pairs={{0,2},{1,7},{2,0},{3,5},{4,6},{5,3},{6,4},{7,1},{8,10},{9,15},{10,... | collective-permute-start | bytes 294920 | tf_op jit(solution)/shard_map/ppermute | solution.py:450
  64.3 9.8 %collective-permute-start.4 = (bf16[96,512]{1,0:T(8,128)(2,1)S(1)}, bf16[96,512]{1,0:T(8,128)(2,1)S(1)}, u32[]{:S(2)}, u32[]{:S(2)}) collective-permute-start(bf16[96,512]{1,0:T(8,128)(2,1)S(1)} %select_convert_fusion.2), channel_id=1, source_target_pairs={{0,8},{1,9},{2,10},{3,11},{4,12},{5,13},{6,14},{7,15},{8,0},{9,1},... | collective-permute-start | bytes 294920 | tf_op jit(solution)/shard_map/ppermute | solution.py:450
  75.1 9.5 %collective-permute-start.5 = (bf16[96,512]{1,0:T(8,128)(2,1)S(1)}, bf16[96,512]{1,0:T(8,128)(2,1)S(1)}, u32[]{:S(2)}, u32[]{:S(2)}) collective-permute-start(bf16[96,512]{1,0:T(8,128)(2,1)S(1)} %select_convert_fusion.1), channel_id=1, source_target_pairs={{0,4},{2,6},{4,0},{6,2},{1,5},{3,7},{5,1},{7,3},{8,12},{10,14},{12... | collective-permute-start | bytes 294920 | tf_op jit(solution)/shard_map/ppermute | solution.py:440
  76.2 15.6 %all-to-all-start.3 = ((bf16[16,4,512]{2,1,0:T(4,128)(2,1)}), bf16[16,4,512]{2,1,0:T(4,128)(2,1)S(1)}, u32[]{:S(2)}, u32[]{:S(2)}) async-start(bf16[16,4,512]{2,1,0:T(4,128)(2,1)} %sum_chips.1), calls=%async_computation.3 | async-start | bytes 131072 | tf_op jit(solution)/shard_map/all_to_all | solution.py:493
  84.7 1.4 %collective-permute-start.6 = (bf16[96,512]{1,0:T(8,128)(2,1)S(1)}, bf16[96,512]{1,0:T(8,128)(2,1)S(1)}, u32[]{:S(2)}, u32[]{:S(2)}) collective-permute-start(bf16[96,512]{1,0:T(8,128)(2,1)S(1)} %select_convert_fusion.mine_ref), channel_id=1, source_target_pairs={{0,1},{1,0},{2,3},{3,2},{4,5},{5,4},{6,7},{7,6},{8,9},{9,8},{10,11... | collective-permute-start | bytes 294920 | tf_op jit(solution)/shard_map/ppermute | solution.py:440

commit v7 on v6

--- a/solution.py
+++ b/solution.py
@@ -212,9 +212,9 @@
     row = lax.broadcasted_iota(jnp.int32, (8, 128), 0)
     last = ROWS // 8 - 1
     for l in range(lane_tiles):
-        losses = lax.fori_loop(
-            0, ROWS // 8, lambda r, carry: spot(r * lane_tiles + l, carry), zero
-        )
+        losses = zero
+        for r in range(ROWS // 8):
+            losses = spot(r * lane_tiles + l, losses)
         for m in range(MEMBERS):
             loss = jnp.sum(losses[m], axis=0, keepdims=True)
             high = loss.astype(BF).astype(F32)

time: 92.7 us -> 92.7 us (level)
  transfers between devices with their start and end apart: 9 -> 9, of which waited for: 4 -> 5; matrix products, arithmetic and copies ran while one was open for 0% -> 0% of each run, Pallas kernels for 5% -> 5%
where the time goes in v7:
time: 92.7 us; the launch traced here: 92.4 us
  blocking collectives  33.3 us (36%)
  starting transfers between devices  24.6 us (27%)
  Pallas kernels  18.1 us (20%)
  waiting for transfers between devices  13.8 us (15%)
  other arithmetic  1.86 us (2%)
    all_to_all x1, blocking collectives, on_device(): gathered = lax.all_to_all(blocks, ('x', 'zl'), 0, 0, tiled=True)  19.4 us
    all_to_all x1, blocking collectives, on_device(): grads = lax.all_to_all(grads, ('x', 'zl'), 0, 0, tiled=True)  13.8 us
    all_to_all x1, starting transfers between devices, on_device(): first = lax.all_to_all(first, ('c', 'zh', 'zl'), 0, 0, tiled=True)  8.38 us
    ppermute x3, starting transfers between devices, cross(): return lax.ppermute(value, ('zh', 'y', 'c'), pairs)  7.89 us
    ppermute x3, waiting for transfers between devices, cross(): return lax.ppermute(value, ('zh', 'y', 'c'), pairs)  7.79 us
    pallas_call x1, Pallas kernels, forward(): pl.pallas_call(forward_kernel, in_specs=[SCALAR, HBM, HBM, HBM, HBM], out...  7.4 us
    all_to_all x1, waiting for transfers between devices, on_device(): first = lax.all_to_all(first, ('c', 'zh', 'zl'), 0, 0, tiled=True)  4.76 us
    all_to_all x1, starting transfers between devices, on_device(): first = lax.all_to_all(first, ('y', 'x'), 0, 0, tiled=True)  4.58 us
  transfers between devices with their start and end apart: 9, of which 5 were waited for; matrix products, arithmetic and copies ran while one was open for 0% of the time, Pallas kernels for 5%

profile of v7, /device:TPU:1, one launch (start us, length us, event | category | flops | bytes accessed | tf_op | source)
XLA Modules:
  0.0 92.4 jit_solution(4912295425747010560)
XLA Ops:
  0.6 0.1 pad_add_fusion.where_ref
  0.7 7.4 %forward.1 = (bf16[1024,1536]{1,0:T(8,128)(2,1)S(1)}, bf16[1024,1536]{1,0:T(8,128)(2,1)S(1)}, bf16[1024,1536]{1,0:T(8,128)(2,1)S(1)}, bf16[16,24,384]{2,1,0:T(8,...) custom-call(s32[3]{0:T(128)S(1)} %pad_add_fusion.where_ref, ...), custom_call_target="tpu_custom_call" | custom-call | tf_op jit(solution)/shard_map/forward/pallas_call | solution.py:142
  8.1 19.4 %all_to_all.20.fields_ref = bf16[16,24,384]{2,1,0:T(8,128)(2,1)S(1)} all-to-all(bf16[16,24,384]{2,1,0:T(8,128)(2,1)S(1)} %get-tuple-element.33), channel_id=1, replica_groups=mesh['zl'=4,'x'=4,'zh'=2,'y'=4,'c'=2] {'x','zl'}, dimensions={0} | all-to-all | bytes 589824 | tf_op jit(solution)/shard_map/all_to_all | solution.py:471
  27.5 1.9 %pairs.1 = bf16[16,24,384]{2,1,0:T(8,128)(2,1)S(1)} custom-call(bf16[16,24,384]{2,1,0:T(8,128)(2,1)S(1)} %all_to_all.20.fields_ref, f32[9,8,128]{2,1,0:T(8,128)S(1)} %get-tuple-element.34.truth_ref, f32[9,8,128]{2,1,0:T(8,128)S(1)} %get-tuple-element.35.area_ref), custom_call_target="tpu_custom_call" | custom-call | tf_op jit(solution)/shard_map/pairs/pallas_call | solution.py:239
  29.5 13.8 %all_to_all.21.blk_ref = bf16[16,24,384]{2,1,0:T(8,128)(2,1)S(1)} all-to-all(bf16[16,24,384]{2,1,0:T(8,128)(2,1)S(1)} %pairs.1), channel_id=1, replica_groups=mesh['zl'=4,'x'=4,'zh'=2,'y'=4,'c'=2] {'x','zl'}, dimensions={0} | all-to-all | bytes 589824 | tf_op jit(solution)/shard_map/all_to_all | solution.py:473
  43.3 2.6 %backward.1 = (bf16[1024,1536]{1,0:T(8,128)(2,1)S(1)}, bf16[16,64,512]{2,1,0:T(8,128)(2,1)S(1)}, bf16[128,1536]{1,0:T(8,128)(2,1)S(1)}) custom-call(s32[1]{0:T(128)} %bitcast.3.core_ref, bf16[16,24,384]{2,1,0:T(8,128)(2,1)S(1)} %all_to_all.21.blk_ref, bf16[1024,1536]{1,0:T(8,128)(2,1)S(1)} %get-tuple-element.36.der_ref, ...), custom_call_target="tpu_custom_call" | custom-call | tf_op jit(solution)/shard_map/backward/pallas_call | solution.py:285
  45.9 2.2 %collective-permute-start = (bf16[16,64,512]{2,1,0:T(8,128)(2,1)S(1)}, bf16[16,64,512]{2,1,0:T(8,128)(2,1)S(1)}, u32[]{:S(2)}, u32[]{:S(2)}) collective-permute-start(bf16[16,64,512]{2,1,0:T(8,128)(2,1)S(1)} %get-tuple-element.40), channel_id=1, source_target_pairs={{0,1},{1,0},{2,3},{3,2},{4,5},{5,4},{6,7},{7,6},{8,9},{9,8},{10,11... | collective-permute-start | bytes 3145736 | tf_op jit(solution)/shard_map/ppermute | solution.py:440
  48.2 1.2 %second.1 = (f32[96,512]{1,0:T(8,128)S(1)}, bf16[96,512]{1,0:T(8,128)(2,1)S(1)}) custom-call(s32[1]{0:T(128)} %bitcast.3.core_ref, bf16[128,1536]{1,0:T(8,128)(2,1)S(1)} %get-tuple-element.47.low_ref, bf16[1024,1536]{1,0:T(8,128)(2,1)S(1)} %get-tuple-element.42.hid_ref), custom_call_target="tpu_custom_call" | custom-call | tf_op jit(solution)/shard_map/second/pallas_call | solution.py:354
  49.4 0.3 collective-permute-start.1
  49.6 1.8 %own_half.1 = f32[16,64,512]{2,1,0:T(8,128)S(1)} custom-call(s32[1]{0:T(128)} %bitcast.3.core_ref, bf16[1024,1536]{1,0:T(8,128)(2,1)S(1)} %get-tuple-element.39.bp_ref, bf16[1024,1536]{1,0:T(8,128)(2,1)S(1)} %get-tuple-element.37.lat_ref), custom_call_target="tpu_custom_call" | custom-call | flops 1610612736 | bytes 8388608 | tf_op jit(solution)/shard_map/own_half/pallas_call | solution.py:300
  51.5 0.0 collective-permute-done.1
  51.5 0.1 select_convert_fusion.2
  51.6 1.4 %add_convert_fusion = bf16[16,64,512]{2,1,0:T(8,128)(2,1)} fusion(f32[16,64,512]{2,1,0:T(8,128)S(1)} %own_half.1, bf16[16,64,512]{2,1,0:T(8,128)(2,1)S(1)} %collective-permute-done), kind=kLoop, calls=%fused_computation | loop fusion | flops 1572864 | bytes 4194304 | tf_op jit(solution)/shard_map/convert_element_type | solution.py:480
  53.0 4.6 %all-to-all-start.2 = ((bf16[16,64,512]{2,1,0:T(8,128)(2,1)}), bf16[16,64,512]{2,1,0:T(8,128)(2,1)S(1)}, u32[]{:S(2)}, u32[]{:S(2)}) async-start(bf16[16,64,512]{2,1,0:T(8,128)(2,1)} %add_convert_fusion), calls=%async_computation.2 | async-start | bytes 2097152 | tf_op jit(solution)/shard_map/all_to_all | solution.py:487
  57.6 6.4 %collective-permute-start.2 = (bf16[96,512]{1,0:T(8,128)(2,1)S(1)}, bf16[96,512]{1,0:T(8,128)(2,1)S(1)}, u32[]{:S(2)}, u32[]{:S(2)}) collective-permute-start(bf16[96,512]{1,0:T(8,128)(2,1)S(1)} %select_convert_fusion.2), channel_id=1, source_target_pairs={{0,10},{1,15},{2,8},{3,13},{4,14},{5,11},{6,12},{7,9},{8,2},{9,7},... | collective-permute-start | bytes 294920 | tf_op jit(solution)/shard_map/ppermute | solution.py:450
  64.0 0.2 collective-permute-start.3
  64.2 1.3 %collective-permute-start.4 = (bf16[96,512]{1,0:T(8,128)(2,1)S(1)}, bf16[96,512]{1,0:T(8,128)(2,1)S(1)}, u32[]{:S(2)}, u32[]{:S(2)}) collective-permute-start(bf16[96,512]{1,0:T(8,128)(2,1)S(1)} %select_convert_fusion.2), channel_id=1, source_target_pairs={{0,8},{1,9},{2,10},{3,11},{4,12},{5,13},{6,14},{7,15},{8,0},{9,1},... | collective-permute-start | bytes 294920 | tf_op jit(solution)/shard_map/ppermute | solution.py:450
  65.5 0.9 emit.1
  66.4 1.9 %collective-permute-done.2 = bf16[96,512]{1,0:T(8,128)(2,1)S(1)} collective-permute-done((bf16[96,512]{1,0:T(8,128)(2,1)S(1)}, bf16[96,512]{1,0:T(8,128)(2,1)S(1)}, u32[]{:S(2)}, u32[]{:S(2)}) %collective-permute-start.2) | collective-permute-done | bytes 98336 | tf_op jit(solution)/shard_map/ppermute | solution.py:450
  68.2 5.9 %collective-permute-done.3 = bf16[96,512]{1,0:T(8,128)(2,1)S(1)} collective-permute-done((bf16[96,512]{1,0:T(8,128)(2,1)S(1)}, bf16[96,512]{1,0:T(8,128)(2,1)S(1)}, u32[]{:S(2)}, u32[]{:S(2)}) %collective-permute-start.3) | collective-permute-done | bytes 98336 | tf_op jit(solution)/shard_map/ppermute | solution.py:450
  74.2 0.0 collective-permute-done.4
  74.2 0.1 select_convert_fusion.1
  74.3 0.1 all-to-all-done.2.parts_ref
  74.4 0.8 sum_chips.1
  75.2 1.1 %collective-permute-start.5 = (bf16[96,512]{1,0:T(8,128)(2,1)S(1)}, bf16[96,512]{1,0:T(8,128)(2,1)S(1)}, u32[]{:S(2)}, u32[]{:S(2)}) collective-permute-start(bf16[96,512]{1,0:T(8,128)(2,1)S(1)} %select_convert_fusion.1), channel_id=1, source_target_pairs={{0,4},{2,6},{4,0},{6,2},{1,5},{3,7},{5,1},{7,3},{8,12},{10,14},{12... | collective-permute-start | bytes 294920 | tf_op jit(solution)/shard_map/ppermute | solution.py:440
  76.3 8.4 %all-to-all-start.3 = ((bf16[16,4,512]{2,1,0:T(4,128)(2,1)}), bf16[16,4,512]{2,1,0:T(4,128)(2,1)S(1)}, u32[]{:S(2)}, u32[]{:S(2)}) async-start(bf16[16,4,512]{2,1,0:T(4,128)(2,1)} %sum_chips.1), calls=%async_computation.3 | async-start | bytes 131072 | tf_op jit(solution)/shard_map/all_to_all | solution.py:493
  84.7 0.1 select_convert_fusion.mine_ref
  84.8 0.2 collective-permute-start.6
  85.0 1.2 %collective-permute-done.6.other_ref = bf16[96,512]{1,0:T(8,128)(2,1)S(1)} collective-permute-done((bf16[96,512]{1,0:T(8,128)(2,1)S(1)}, bf16[96,512]{1,0:T(8,128)(2,1)S(1)}, u32[]{:S(2)}, u32[]{:S(2)}) %collective-permute-start.6) | collective-permute-done | bytes 98336 | tf_op jit(solution)/shard_map/ppermute | solution.py:440
  86.2 0.9 finish.1
  87.1 4.8 %all-to-all-done.3.parts_ref = bf16[16,4,512]{2,1,0:T(4,128)(2,1)S(1)} async-done(((bf16[16,4,512]{2,1,0:T(4,128)(2,1)}), bf16[16,4,512]{2,1,0:T(4,128)(2,1)S(1)}, u32[]{:S(2)}, u32[]{:S(2)}) %all-to-all-start.3) | async-done | bytes 65568 | tf_op jit(solution)/shard_map/all_to_all | solution.py:493
  91.8 0.6 sum_last.1
  (9 shorter events, 0.1 us)
Async XLA Ops:
  45.9 5.7 %collective-permute-start = (bf16[16,64,512]{2,1,0:T(8,128)(2,1)S(1)}, bf16[16,64,512]{2,1,0:T(8,128)(2,1)S(1)}, u32[]{:S(2)}, u32[]{:S(2)}) collective-permute-start(bf16[16,64,512]{2,1,0:T(8,128)(2,1)S(1)} %get-tuple-element.40), channel_id=1, source_target_pairs={{0,1},{1,0},{2,3},{3,2},{4,5},{5,4},{6,7},{7,6},{8,9},{9,8},{10,11... | collective-permute-start | bytes 3145736 | tf_op jit(solution)/shard_map/ppermute | solution.py:440
  49.4 2.1 %collective-permute-start.1 = (bf16[96,512]{1,0:T(8,128)(2,1)S(1)}, bf16[96,512]{1,0:T(8,128)(2,1)S(1)}, u32[]{:S(2)}, u32[]{:S(2)}) collective-permute-start(bf16[96,512]{1,0:T(8,128)(2,1)S(1)} %get-tuple-element.44), channel_id=1, source_target_pairs={{0,1},{1,0},{2,3},{3,2},{4,5},{5,4},{6,7},{7,6},{8,9},{9,8},{10,11... | collective-permute-start | bytes 294920 | tf_op jit(solution)/shard_map/ppermute | solution.py:440
  53.0 21.4 %all-to-all-start.2 = ((bf16[16,64,512]{2,1,0:T(8,128)(2,1)}), bf16[16,64,512]{2,1,0:T(8,128)(2,1)S(1)}, u32[]{:S(2)}, u32[]{:S(2)}) async-start(bf16[16,64,512]{2,1,0:T(8,128)(2,1)} %add_convert_fusion), calls=%async_computation.2 | async-start | bytes 2097152 | tf_op jit(solution)/shard_map/all_to_all | solution.py:487
  57.6 10.6 %collective-permute-start.2 = (bf16[96,512]{1,0:T(8,128)(2,1)S(1)}, bf16[96,512]{1,0:T(8,128)(2,1)S(1)}, u32[]{:S(2)}, u32[]{:S(2)}) collective-permute-start(bf16[96,512]{1,0:T(8,128)(2,1)S(1)} %select_convert_fusion.2), channel_id=1, source_target_pairs={{0,10},{1,15},{2,8},{3,13},{4,14},{5,11},{6,12},{7,9},{8,2},{9,7},... | collective-permute-start | bytes 294920 | tf_op jit(solution)/shard_map/ppermute | solution.py:450
  64.0 10.1 %collective-permute-start.3 = (bf16[96,512]{1,0:T(8,128)(2,1)S(1)}, bf16[96,512]{1,0:T(8,128)(2,1)S(1)}, u32[]{:S(2)}, u32[]{:S(2)}) collective-permute-start(bf16[96,512]{1,0:T(8,128)(2,1)S(1)} %select_convert_fusion.2), channel_id=1, source_target_pairs={{0,2},{1,7},{2,0},{3,5},{4,6},{5,3},{6,4},{7,1},{8,10},{9,15},{10,... | collective-permute-start | bytes 294920 | tf_op jit(solution)/shard_map/ppermute | solution.py:450
  64.2 9.9 %collective-permute-start.4 = (bf16[96,512]{1,0:T(8,128)(2,1)S(1)}, bf16[96,512]{1,0:T(8,128)(2,1)S(1)}, u32[]{:S(2)}, u32[]{:S(2)}) collective-permute-start(bf16[96,512]{1,0:T(8,128)(2,1)S(1)} %select_convert_fusion.2), channel_id=1, source_target_pairs={{0,8},{1,9},{2,10},{3,11},{4,12},{5,13},{6,14},{7,15},{8,0},{9,1},... | collective-permute-start | bytes 294920 | tf_op jit(solution)/shard_map/ppermute | solution.py:450
  75.2 9.5 %collective-permute-start.5 = (bf16[96,512]{1,0:T(8,128)(2,1)S(1)}, bf16[96,512]{1,0:T(8,128)(2,1)S(1)}, u32[]{:S(2)}, u32[]{:S(2)}) collective-permute-start(bf16[96,512]{1,0:T(8,128)(2,1)S(1)} %select_convert_fusion.1), channel_id=1, source_target_pairs={{0,4},{2,6},{4,0},{6,2},{1,5},{3,7},{5,1},{7,3},{8,12},{10,14},{12... | collective-permute-start | bytes 294920 | tf_op jit(solution)/shard_map/ppermute | solution.py:440
  76.3 15.5 %all-to-all-start.3 = ((bf16[16,4,512]{2,1,0:T(4,128)(2,1)}), bf16[16,4,512]{2,1,0:T(4,128)(2,1)S(1)}, u32[]{:S(2)}, u32[]{:S(2)}) async-start(bf16[16,4,512]{2,1,0:T(4,128)(2,1)} %sum_chips.1), calls=%async_computation.3 | async-start | bytes 131072 | tf_op jit(solution)/shard_map/all_to_all | solution.py:493
  84.8 1.4 %collective-permute-start.6 = (bf16[96,512]{1,0:T(8,128)(2,1)S(1)}, bf16[96,512]{1,0:T(8,128)(2,1)S(1)}, u32[]{:S(2)}, u32[]{:S(2)}) collective-permute-start(bf16[96,512]{1,0:T(8,128)(2,1)S(1)} %select_convert_fusion.mine_ref), channel_id=1, source_target_pairs={{0,1},{1,0},{2,3},{3,2},{4,5},{5,4},{6,7},{7,6},{8,9},{9,8},{10,11... | collective-permute-start | bytes 294920 | tf_op jit(solution)/shard_map/ppermute | solution.py:440
